TPU v7x, 128 devices: a whole 4x4x4 slice. The times are simulated.
128 devices in a mesh: outer: 16 (over y_lo, z, core), inner: 8 (over x, y_hi).
Axes of the slice: x: 4, y: 4 (y_hi: 2, y_lo: 2; y = y_hi * 2 + y_lo), z: 4, core: 2. Of those that a mesh axis runs over, the one named last changes fastest.
Arguments:
- query_rows: bfloat16 [16384, 1024], P(('outer', 'inner')), may hold values from -8 to 8
- key_rows: bfloat16 [16384, 128], P(('outer', 'inner')), may hold values from -6 to 6
- value_rows: bfloat16 [16384, 128], P(('outer', 'inner')), may hold values from -0.59765625 to 0.59765625
- saved_output: bfloat16 [16384, 1024], P(('outer', 'inner')), may hold values from -0.59765625 to 0.59765625
- output_grad: bfloat16 [16384, 1024], P(('outer', 'inner')), may hold values from -6 to 6
- logsumexp: float32 [8, 16384], P(None, ('outer', 'inner')), as said below
- block_order: int32 [256], replicated, may hold values from 0 to 255, as said below
Outputs:
- query_grad: bfloat16 [16384, 1024], P(('outer', 'inner'))
- key_grad: bfloat16 [16384, 128], P(('outer', 'inner'))
- value_grad: bfloat16 [16384, 128], P(('outer', 'inner'))
Inputs may be any that keep to these rules, and one draw needn't show every extreme that they name: `block_order`: each number from 0 to 255 appears once. `logsumexp`: close to the log of the softmax total of the query at that position.
All inputs are finite; a program needn't handle non-finite values.
Results may differ from a plain program's by a relative error of at most 0.005.
Values may be sent and summed in bfloat16 or wider, within the bound.
No kernel may reach another device: no remote copies, remote signals or barrier semaphores. Data moves between devices by JAX's collectives and lax.ppermute only.
A program may use at most 128 MiB of HBM per device.

v0:
```python
import math

import jax
import jax.numpy as jnp
from jax import lax
from jax.sharding import PartitionSpec as P


def from_behind(block, axis, distance):
    devices = range(lax.axis_size(axis))
    route = [((i - distance) % len(devices), i) for i in devices]
    return lax.ppermute(block, axis, route)


def block_positions(block_order, owners, block_len):
    wanted = (owners[:, None] * 2 + jnp.arange(2, dtype=jnp.int32)[None, :]).reshape(-1)
    listed = jnp.arange(block_order.shape[0], dtype=jnp.int32)
    chosen = jnp.sum(jnp.where(wanted[:, None] == listed[None, :], block_order[None, :], 0), axis=1)
    return (chosen[:, None] * block_len + jnp.arange(block_len, dtype=jnp.int32)[None, :]).reshape(
        -1
    )


def tile_terms(query_heads, grad_heads, log_totals, deltas, query_pos, stacked, key_pos, width):
    key_part = stacked[:, :width]
    value_part = stacked[:, width:]
    scale = 1.0 / math.sqrt(width)
    scores = (
        jnp.einsum("thd,kd->htk", query_heads, key_part, preferred_element_type=jnp.float32) * scale
    )
    allowed = query_pos[None, :, None] >= key_pos[None, None, :]
    probs = jnp.where(allowed, jnp.exp(scores - log_totals[:, :, None]), 0.0)
    dprobs = jnp.einsum("thd,kd->htk", grad_heads, value_part, preferred_element_type=jnp.float32)
    dscores = probs * (dprobs - deltas[:, :, None])
    probs_half = probs.astype(jnp.bfloat16)
    dscores_half = dscores.astype(jnp.bfloat16)
    value_add = jnp.einsum(
        "htk,thd->kd", probs_half, grad_heads, preferred_element_type=jnp.float32
    )
    key_add = (
        jnp.einsum("htk,thd->kd", dscores_half, query_heads, preferred_element_type=jnp.float32)
        * scale
    )
    query_add = (
        jnp.einsum("htk,kd->thd", dscores_half, key_part, preferred_element_type=jnp.float32)
        * scale
    )
    return (query_add, jnp.concatenate([key_add, value_add], axis=1))


def attend_back(query_heads, grad_heads, log_totals, deltas, query_pos, stacked, key_pos, width):
    return tile_terms(
        query_heads, grad_heads, log_totals, deltas, query_pos, stacked, key_pos, width
    )


def body(query_rows, key_rows, value_rows, saved_output, output_grad, logsumexp, block_order):
    row_count = query_rows.shape[0]
    width = key_rows.shape[1]
    head_count = query_rows.shape[1] // width
    block_len = row_count // 2
    outer_count = lax.axis_size("outer")
    inner_count = lax.axis_size("inner")
    outer_self = lax.axis_index("outer")
    inner_self = lax.axis_index("inner")
    saved_heads = saved_output.reshape(row_count, head_count, width)
    grad_local = output_grad.reshape(row_count, head_count, width)
    deltas = jnp.sum(grad_local.astype(jnp.float32) * saved_heads.astype(jnp.float32), axis=2).T
    stacked = jnp.concatenate([key_rows, value_rows], axis=1)
    outer_ids = jnp.arange(outer_count, dtype=jnp.int32)
    own_index = jnp.reshape(outer_self * inner_count + inner_self, (1,))
    query_pos = block_positions(block_order, own_index, block_len)
    query_heads = query_rows.reshape(row_count, head_count, width)
    holder = jnp.zeros((row_count, 2 * width), jnp.float32)
    query_acc = jnp.zeros((row_count, head_count, width), jnp.float32)

    def turn_step(turn, carry):
        moving, holder, query_acc = carry
        owner_inner = (inner_self - turn) % inner_count
        grouped = lax.all_gather(moving, "outer", axis=0, tiled=True)
        key_pos = block_positions(block_order, outer_ids * inner_count + owner_inner, block_len)
        query_add, terms = attend_back(
            query_heads, grad_local, logsumexp, deltas, query_pos, grouped, key_pos, width
        )
        shares = lax.psum_scatter(terms, "outer", scatter_dimension=0, tiled=True)
        moving = from_behind(moving, "inner", 1)
        holder = from_behind(holder + shares, "inner", 1)
        return (moving, holder, query_acc + query_add)

    moving, holder, query_acc = lax.fori_loop(
        0, inner_count, turn_step, (stacked, holder, query_acc)
    )
    query_grad = query_acc.reshape(row_count, head_count * width).astype(jnp.bfloat16)
    return (
        query_grad,
        holder[:, :width].astype(jnp.bfloat16),
        holder[:, width:].astype(jnp.bfloat16),
    )


def solution(mesh):
    placed = (
        P(("outer", "inner"), None),
        P(("outer", "inner"), None),
        P(("outer", "inner"), None),
        P(("outer", "inner"), None),
        P(("outer", "inner"), None),
        P(None, ("outer", "inner")),
        P(),
    )
    return jax.shard_map(
        body,
        mesh=mesh,
        in_specs=placed,
        out_specs=(
            P(("outer", "inner"), None),
            P(("outer", "inner"), None),
            P(("outer", "inner"), None),
        ),
        check_vma=False,
    )
```

profile of v0, /device:TPU:0, one launch (start us, length us, event | category | flops | bytes accessed | tf_op | source)
XLA Modules:
  0.0 962.2 jit_solution(4299732200968411975)
XLA Ops:
  12.3 941.9 %while.20 = (s32[]{:T(128)}, bf16[128,256]{1,0:T(8,128)(2,1)S(1)}, f32[128,256]{0,1:T(8,128)S(1)}, f32[128,8,128]{2,0,1:T(8,128)S(1)}, s32[]{:T(128)}, /*index=5...) while((s32[]{:T(128)}, bf16[128,256]{1,0:T(8,128)(2,1)S(1)}, ...), condition=%wide.region_5.6_spmd.clone, body=%wide.region_2.5_spmd.clone.sunk | while | flops 2706827520 | bytes 81134248 | solution.py:90
  14.8 35.7 %all-gather.2.cloned.1.call-done = bf16[2048,256]{1,0:T(8,128)(2,1)} async-done(((bf16[128,256]{1,0:T(8,128)(2,1)}), bf16[2048,256]{1,0:T(8,128)(2,1)}) %all-gather.2.cloned.1.call-update) | async-done | bytes 1048592 | tf_op jit(solution)/shard_map/while/body/eval_jaxpr/all_gather | solution.py:80
  62.3 2.9 collective-permute-start
  65.2 60.8 %reduce-scatter.2.cloned.1.call-done = f32[128,256]{0,1:T(8,128)} async-done(((f32[2048,256]{0,1:T(8,128)}), f32[128,256]{0,1:T(8,128)}) %reduce-scatter.2.cloned.1.call-update) | async-done | bytes 131088 | tf_op jit(solution)/shard_map/while/body/eval_jaxpr/reduce_scatter | solution.py:85
  129.8 3.7 fusion.56
  138.1 29.3 %all-gather.2.cloned.1.call-done = bf16[2048,256]{1,0:T(8,128)(2,1)} async-done(((bf16[128,256]{1,0:T(8,128)(2,1)}), bf16[2048,256]{1,0:T(8,128)(2,1)}) %all-gather.2.cloned.1.call-update) | async-done | bytes 1048592 | tf_op jit(solution)/shard_map/while/body/eval_jaxpr/all_gather | solution.py:80
  182.1 60.8 %reduce-scatter.2.cloned.1.call-done = f32[128,256]{0,1:T(8,128)} async-done(((f32[2048,256]{0,1:T(8,128)}), f32[128,256]{0,1:T(8,128)}) %reduce-scatter.2.cloned.1.call-update) | async-done | bytes 131088 | tf_op jit(solution)/shard_map/while/body/eval_jaxpr/reduce_scatter | solution.py:85
  246.6 3.7 fusion.56
  254.9 29.3 %all-gather.2.cloned.1.call-done = bf16[2048,256]{1,0:T(8,128)(2,1)} async-done(((bf16[128,256]{1,0:T(8,128)(2,1)}), bf16[2048,256]{1,0:T(8,128)(2,1)}) %all-gather.2.cloned.1.call-update) | async-done | bytes 1048592 | tf_op jit(solution)/shard_map/while/body/eval_jaxpr/all_gather | solution.py:80
  296.1 2.9 collective-permute-start
  298.9 60.8 %reduce-scatter.2.cloned.1.call-done = f32[128,256]{0,1:T(8,128)} async-done(((f32[2048,256]{0,1:T(8,128)}), f32[128,256]{0,1:T(8,128)}) %reduce-scatter.2.cloned.1.call-update) | async-done | bytes 131088 | tf_op jit(solution)/shard_map/while/body/eval_jaxpr/reduce_scatter | solution.py:85
  363.5 3.7 fusion.56
  371.8 29.3 %all-gather.2.cloned.1.call-done = bf16[2048,256]{1,0:T(8,128)(2,1)} async-done(((bf16[128,256]{1,0:T(8,128)(2,1)}), bf16[2048,256]{1,0:T(8,128)(2,1)}) %all-gather.2.cloned.1.call-update) | async-done | bytes 1048592 | tf_op jit(solution)/shard_map/while/body/eval_jaxpr/all_gather | solution.py:80
  413.0 2.9 collective-permute-start
  415.8 60.8 %reduce-scatter.2.cloned.1.call-done = f32[128,256]{0,1:T(8,128)} async-done(((f32[2048,256]{0,1:T(8,128)}), f32[128,256]{0,1:T(8,128)}) %reduce-scatter.2.cloned.1.call-update) | async-done | bytes 131088 | tf_op jit(solution)/shard_map/while/body/eval_jaxpr/reduce_scatter | solution.py:85
  480.4 3.7 fusion.56
  488.7 29.5 %all-gather.2.cloned.1.call-done = bf16[2048,256]{1,0:T(8,128)(2,1)} async-done(((bf16[128,256]{1,0:T(8,128)(2,1)}), bf16[2048,256]{1,0:T(8,128)(2,1)}) %all-gather.2.cloned.1.call-update) | async-done | bytes 1048592 | tf_op jit(solution)/shard_map/while/body/eval_jaxpr/all_gather | solution.py:80
  530.1 2.9 collective-permute-start
  532.9 60.8 %reduce-scatter.2.cloned.1.call-done = f32[128,256]{0,1:T(8,128)} async-done(((f32[2048,256]{0,1:T(8,128)}), f32[128,256]{0,1:T(8,128)}) %reduce-scatter.2.cloned.1.call-update) | async-done | bytes 131088 | tf_op jit(solution)/shard_map/while/body/eval_jaxpr/reduce_scatter | solution.py:85
  597.5 3.7 fusion.56
  605.8 29.5 %all-gather.2.cloned.1.call-done = bf16[2048,256]{1,0:T(8,128)(2,1)} async-done(((bf16[128,256]{1,0:T(8,128)(2,1)}), bf16[2048,256]{1,0:T(8,128)(2,1)}) %all-gather.2.cloned.1.call-update) | async-done | bytes 1048592 | tf_op jit(solution)/shard_map/while/body/eval_jaxpr/all_gather | solution.py:80
  647.2 2.9 collective-permute-start
  650.1 60.8 %reduce-scatter.2.cloned.1.call-done = f32[128,256]{0,1:T(8,128)} async-done(((f32[2048,256]{0,1:T(8,128)}), f32[128,256]{0,1:T(8,128)}) %reduce-scatter.2.cloned.1.call-update) | async-done | bytes 131088 | tf_op jit(solution)/shard_map/while/body/eval_jaxpr/reduce_scatter | solution.py:85
  714.6 3.7 fusion.56
  722.9 29.5 %all-gather.2.cloned.1.call-done = bf16[2048,256]{1,0:T(8,128)(2,1)} async-done(((bf16[128,256]{1,0:T(8,128)(2,1)}), bf16[2048,256]{1,0:T(8,128)(2,1)}) %all-gather.2.cloned.1.call-update) | async-done | bytes 1048592 | tf_op jit(solution)/shard_map/while/body/eval_jaxpr/all_gather | solution.py:80
  764.3 2.8 collective-permute-start
  767.1 60.8 %reduce-scatter.2.cloned.1.call-done = f32[128,256]{0,1:T(8,128)} async-done(((f32[2048,256]{0,1:T(8,128)}), f32[128,256]{0,1:T(8,128)}) %reduce-scatter.2.cloned.1.call-update) | async-done | bytes 131088 | tf_op jit(solution)/shard_map/while/body/eval_jaxpr/reduce_scatter | solution.py:85
  831.6 3.7 fusion.56
  840.0 29.1 %all-gather.2.cloned.1.call-done = bf16[2048,256]{1,0:T(8,128)(2,1)} async-done(((bf16[128,256]{1,0:T(8,128)(2,1)}), bf16[2048,256]{1,0:T(8,128)(2,1)}) %all-gather.2.cloned.1.call-update) | async-done | bytes 1048592 | tf_op jit(solution)/shard_map/while/body/eval_jaxpr/all_gather | solution.py:80
  880.9 2.8 collective-permute-start
  883.8 60.9 %reduce-scatter.2.cloned.1.call-done = f32[128,256]{0,1:T(8,128)} async-done(((f32[2048,256]{0,1:T(8,128)}), f32[128,256]{0,1:T(8,128)}) %reduce-scatter.2.cloned.1.call-update) | async-done | bytes 131088 | tf_op jit(solution)/shard_map/while/body/eval_jaxpr/reduce_scatter | solution.py:85
  948.3 3.7 fusion.56
  (270 shorter events, 170.0 us)
Async XLA Ops:
  12.3 38.2 %all-gather.2.cloned.1.call-start = ((), (), s32[]{:S(2)}) async-start(), calls=%async_computation.1 | async-start | bytes 1114112 | tf_op jit(solution)/shard_map/while/body/eval_jaxpr/all_gather | solution.py:80
  13.0 113.0 %reduce-scatter.2.cloned.1.call-start = ((), (), s32[]{:S(2)}) async-start(), calls=%async_computation.2 | async-start | bytes 2228224 | tf_op jit(solution)/shard_map/while/body/eval_jaxpr/reduce_scatter | solution.py:85
  62.3 71.1 %collective-permute-start = (bf16[128,256]{1,0:T(8,128)(2,1)S(1)}, bf16[128,256]{1,0:T(8,128)(2,1)S(1)}, u32[]{:S(2)}, u32[]{:S(2)}) collective-permute-start(bf16[128,256]{1,0:T(8,128)(2,1)S(1)} %copy-done.2), channel_id=1, source_target_pairs={{7,0},{0,1},{1,2},{2,3},{3,4},{4,5},{5,6},{6,7},{15,8},{8,9},{9,10... | collective-permute-start | bytes 196616 | tf_op jit(solution)/shard_map/while/body/eval_jaxpr/ppermute | solution.py:12
  127.0 8.7 collective-permute-start.1
  135.6 31.8 %all-gather.2.cloned.1.call-start = ((), (), s32[]{:S(2)}) async-start(), calls=%async_computation.1 | async-start | bytes 1114112 | tf_op jit(solution)/shard_map/while/body/eval_jaxpr/all_gather | solution.py:80
  136.3 106.6 %reduce-scatter.2.cloned.1.call-start = ((), (), s32[]{:S(2)}) async-start(), calls=%async_computation.2 | async-start | bytes 2228224 | tf_op jit(solution)/shard_map/while/body/eval_jaxpr/reduce_scatter | solution.py:85
  179.3 71.0 %collective-permute-start = (bf16[128,256]{1,0:T(8,128)(2,1)S(1)}, bf16[128,256]{1,0:T(8,128)(2,1)S(1)}, u32[]{:S(2)}, u32[]{:S(2)}) collective-permute-start(bf16[128,256]{1,0:T(8,128)(2,1)S(1)} %copy-done.2), channel_id=1, source_target_pairs={{7,0},{0,1},{1,2},{2,3},{3,4},{4,5},{5,6},{6,7},{15,8},{8,9},{9,10... | collective-permute-start | bytes 196616 | tf_op jit(solution)/shard_map/while/body/eval_jaxpr/ppermute | solution.py:12
  243.9 8.7 collective-permute-start.1
  252.5 31.7 %all-gather.2.cloned.1.call-start = ((), (), s32[]{:S(2)}) async-start(), calls=%async_computation.1 | async-start | bytes 1114112 | tf_op jit(solution)/shard_map/while/body/eval_jaxpr/all_gather | solution.py:80
  253.2 106.6 %reduce-scatter.2.cloned.1.call-start = ((), (), s32[]{:S(2)}) async-start(), calls=%async_computation.2 | async-start | bytes 2228224 | tf_op jit(solution)/shard_map/while/body/eval_jaxpr/reduce_scatter | solution.py:85
  296.1 71.1 %collective-permute-start = (bf16[128,256]{1,0:T(8,128)(2,1)S(1)}, bf16[128,256]{1,0:T(8,128)(2,1)S(1)}, u32[]{:S(2)}, u32[]{:S(2)}) collective-permute-start(bf16[128,256]{1,0:T(8,128)(2,1)S(1)} %copy-done.2), channel_id=1, source_target_pairs={{7,0},{0,1},{1,2},{2,3},{3,4},{4,5},{5,6},{6,7},{15,8},{8,9},{9,10... | collective-permute-start | bytes 196616 | tf_op jit(solution)/shard_map/while/body/eval_jaxpr/ppermute | solution.py:12
  360.7 8.7 collective-permute-start.1
  369.3 31.8 %all-gather.2.cloned.1.call-start = ((), (), s32[]{:S(2)}) async-start(), calls=%async_computation.1 | async-start | bytes 1114112 | tf_op jit(solution)/shard_map/while/body/eval_jaxpr/all_gather | solution.py:80
  370.0 106.6 %reduce-scatter.2.cloned.1.call-start = ((), (), s32[]{:S(2)}) async-start(), calls=%async_computation.2 | async-start | bytes 2228224 | tf_op jit(solution)/shard_map/while/body/eval_jaxpr/reduce_scatter | solution.py:85
  413.0 71.1 %collective-permute-start = (bf16[128,256]{1,0:T(8,128)(2,1)S(1)}, bf16[128,256]{1,0:T(8,128)(2,1)S(1)}, u32[]{:S(2)}, u32[]{:S(2)}) collective-permute-start(bf16[128,256]{1,0:T(8,128)(2,1)S(1)} %copy-done.2), channel_id=1, source_target_pairs={{7,0},{0,1},{1,2},{2,3},{3,4},{4,5},{5,6},{6,7},{15,8},{8,9},{9,10... | collective-permute-start | bytes 196616 | tf_op jit(solution)/shard_map/while/body/eval_jaxpr/ppermute | solution.py:12
  477.6 8.7 collective-permute-start.1
  486.2 32.0 %all-gather.2.cloned.1.call-start = ((), (), s32[]{:S(2)}) async-start(), calls=%async_computation.1 | async-start | bytes 1114112 | tf_op jit(solution)/shard_map/while/body/eval_jaxpr/all_gather | solution.py:80
  487.0 106.8 %reduce-scatter.2.cloned.1.call-start = ((), (), s32[]{:S(2)}) async-start(), calls=%async_computation.2 | async-start | bytes 2228224 | tf_op jit(solution)/shard_map/while/body/eval_jaxpr/reduce_scatter | solution.py:85
  530.1 71.1 %collective-permute-start = (bf16[128,256]{1,0:T(8,128)(2,1)S(1)}, bf16[128,256]{1,0:T(8,128)(2,1)S(1)}, u32[]{:S(2)}, u32[]{:S(2)}) collective-permute-start(bf16[128,256]{1,0:T(8,128)(2,1)S(1)} %copy-done.2), channel_id=1, source_target_pairs={{7,0},{0,1},{1,2},{2,3},{3,4},{4,5},{5,6},{6,7},{15,8},{8,9},{9,10... | collective-permute-start | bytes 196616 | tf_op jit(solution)/shard_map/while/body/eval_jaxpr/ppermute | solution.py:12
  594.7 8.7 collective-permute-start.1
  603.4 32.0 %all-gather.2.cloned.1.call-start = ((), (), s32[]{:S(2)}) async-start(), calls=%async_computation.1 | async-start | bytes 1114112 | tf_op jit(solution)/shard_map/while/body/eval_jaxpr/all_gather | solution.py:80
  604.1 106.8 %reduce-scatter.2.cloned.1.call-start = ((), (), s32[]{:S(2)}) async-start(), calls=%async_computation.2 | async-start | bytes 2228224 | tf_op jit(solution)/shard_map/while/body/eval_jaxpr/reduce_scatter | solution.py:85
  647.2 71.1 %collective-permute-start = (bf16[128,256]{1,0:T(8,128)(2,1)S(1)}, bf16[128,256]{1,0:T(8,128)(2,1)S(1)}, u32[]{:S(2)}, u32[]{:S(2)}) collective-permute-start(bf16[128,256]{1,0:T(8,128)(2,1)S(1)} %copy-done.2), channel_id=1, source_target_pairs={{7,0},{0,1},{1,2},{2,3},{3,4},{4,5},{5,6},{6,7},{15,8},{8,9},{9,10... | collective-permute-start | bytes 196616 | tf_op jit(solution)/shard_map/while/body/eval_jaxpr/ppermute | solution.py:12
  711.8 8.7 collective-permute-start.1
  720.4 32.0 %all-gather.2.cloned.1.call-start = ((), (), s32[]{:S(2)}) async-start(), calls=%async_computation.1 | async-start | bytes 1114112 | tf_op jit(solution)/shard_map/while/body/eval_jaxpr/all_gather | solution.py:80
  721.2 106.8 %reduce-scatter.2.cloned.1.call-start = ((), (), s32[]{:S(2)}) async-start(), calls=%async_computation.2 | async-start | bytes 2228224 | tf_op jit(solution)/shard_map/while/body/eval_jaxpr/reduce_scatter | solution.py:85
  764.3 71.0 %collective-permute-start = (bf16[128,256]{1,0:T(8,128)(2,1)S(1)}, bf16[128,256]{1,0:T(8,128)(2,1)S(1)}, u32[]{:S(2)}, u32[]{:S(2)}) collective-permute-start(bf16[128,256]{1,0:T(8,128)(2,1)S(1)} %copy-done.2), channel_id=1, source_target_pairs={{7,0},{0,1},{1,2},{2,3},{3,4},{4,5},{5,6},{6,7},{15,8},{8,9},{9,10... | collective-permute-start | bytes 196616 | tf_op jit(solution)/shard_map/while/body/eval_jaxpr/ppermute | solution.py:12
  828.9 8.7 collective-permute-start.1
  837.5 31.5 %all-gather.2.cloned.1.call-start = ((), (), s32[]{:S(2)}) async-start(), calls=%async_computation.1 | async-start | bytes 1114112 | tf_op jit(solution)/shard_map/while/body/eval_jaxpr/all_gather | solution.py:80
  838.2 106.4 %reduce-scatter.2.cloned.1.call-start = ((), (), s32[]{:S(2)}) async-start(), calls=%async_computation.2 | async-start | bytes 2228224 | tf_op jit(solution)/shard_map/while/body/eval_jaxpr/reduce_scatter | solution.py:85
  880.9 71.1 %collective-permute-start = (bf16[128,256]{1,0:T(8,128)(2,1)S(1)}, bf16[128,256]{1,0:T(8,128)(2,1)S(1)}, u32[]{:S(2)}, u32[]{:S(2)}) collective-permute-start(bf16[128,256]{1,0:T(8,128)(2,1)S(1)} %copy-done.2), channel_id=1, source_target_pairs={{7,0},{0,1},{1,2},{2,3},{3,4},{4,5},{5,6},{6,7},{15,8},{8,9},{9,10... | collective-permute-start | bytes 196616 | tf_op jit(solution)/shard_map/while/body/eval_jaxpr/ppermute | solution.py:12
  945.5 8.7 collective-permute-start.1
  (32 other events, 333.5 us)
Sparse Core Ops, SparseCore 0:
  15.4 35.0 all-gather.1
  62.5 63.5 reduce-scatter.1
  138.7 28.6 all-gather.1
  179.4 63.5 reduce-scatter.1
  255.3 28.8 all-gather.1
  296.2 63.5 reduce-scatter.1
  372.4 28.6 all-gather.1
  413.1 63.5 reduce-scatter.1
  489.3 28.8 all-gather.1
  530.2 63.5 reduce-scatter.1
  606.5 28.8 all-gather.1
  647.3 63.5 reduce-scatter.1
  723.6 28.8 all-gather.1
  764.4 63.5 reduce-scatter.1
  840.3 28.6 all-gather.1
  881.0 63.5 reduce-scatter.1
where the time goes:
time: 963 us; the launch traced here: 962 us
  waiting for transfers between devices  746 us (77%)
  matrix products  96.2 us (10%)
  starting transfers between devices  45.5 us (5%)
  other arithmetic  33 us (3%)
  local copies, waits for them, and re-layouts  26.6 us (3%)
  between operations  13.8 us (1%)
    reduce_scatter x8, waiting for transfers between devices, turn_step(): shares = lax.psum_scatter(terms, 'outer', scatter_dimension=0, tiled=True)  487 us
    all_gather x8, waiting for transfers between devices, turn_step(): grouped = lax.all_gather(moving, 'outer', axis=0, tiled=True)  241 us
    ppermute x16, starting transfers between devices, from_behind(): return lax.ppermute(block, axis, route)  45.1 us
    dot_general x8, matrix products, tile_terms(): jnp.einsum('htk,kd->thd', dscores_half, key_part, preferred_element_type=...  29.4 us
    dot_general x8, matrix products, tile_terms(): jnp.einsum('thd,kd->htk', grad_heads, value_part, preferred_element_type=...  22.2 us
    while x72, local copies, waits for them, and re-layouts  20.5 us
  transfers between devices with their start and end apart: 32, of which 24 were waited for; matrix products, arithmetic and copies ran while one was open for 5% of the time, Pallas kernels for 0%

commit v1 on v0

v1 whole, which is shorter than its diff:
```python
import functools
import math

import jax
import jax.numpy as jnp
from jax import lax
from jax.experimental import pallas as pl
from jax.experimental.pallas import tpu as pltpu
from jax.sharding import PartitionSpec as P

WIDTH = 128
BLOCK = 64
KEY_TILE = 512
PAIR = 2
HALF_HEADS = 4
COLS = HALF_HEADS * BLOCK
LOG2E = 1.4426950408889634
AXES = ("outer", "inner")


def linear(x, y, z, core):
    return (((y % 2) * 4 + z) * 2 + core) * 8 + x * 2 + y // 2


def place(index):
    inner = index % 8
    outer = index // 8
    return inner // 2, (inner % 2) * 2 + outer // 8, (outer // 2) % 4, outer % 2


def shift(block, dx=0, dy=0, dz=0, dcore=0):
    route = []
    for index in range(128):
        x, y, z, core = place(index)
        to = linear((x + dx) % 4, (y + dy) % 4, (z + dz) % 4, (core + dcore) % 2)
        route.append((index, to))
    return lax.ppermute(block, AXES, route)


def nt(a, b):
    return lax.dot_general(a, b, (((1,), (1,)), ((), ())), preferred_element_type=jnp.float32)


def nn(a, b):
    return lax.dot_general(a, b, (((1,), (0,)), ((), ())), preferred_element_type=jnp.float32)


def attend_kernel(
    q_rank, k_rank, q_sorted, k_sorted,
    pay0, pay1, pay2, pay3, st0, st1, st2, st3, kv_own, kv_sib,
    dq0, dq1, dq2, dq3, dkv_own, dkv_sib,
    ks, vs, kt, dk, dv, qs, gs, dq, lse_s, del_s, s_scr, p_scr, ti, tj,
):
    pays, stats, dqs = (pay0, pay1, pay2, pay3), (st0, st1, st2, st3), (dq0, dq1, dq2, dq3)
    key_blocks, query_blocks = k_rank.shape[0], q_rank.shape[0]
    per_tile = KEY_TILE // BLOCK
    key_tiles, query_tiles = key_blocks // per_tile, query_blocks // PAIR
    half_keys = key_blocks // 2
    span = PAIR * COLS
    scale = 1.0 / math.sqrt(WIDTH)
    factor = scale * LOG2E

    for half, kv in enumerate((kv_own, kv_sib)):
        def bring(r, _, kv=kv, half=half):
            src = pl.multiple_of(r * BLOCK, BLOCK)
            dst = pl.multiple_of(k_rank[half * half_keys + r] * BLOCK, BLOCK)
            ks[pl.ds(dst, BLOCK), :] = kv[pl.ds(src, BLOCK), :WIDTH]
            vs[pl.ds(dst, BLOCK), :] = kv[pl.ds(src, BLOCK), WIDTH:]
            return 0
        lax.fori_loop(0, half_keys, bring, 0, unroll=4)

    def ready(j, _):
        kt[j] = ks[pl.ds(pl.multiple_of(j * KEY_TILE, KEY_TILE), KEY_TILE), :].T
        dk[j] = jnp.zeros((KEY_TILE, WIDTH), jnp.float32)
        dv[j] = jnp.zeros((KEY_TILE, WIDTH), jnp.float32)
        return 0
    lax.fori_loop(0, key_tiles, ready, 0)

    for s in range(query_blocks):
        pay, stat, rows = pays[s // 4], stats[s // 4], (s % 4) * BLOCK
        rank = q_rank[s]
        dst = pl.multiple_of(rank * COLS, COLS)
        for h in range(HALF_HEADS):
            qs[pl.ds(dst + h * BLOCK, BLOCK), :] = pay[rows:rows + BLOCK, h * WIDTH:(h + 1) * WIDTH]
            gs[pl.ds(dst + h * BLOCK, BLOCK), :] = pay[
                rows:rows + BLOCK, (HALF_HEADS + h) * WIDTH:(HALF_HEADS + h + 1) * WIDTH]
        top, lanes = (s % 4) // 2 * 8, slice((s % 2) * BLOCK, (s % 2 + 1) * BLOCK)
        lse_s[pl.ds(rank, 1), :] = jnp.concatenate(
            [stat[top + h:top + h + 1, lanes] for h in range(HALF_HEADS)], axis=1) * LOG2E
        del_s[pl.ds(rank, 1), :] = jnp.concatenate(
            [stat[top + HALF_HEADS + h:top + HALF_HEADS + h + 1, lanes] for h in range(HALF_HEADS)],
            axis=1)

    def listing(i, carry):
        n, total = carry
        dq[i] = jnp.zeros((WIDTH, span), jnp.float32)
        top = q_sorted[i * PAIR + PAIR - 1]
        n = lax.while_loop(
            lambda n: (n < key_blocks) & (k_sorted[jnp.minimum(n, key_blocks - 1)] <= top),
            lambda n: n + 1, n)
        def put(j, total):
            ti[total] = i
            tj[total] = j
            return total + 1
        return n, lax.fori_loop(0, (n + per_tile - 1) // per_tile, put, total)
    _, total = lax.fori_loop(0, query_tiles, listing, (jnp.int32(0), jnp.int32(0)))
    for extra in range(2):
        ti[total + extra] = 0
        tj[total + extra] = 0

    in_query = lax.broadcasted_iota(jnp.int32, (1, span), 1) % BLOCK
    in_key = lax.broadcasted_iota(jnp.int32, (BLOCK, span), 0)

    def front(t, slot):
        i, j = ti[t], tj[t]
        ko, qo = pl.multiple_of(j * KEY_TILE, KEY_TILE), pl.multiple_of(i * span, span)
        s_scr[slot] = nt(ks[pl.ds(ko, KEY_TILE), :], qs[pl.ds(qo, span), :])
        p_scr[slot] = nt(vs[pl.ds(ko, KEY_TILE), :], gs[pl.ds(qo, span), :])

    def back(t, slot):
        i, j = ti[t], tj[t]
        live = t < total
        qo = pl.multiple_of(i * span, span)
        lse = jnp.concatenate([lse_s[pl.ds(i * PAIR + u, 1), :] for u in range(PAIR)], axis=1)
        delta = jnp.concatenate([del_s[pl.ds(i * PAIR + u, 1), :] for u in range(PAIR)], axis=1)
        query_pos = in_query + jnp.concatenate(
            [jnp.full((1, COLS), jnp.where(live, q_sorted[i * PAIR + u] * BLOCK, -BLOCK), jnp.int32)
             for u in range(PAIR)], axis=1)
        probs_parts, dscores_parts = [], []
        for u in range(per_tile):
            scores = s_scr[slot, u * BLOCK:(u + 1) * BLOCK, :]
            dprobs = p_scr[slot, u * BLOCK:(u + 1) * BLOCK, :]
            allowed = in_key <= query_pos - k_sorted[j * per_tile + u] * BLOCK
            probs = jnp.where(allowed, jnp.exp2(scores * factor - lse), 0.0)
            dscores_parts.append((probs * (dprobs - delta)).astype(jnp.bfloat16))
            probs_parts.append(probs.astype(jnp.bfloat16))
        probs_half = jnp.concatenate(probs_parts, axis=0)
        dscores_half = jnp.concatenate(dscores_parts, axis=0)
        dv[j] += nn(probs_half, gs[pl.ds(qo, span), :])
        dk[j] += nn(dscores_half, qs[pl.ds(qo, span), :])
        dq[i] += nn(kt[j], dscores_half)

    front(0, 0)

    def two(h, _):
        front(2 * h + 1, 1)
        back(2 * h, 0)
        front(2 * h + 2, 0)
        back(2 * h + 1, 1)
        return 0
    lax.fori_loop(0, (total + 1) // 2, two, 0)

    def turn(i, _):
        rows = (dq[i].T * scale).astype(jnp.bfloat16)
        qs[pl.ds(pl.multiple_of(i * span, span), span), :] = rows
        return 0
    lax.fori_loop(0, query_tiles, turn, 0)
    for s in range(query_blocks):
        src = pl.multiple_of(q_rank[s] * COLS, COLS)
        rows = (s % 4) * BLOCK
        for h in range(HALF_HEADS):
            dqs[s // 4][rows:rows + BLOCK, h * WIDTH:(h + 1) * WIDTH] = qs[
                pl.ds(src + h * BLOCK, BLOCK), :]
    for half, out in enumerate((dkv_own, dkv_sib)):
        def give(r, _, out=out, half=half):
            dst = pl.multiple_of(r * BLOCK, BLOCK)
            rank = k_rank[half * half_keys + r]
            j, src = rank // per_tile, pl.multiple_of(rank % per_tile * BLOCK, BLOCK)
            out[pl.ds(dst, BLOCK), :WIDTH] = (dk[j, pl.ds(src, BLOCK), :] * scale).astype(jnp.bfloat16)
            out[pl.ds(dst, BLOCK), WIDTH:] = dv[j, pl.ds(src, BLOCK), :].astype(jnp.bfloat16)
            return 0
        lax.fori_loop(0, half_keys, give, 0, unroll=4)


def attend(q_rank, k_rank, q_sorted, k_sorted, pays, stats, kv_own, kv_sib):
    key_blocks, query_blocks = k_rank.shape[0], q_rank.shape[0]
    keys = key_blocks * BLOCK
    key_tiles, query_tiles = keys // KEY_TILE, query_blocks // PAIR
    span = PAIR * COLS
    bf16, f32 = jnp.bfloat16, jnp.float32
    smem, vmem = pl.BlockSpec(memory_space=pltpu.SMEM), pl.BlockSpec(memory_space=pltpu.VMEM)
    listed = query_tiles * key_tiles + 2
    return pl.pallas_call(
        attend_kernel,
        in_specs=[smem] * 4 + [vmem] * 10,
        out_specs=[vmem] * 6,
        out_shape=[jax.ShapeDtypeStruct((4 * BLOCK, HALF_HEADS * WIDTH), bf16)] * 4
        + [jax.ShapeDtypeStruct((keys // 2, 2 * WIDTH), bf16)] * 2,
        scratch_shapes=[
            pltpu.VMEM((keys, WIDTH), bf16),
            pltpu.VMEM((keys, WIDTH), bf16),
            pltpu.VMEM((key_tiles, WIDTH, KEY_TILE), bf16),
            pltpu.VMEM((key_tiles, KEY_TILE, WIDTH), f32),
            pltpu.VMEM((key_tiles, KEY_TILE, WIDTH), f32),
            pltpu.VMEM((query_blocks * COLS, WIDTH), bf16),
            pltpu.VMEM((query_blocks * COLS, WIDTH), bf16),
            pltpu.VMEM((query_tiles, WIDTH, span), f32),
            pltpu.VMEM((query_blocks, COLS), f32),
            pltpu.VMEM((query_blocks, COLS), f32),
            pltpu.VMEM((2, KEY_TILE, span), f32),
            pltpu.VMEM((2, KEY_TILE, span), f32),
            pltpu.SMEM((listed,), jnp.int32),
            pltpu.SMEM((listed,), jnp.int32),
        ],
        compiler_params=pltpu.CompilerParams(vmem_limit_bytes=48 * 1024 * 1024),
    )(q_rank, k_rank, q_sorted, k_sorted, *pays, *stats, kv_own, kv_sib)


def ranked(block_order, blocks):
    listed = jnp.arange(block_order.shape[0], dtype=jnp.int32)
    pos = jnp.sum(jnp.where(blocks[:, None] == listed[None, :], block_order[None, :], 0), axis=1)
    rank = jnp.sum((pos[None, :] < pos[:, None]).astype(jnp.int32), axis=1)
    at = jnp.arange(blocks.shape[0], dtype=jnp.int32)
    return rank, jnp.sum(jnp.where(rank[None, :] == at[:, None], pos[None, :], 0), axis=1)


def total_of(parts):
    return functools.reduce(lambda a, b: a + b, [p.astype(jnp.float32) for p in parts])


def body(query_rows, key_rows, value_rows, saved_output, output_grad, logsumexp, block_order):
    rows = query_rows.shape[0]
    half = HALF_HEADS * WIDTH
    x, y, z, core = place(lax.axis_index("outer") * 8 + lax.axis_index("inner"))
    first = core == 0

    def mine(array):
        return jnp.where(first, array[:, :half], array[:, half:])

    def other(array):
        return jnp.where(first, array[:, half:], array[:, :half])

    kv = jnp.concatenate([key_rows, value_rows], axis=1)
    kv_line = jnp.concatenate([kv] + [shift(kv, dz=-d) for d in (1, 2, 3)], axis=0)
    sib = shift(jnp.concatenate([other(query_rows), other(output_grad)], axis=1), dcore=1)
    pay = jnp.concatenate(
        [jnp.concatenate([mine(query_rows), mine(output_grad)], axis=1), sib], axis=0)
    pays = [pay] + [shift(pay, dy=-d) for d in (1, 2, 3)]
    kv_own = jnp.concatenate([kv_line] + [shift(kv_line, dx=-d) for d in (1, 2, 3)], axis=0)
    kv_sib = shift(kv_own, dcore=1)

    heads = (rows, 2 * HALF_HEADS, WIDTH)
    delta = jnp.sum(
        output_grad.reshape(heads).astype(jnp.float32)
        * saved_output.reshape(heads).astype(jnp.float32), axis=2).T
    low = jnp.concatenate([logsumexp[:HALF_HEADS], delta[:HALF_HEADS]], axis=0)
    high = jnp.concatenate([logsumexp[HALF_HEADS:], delta[HALF_HEADS:]], axis=0)
    stat = jnp.concatenate(
        [jnp.where(first, low, high), shift(jnp.where(first, high, low), dcore=1)], axis=0)
    stats = [stat] + [shift(stat, dy=-d) for d in (1, 2, 3)]

    four = jnp.arange(4, dtype=jnp.int32)
    two = jnp.arange(2, dtype=jnp.int32)
    dy, cs, b = (a.reshape(-1) for a in jnp.meshgrid(four, two, two, indexing="ij"))
    q_rank, q_sorted = ranked(block_order, 2 * linear(x, (y + dy) % 4, z, (core + cs) % 2) + b)
    cs, dx, dz, b = (a.reshape(-1) for a in jnp.meshgrid(two, four, four, two, indexing="ij"))
    k_rank, k_sorted = ranked(
        block_order, 2 * linear((x + dx) % 4, y, (z + dz) % 4, (core + cs) % 2) + b)

    *dqs, dkv_own, dkv_sib = attend(
        q_rank, k_rank, q_sorted, k_sorted, pays, stats, kv_own, kv_sib)

    dkv = total_of([dkv_own, shift(dkv_sib, dcore=1)]).astype(jnp.bfloat16)
    dq = total_of([dqs[0]] + [shift(dqs[d], dy=d) for d in (1, 2, 3)]).astype(jnp.bfloat16)
    quarter = dkv.shape[0] // 4
    parts = [dkv[d * quarter:(d + 1) * quarter] for d in range(4)]
    line = total_of([parts[0]] + [shift(parts[d], dx=d) for d in (1, 2, 3)]).astype(jnp.bfloat16)
    parts = [line[d * rows:(d + 1) * rows] for d in range(4)]
    done = total_of([parts[0]] + [shift(parts[d], dz=d) for d in (1, 2, 3)])
    near, far = dq[:rows], shift(dq[rows:], dcore=1)
    query_grad = jnp.concatenate(
        [jnp.where(first, near, far), jnp.where(first, far, near)], axis=1)
    return (
        query_grad,
        done[:, :WIDTH].astype(jnp.bfloat16),
        done[:, WIDTH:].astype(jnp.bfloat16),
    )


def solution(mesh):
    rows = P(AXES, None)
    return jax.shard_map(
        body,
        mesh=mesh,
        in_specs=(rows, rows, rows, rows, rows, P(None, AXES), P()),
        out_specs=(rows, rows, rows),
        check_vma=False,
    )
```

time: 963 us -> 153 us (0.16)
  waiting for transfers between devices: 746 us -> 59.1 us
  matrix products: 96.2 us -> 0 us
  Pallas kernels: 0 us -> 36.9 us
  other arithmetic: 33 us -> 3.8 us
  local copies, waits for them, and re-layouts: 26.6 us -> 4.71 us
  between operations: 13.8 us -> 1.05 us
    reduce_scatter x8 -> x0, waiting for transfers between devices: 487 us -> none  [turn_step(): shares = lax.psum_scatter(terms, 'outer', scatter_dimension=0, tiled=True)]
    all_gather x8 -> x0, waiting for transfers between devices: 241 us -> none  [turn_step(): grouped = lax.all_gather(moving, 'outer', axis=0, tiled=True)]
    dot_general x40 -> x0, matrix products: 96.2 us -> none  [the longest x8 29.4 us: tile_terms(): jnp.einsum('htk,kd->thd', dscores_half, key_part, preferred_element_type=...]
    ppermute x16 -> x26, waiting for transfers between devices: 17.4 us -> 59.1 us  [shift(): return lax.ppermute(block, AXES, route)]
    pallas_call x0 -> x1, Pallas kernels: none -> 36.9 us  [attend(): pl.pallas_call(attend_kernel, in_specs=[smem] * 4 + [vmem] * 10, out_spec...]
    while x73 -> x0, local copies, waits for them, and re-layouts: 20.6 us -> none
    concatenate x9 -> x5, other arithmetic: 12.5 us -> 0.82 us  [the longest x1 0.73 us: body(): jnp.concatenate([jnp.where(first, near, far), jnp.where(first, far, near)...]
    ppermute x16 -> x26, starting transfers between devices: 45.1 us -> 47.4 us  [shift(): return lax.ppermute(block, AXES, route)]
  transfers between devices with their start and end apart: 32 -> 26, of which waited for: 24 -> 13; matrix products, arithmetic and copies ran while one was open for 5% -> 3% of each run, Pallas kernels for 0% -> 0%
where the time goes in v1:
time: 153 us
  waiting for transfers between devices  59.1 us (39%)
  starting transfers between devices  47.4 us (31%)
  Pallas kernels  36.9 us (24%)
  local copies, waits for them, and re-layouts  4.71 us (3%)
  other arithmetic  3.8 us (2%)
    ppermute x26, waiting for transfers between devices, shift(): return lax.ppermute(block, AXES, route)  59.1 us
    ppermute x26, starting transfers between devices, shift(): return lax.ppermute(block, AXES, route)  47.4 us
    pallas_call x1, Pallas kernels, attend(): pl.pallas_call(attend_kernel, in_specs=[smem] * 4 + [vmem] * 10, out_spec...  36.9 us
  transfers between devices with their start and end apart: 26, of which 13 were waited for; matrix products, arithmetic and copies ran while one was open for 3% of the time, Pallas kernels for 0%

profile of v1, /device:TPU:0, one launch (start us, length us, event | category | flops | bytes accessed | tf_op | source)
XLA Modules:
  0.0 152.9 jit_solution(15551199475620549052)
XLA Ops:
  0.6 0.8 constant_dynamic-update-slice_fusion.1
  1.4 0.8 constant_dynamic-update-slice_fusion
  2.2 2.1 %collective-permute-start.10 = (bf16[128,256]{1,0:T(8,128)(2,1)S(1)}, bf16[128,256]{1,0:T(8,128)(2,1)S(1)}, u32[]{:S(2)}, u32[]{:S(2)}) collective-permute-start(bf16[128,256]{1,0:T(8,128)(2,1)S(1)} %get-tuple-element.29), channel_id=1, source_target_pairs={{0,16},{1,17},{2,18},{3,19},{4,20},{5,21},{6,22},{7,23},{8,24},{9,... | collective-permute-start | bytes 196616 | tf_op jit(solution)/shard_map/ppermute | solution.py:37
  4.3 3.6 %collective-permute-start.9 = (bf16[128,256]{1,0:T(8,128)(2,1)S(1)}, bf16[128,256]{1,0:T(8,128)(2,1)S(1)}, u32[]{:S(2)}, u32[]{:S(2)}) collective-permute-start(bf16[128,256]{1,0:T(8,128)(2,1)S(1)} %get-tuple-element.29), channel_id=1, source_target_pairs={{0,32},{1,33},{2,34},{3,35},{4,36},{5,37},{6,38},{7,39},{8,40},{9,... | collective-permute-start | bytes 196616 | tf_op jit(solution)/shard_map/ppermute | solution.py:37
  7.8 1.0 collective-permute-start.8
  8.8 1.1 multiply_bitcast_fusion
  12.3 1.6 %collective-permute-start.13 = (bf16[512,256]{1,0:T(8,128)(2,1)S(1)}, bf16[512,256]{1,0:T(8,128)(2,1)S(1)}, u32[]{:S(2)}, u32[]{:S(2)}) collective-permute-start(bf16[512,256]{1,0:T(8,128)(2,1)S(1)} %pad_maximum_fusion.2), channel_id=1, source_target_pairs={{0,2},{1,3},{2,4},{3,5},{4,6},{5,7},{6,0},{7,1},{8,10},{9,11},{10,... | collective-permute-start | bytes 786440 | tf_op jit(solution)/shard_map/ppermute | solution.py:37
  13.8 2.7 %collective-permute-start.12 = (bf16[512,256]{1,0:T(8,128)(2,1)S(1)}, bf16[512,256]{1,0:T(8,128)(2,1)S(1)}, u32[]{:S(2)}, u32[]{:S(2)}) collective-permute-start(bf16[512,256]{1,0:T(8,128)(2,1)S(1)} %pad_maximum_fusion.2), channel_id=1, source_target_pairs={{0,4},{1,5},{2,6},{3,7},{4,0},{5,1},{6,2},{7,3},{8,12},{9,13},{10,... | collective-permute-start | bytes 786440 | tf_op jit(solution)/shard_map/ppermute | solution.py:37
  16.6 1.4 collective-permute-start.11
  18.0 10.2 %collective-permute-done.11 = bf16[512,256]{1,0:T(8,128)(2,1)S(1)} collective-permute-done((bf16[512,256]{1,0:T(8,128)(2,1)S(1)}, bf16[512,256]{1,0:T(8,128)(2,1)S(1)}, u32[]{:S(2)}, u32[]{:S(2)}) %collective-permute-start.11) | collective-permute-done | bytes 262176 | tf_op jit(solution)/shard_map/ppermute | solution.py:37
  29.3 1.6 %collective-permute-start.3 = (bf16[256,1024]{1,0:T(8,128)(2,1)S(1)}, bf16[256,1024]{1,0:T(8,128)(2,1)S(1)}, u32[]{:S(2)}, u32[]{:S(2)}) collective-permute-start(bf16[256,1024]{1,0:T(8,128)(2,1)S(1)} %pad_maximum_fusion.pay0), channel_id=1, source_target_pairs={{0,64},{1,65},{2,66},{3,67},{4,68},{5,69},{6,70},{7,71},{8,72},{9,... | collective-permute-start | bytes 1572872 | tf_op jit(solution)/shard_map/ppermute | solution.py:37
  30.9 2.9 %collective-permute-start.2 = (bf16[256,1024]{1,0:T(8,128)(2,1)S(1)}, bf16[256,1024]{1,0:T(8,128)(2,1)S(1)}, u32[]{:S(2)}, u32[]{:S(2)}) collective-permute-start(bf16[256,1024]{1,0:T(8,128)(2,1)S(1)} %pad_maximum_fusion.pay0), channel_id=1, source_target_pairs={{0,1},{1,0},{2,3},{3,2},{4,5},{5,4},{6,7},{7,6},{8,9},{9,8},{10,11... | collective-permute-start | bytes 1572872 | tf_op jit(solution)/shard_map/ppermute | solution.py:37
  33.8 1.3 collective-permute-start.1
  36.3 17.9 %collective-permute-done.7.st3 = f32[16,128]{1,0:T(8,128)S(1)} collective-permute-done((f32[16,128]{1,0:T(8,128)S(1)}, f32[16,128]{1,0:T(8,128)S(1)}, u32[]{:S(2)}, u32[]{:S(2)}) %collective-permute-start.7) | collective-permute-done | bytes 8224 | tf_op jit(solution)/shard_map/ppermute | solution.py:37
  54.2 4.1 %collective-permute-start.6 = (f32[16,128]{1,0:T(8,128)S(1)}, f32[16,128]{1,0:T(8,128)S(1)}, u32[]{:S(2)}, u32[]{:S(2)}) collective-permute-start(f32[16,128]{1,0:T(8,128)S(1)} %pad_maximum_fusion.4.st0), channel_id=1, source_target_pairs={{0,1},{1,0},{2,3},{3,2},{4,5},{5,4},{6,7},{7,6},{8,9},{9,8},{10,11... | collective-permute-start | bytes 24584 | tf_op jit(solution)/shard_map/ppermute | solution.py:37
  58.4 1.5 collective-permute-done.6.st2
  59.9 3.3 %collective-permute-start.5 = (f32[16,128]{1,0:T(8,128)S(1)}, f32[16,128]{1,0:T(8,128)S(1)}, u32[]{:S(2)}, u32[]{:S(2)}) collective-permute-start(f32[16,128]{1,0:T(8,128)S(1)} %pad_maximum_fusion.4.st0), channel_id=1, source_target_pairs={{0,65},{1,64},{2,67},{3,66},{4,69},{5,68},{6,71},{7,70},{8,73},{9,... | collective-permute-start | bytes 24584 | tf_op jit(solution)/shard_map/ppermute | solution.py:37
  63.3 1.3 collective-permute-done.5.st1
  64.6 1.0 copy-done.1
  65.6 36.9 %shard_map.94 = (bf16[256,512]{1,0:T(8,128)(2,1)S(1)}, bf16[256,512]{1,0:T(8,128)(2,1)S(1)}, bf16[256,512]{1,0:T(8,128)(2,1)S(1)}, bf16[256,512]{1,0:T(8,128)(2,...) custom-call(s32[16]{0:T(128)S(1)} %convert_reduce_fusion.1.q_rank, ...), custom_call_target="tpu_custom_call" | custom-call | tf_op jit(solution)/shard_map/pallas_call | solution.py:183
  102.7 6.6 %collective-permute-start.16 = (bf16[256,512]{1,0:T(8,128)(2,1)S(1)}, bf16[256,512]{1,0:T(8,128)(2,1)S(1)}, u32[]{:S(2)}, u32[]{:S(2)}) collective-permute-start(bf16[256,512]{1,0:T(8,128)(2,1)S(1)} %get-tuple-element.11), channel_id=1, source_target_pairs={{0,1},{1,0},{2,3},{3,2},{4,5},{5,4},{6,7},{7,6},{8,9},{9,8},{10,11... | collective-permute-start | bytes 786440 | tf_op jit(solution)/shard_map/ppermute | solution.py:37
  109.2 1.8 %collective-permute-start.17 = (bf16[256,512]{1,0:T(8,128)(2,1)S(1)}, bf16[256,512]{1,0:T(8,128)(2,1)S(1)}, u32[]{:S(2)}, u32[]{:S(2)}) collective-permute-start(bf16[256,512]{1,0:T(8,128)(2,1)S(1)} %get-tuple-element.12), channel_id=1, source_target_pairs={{0,65},{1,64},{2,67},{3,66},{4,69},{5,68},{6,71},{7,70},{8,73},{9,... | collective-permute-start | bytes 786440 | tf_op jit(solution)/shard_map/ppermute | solution.py:37
  111.0 3.7 %collective-permute-done.15 = bf16[256,512]{1,0:T(8,128)(2,1)S(1)} collective-permute-done((bf16[256,512]{1,0:T(8,128)(2,1)S(1)}, bf16[256,512]{1,0:T(8,128)(2,1)S(1)}, u32[]{:S(2)}, u32[]{:S(2)}) %collective-permute-start.15) | collective-permute-done | bytes 262176 | tf_op jit(solution)/shard_map/ppermute | solution.py:37
  114.7 6.8 %collective-permute-done.16 = bf16[256,512]{1,0:T(8,128)(2,1)S(1)} collective-permute-done((bf16[256,512]{1,0:T(8,128)(2,1)S(1)}, bf16[256,512]{1,0:T(8,128)(2,1)S(1)}, u32[]{:S(2)}, u32[]{:S(2)}) %collective-permute-start.16) | collective-permute-done | bytes 262176 | tf_op jit(solution)/shard_map/ppermute | solution.py:37
  122.2 7.2 %collective-permute-start.22 = (bf16[512,256]{1,0:T(8,128)(2,1)S(1)}, bf16[512,256]{1,0:T(8,128)(2,1)S(1)}, u32[]{:S(2)}, u32[]{:S(2)}) collective-permute-start(bf16[512,256]{1,0:T(8,128)(2,1)S(1)} %get-tuple-element.16), channel_id=1, source_target_pairs={{0,6},{1,7},{2,0},{3,1},{4,2},{5,3},{6,4},{7,5},{8,14},{9,15},{10,... | collective-permute-start | bytes 786440 | tf_op jit(solution)/shard_map/ppermute | solution.py:37
  129.3 1.4 collective-permute-start.21
  130.8 5.5 %collective-permute-done.20 = bf16[512,256]{1,0:T(8,128)(2,1)S(1)} collective-permute-done((bf16[512,256]{1,0:T(8,128)(2,1)S(1)}, bf16[512,256]{1,0:T(8,128)(2,1)S(1)}, u32[]{:S(2)}, u32[]{:S(2)}) %collective-permute-start.20) | collective-permute-done | bytes 262176 | tf_op jit(solution)/shard_map/ppermute | solution.py:37
  136.2 5.0 %collective-permute-done.22 = bf16[512,256]{1,0:T(8,128)(2,1)S(1)} collective-permute-done((bf16[512,256]{1,0:T(8,128)(2,1)S(1)}, bf16[512,256]{1,0:T(8,128)(2,1)S(1)}, u32[]{:S(2)}, u32[]{:S(2)}) %collective-permute-start.22) | collective-permute-done | bytes 262176 | tf_op jit(solution)/shard_map/ppermute | solution.py:37
  141.2 1.8 %collective-permute-done.21 = bf16[512,256]{1,0:T(8,128)(2,1)S(1)} collective-permute-done((bf16[512,256]{1,0:T(8,128)(2,1)S(1)}, bf16[512,256]{1,0:T(8,128)(2,1)S(1)}, u32[]{:S(2)}, u32[]{:S(2)}) %collective-permute-start.21) | collective-permute-done | bytes 262176 | tf_op jit(solution)/shard_map/ppermute | solution.py:37
  143.3 3.2 %collective-permute-start.25 = (bf16[128,256]{1,0:T(8,128)(2,1)S(1)}, bf16[128,256]{1,0:T(8,128)(2,1)S(1)}, u32[]{:S(2)}, u32[]{:S(2)}) collective-permute-start(bf16[128,256]{1,0:T(8,128)(2,1)S(1)} %get-tuple-element.21), channel_id=1, source_target_pairs={{0,48},{1,49},{2,50},{3,51},{4,52},{5,53},{6,54},{7,55},{8,56},{9,... | collective-permute-start | bytes 196616 | tf_op jit(solution)/shard_map/ppermute | solution.py:37
  147.2 1.5 collective-permute-done.23
  149.0 3.3 %collective-permute-done.24 = bf16[128,256]{1,0:T(8,128)(2,1)S(1)} collective-permute-done((bf16[128,256]{1,0:T(8,128)(2,1)S(1)}, bf16[128,256]{1,0:T(8,128)(2,1)S(1)}, u32[]{:S(2)}, u32[]{:S(2)}) %collective-permute-start.24) | collective-permute-done | bytes 65568 | tf_op jit(solution)/shard_map/ppermute | solution.py:37
  (84 shorter events, 7.2 us)
Async XLA Ops:
  2.2 10.0 %collective-permute-start.10 = (bf16[128,256]{1,0:T(8,128)(2,1)S(1)}, bf16[128,256]{1,0:T(8,128)(2,1)S(1)}, u32[]{:S(2)}, u32[]{:S(2)}) collective-permute-start(bf16[128,256]{1,0:T(8,128)(2,1)S(1)} %get-tuple-element.29), channel_id=1, source_target_pairs={{0,16},{1,17},{2,18},{3,19},{4,20},{5,21},{6,22},{7,23},{8,24},{9,... | collective-permute-start | bytes 196616 | tf_op jit(solution)/shard_map/ppermute | solution.py:37
  4.3 8.0 %collective-permute-start.9 = (bf16[128,256]{1,0:T(8,128)(2,1)S(1)}, bf16[128,256]{1,0:T(8,128)(2,1)S(1)}, u32[]{:S(2)}, u32[]{:S(2)}) collective-permute-start(bf16[128,256]{1,0:T(8,128)(2,1)S(1)} %get-tuple-element.29), channel_id=1, source_target_pairs={{0,32},{1,33},{2,34},{3,35},{4,36},{5,37},{6,38},{7,39},{8,40},{9,... | collective-permute-start | bytes 196616 | tf_op jit(solution)/shard_map/ppermute | solution.py:37
  7.8 4.4 %collective-permute-start.8 = (bf16[128,256]{1,0:T(8,128)(2,1)S(1)}, bf16[128,256]{1,0:T(8,128)(2,1)S(1)}, u32[]{:S(2)}, u32[]{:S(2)}) collective-permute-start(bf16[128,256]{1,0:T(8,128)(2,1)S(1)} %get-tuple-element.29), channel_id=1, source_target_pairs={{0,48},{1,49},{2,50},{3,51},{4,52},{5,53},{6,54},{7,55},{8,56},{9,... | collective-permute-start | bytes 196616 | tf_op jit(solution)/shard_map/ppermute | solution.py:37
  9.9 0.7 copy-start.5
  10.0 1.0 copy-start.2
  10.0 1.0 copy-start.3
  10.6 24.7 %collective-permute-start.4 = (f32[8,128]{1,0:T(8,128)S(1)}, f32[8,128]{1,0:T(8,128)S(1)}, u32[]{:S(2)}, u32[]{:S(2)}) collective-permute-start(f32[8,128]{1,0:T(8,128)S(1)} %get-tuple-element.34), channel_id=1, source_target_pairs={{0,8},{1,9},{2,10},{3,11},{4,12},{5,13},{6,14},{7,15},{8,0},{9,1},... | collective-permute-start | bytes 12296 | tf_op jit(solution)/shard_map/ppermute | solution.py:37
  11.1 18.1 %collective-permute-start = (bf16[128,1024]{1,0:T(8,128)(2,1)S(1)}, bf16[128,1024]{1,0:T(8,128)(2,1)S(1)}, u32[]{:S(2)}, u32[]{:S(2)}) collective-permute-start(bf16[128,1024]{1,0:T(8,128)(2,1)S(1)} %pad_maximum_fusion.1), channel_id=1, source_target_pairs={{0,8},{1,9},{2,10},{3,11},{4,12},{5,13},{6,14},{7,15},{8,0},{9,1},... | collective-permute-start | bytes 786440 | tf_op jit(solution)/shard_map/ppermute | solution.py:37
  12.3 16.6 %copy-start.4 = (s32[256]{0:T(256)S(1)}, s32[256]{0:T(256)}, u32[]{:S(2)}) copy-start(s32[256]{0:T(256)} %param.13) | copy-start | bytes 3076
  12.3 16.4 %collective-permute-start.13 = (bf16[512,256]{1,0:T(8,128)(2,1)S(1)}, bf16[512,256]{1,0:T(8,128)(2,1)S(1)}, u32[]{:S(2)}, u32[]{:S(2)}) collective-permute-start(bf16[512,256]{1,0:T(8,128)(2,1)S(1)} %pad_maximum_fusion.2), channel_id=1, source_target_pairs={{0,2},{1,3},{2,4},{3,5},{4,6},{5,7},{6,0},{7,1},{8,10},{9,11},{10,... | collective-permute-start | bytes 786440 | tf_op jit(solution)/shard_map/ppermute | solution.py:37
  13.8 14.8 %collective-permute-start.12 = (bf16[512,256]{1,0:T(8,128)(2,1)S(1)}, bf16[512,256]{1,0:T(8,128)(2,1)S(1)}, u32[]{:S(2)}, u32[]{:S(2)}) collective-permute-start(bf16[512,256]{1,0:T(8,128)(2,1)S(1)} %pad_maximum_fusion.2), channel_id=1, source_target_pairs={{0,4},{1,5},{2,6},{3,7},{4,0},{5,1},{6,2},{7,3},{8,12},{9,13},{10,... | collective-permute-start | bytes 786440 | tf_op jit(solution)/shard_map/ppermute | solution.py:37
  16.6 11.7 %collective-permute-start.11 = (bf16[512,256]{1,0:T(8,128)(2,1)S(1)}, bf16[512,256]{1,0:T(8,128)(2,1)S(1)}, u32[]{:S(2)}, u32[]{:S(2)}) collective-permute-start(bf16[512,256]{1,0:T(8,128)(2,1)S(1)} %pad_maximum_fusion.2), channel_id=1, source_target_pairs={{0,6},{1,7},{2,0},{3,1},{4,2},{5,3},{6,4},{7,5},{8,14},{9,15},{10,... | collective-permute-start | bytes 786440 | tf_op jit(solution)/shard_map/ppermute | solution.py:37
  28.7 35.9 %copy-start = (bf16[2048,256]{1,0:T(8,128)(2,1)}, bf16[2048,256]{1,0:T(8,128)(2,1)S(1)}, u32[]{:S(2)}) copy-start(bf16[2048,256]{1,0:T(8,128)(2,1)S(1)} %constant_dynamic-update-slice_fusion.2.kv_own) | copy-start | bytes 3145732
  28.7 35.9 %collective-permute-start.14 = (bf16[2048,256]{1,0:T(8,128)(2,1)S(1)}, bf16[2048,256]{1,0:T(8,128)(2,1)S(1)}, u32[]{:S(2)}, u32[]{:S(2)}) collective-permute-start(bf16[2048,256]{1,0:T(8,128)(2,1)S(1)} %constant_dynamic-update-slice_fusion.2.kv_own), channel_id=1, source_target_pairs={{0,8},{1,9},{2,10},{3,11},{4,12},{5,13},{6,14},{7,15},{8,0},{9,1},... | collective-permute-start | bytes 3145736 | tf_op jit(solution)/shard_map/ppermute | solution.py:37
  29.3 35.3 %collective-permute-start.3 = (bf16[256,1024]{1,0:T(8,128)(2,1)S(1)}, bf16[256,1024]{1,0:T(8,128)(2,1)S(1)}, u32[]{:S(2)}, u32[]{:S(2)}) collective-permute-start(bf16[256,1024]{1,0:T(8,128)(2,1)S(1)} %pad_maximum_fusion.pay0), channel_id=1, source_target_pairs={{0,64},{1,65},{2,66},{3,67},{4,68},{5,69},{6,70},{7,71},{8,72},{9,... | collective-permute-start | bytes 1572872 | tf_op jit(solution)/shard_map/ppermute | solution.py:37
  30.9 33.7 %collective-permute-start.2 = (bf16[256,1024]{1,0:T(8,128)(2,1)S(1)}, bf16[256,1024]{1,0:T(8,128)(2,1)S(1)}, u32[]{:S(2)}, u32[]{:S(2)}) collective-permute-start(bf16[256,1024]{1,0:T(8,128)(2,1)S(1)} %pad_maximum_fusion.pay0), channel_id=1, source_target_pairs={{0,1},{1,0},{2,3},{3,2},{4,5},{5,4},{6,7},{7,6},{8,9},{9,8},{10,11... | collective-permute-start | bytes 1572872 | tf_op jit(solution)/shard_map/ppermute | solution.py:37
  33.8 30.8 %collective-permute-start.1 = (bf16[256,1024]{1,0:T(8,128)(2,1)S(1)}, bf16[256,1024]{1,0:T(8,128)(2,1)S(1)}, u32[]{:S(2)}, u32[]{:S(2)}) collective-permute-start(bf16[256,1024]{1,0:T(8,128)(2,1)S(1)} %pad_maximum_fusion.pay0), channel_id=1, source_target_pairs={{0,65},{1,64},{2,67},{3,66},{4,69},{5,68},{6,71},{7,70},{8,73},{9,... | collective-permute-start | bytes 1572872 | tf_op jit(solution)/shard_map/ppermute | solution.py:37
  35.3 18.8 %collective-permute-start.7 = (f32[16,128]{1,0:T(8,128)S(1)}, f32[16,128]{1,0:T(8,128)S(1)}, u32[]{:S(2)}, u32[]{:S(2)}) collective-permute-start(f32[16,128]{1,0:T(8,128)S(1)} %pad_maximum_fusion.4.st0), channel_id=1, source_target_pairs={{0,64},{1,65},{2,66},{3,67},{4,68},{5,69},{6,70},{7,71},{8,72},{9,... | collective-permute-start | bytes 24584 | tf_op jit(solution)/shard_map/ppermute | solution.py:37
  54.2 5.7 %collective-permute-start.6 = (f32[16,128]{1,0:T(8,128)S(1)}, f32[16,128]{1,0:T(8,128)S(1)}, u32[]{:S(2)}, u32[]{:S(2)}) collective-permute-start(f32[16,128]{1,0:T(8,128)S(1)} %pad_maximum_fusion.4.st0), channel_id=1, source_target_pairs={{0,1},{1,0},{2,3},{3,2},{4,5},{5,4},{6,7},{7,6},{8,9},{9,8},{10,11... | collective-permute-start | bytes 24584 | tf_op jit(solution)/shard_map/ppermute | solution.py:37
  59.9 4.7 %collective-permute-start.5 = (f32[16,128]{1,0:T(8,128)S(1)}, f32[16,128]{1,0:T(8,128)S(1)}, u32[]{:S(2)}, u32[]{:S(2)}) collective-permute-start(f32[16,128]{1,0:T(8,128)S(1)} %pad_maximum_fusion.4.st0), channel_id=1, source_target_pairs={{0,65},{1,64},{2,67},{3,66},{4,69},{5,68},{6,71},{7,70},{8,73},{9,... | collective-permute-start | bytes 24584 | tf_op jit(solution)/shard_map/ppermute | solution.py:37
  64.6 1.0 copy-start.1
  102.5 19.2 %collective-permute-start.19 = (bf16[2048,256]{1,0:T(8,128)(2,1)S(1)}, bf16[2048,256]{1,0:T(8,128)(2,1)S(1)}, u32[]{:S(2)}, u32[]{:S(2)}) collective-permute-start(bf16[2048,256]{1,0:T(8,128)(2,1)S(1)} %get-tuple-element.14), channel_id=1, source_target_pairs={{0,8},{1,9},{2,10},{3,11},{4,12},{5,13},{6,14},{7,15},{8,0},{9,1},... | collective-permute-start | bytes 3145736 | tf_op jit(solution)/shard_map/ppermute | solution.py:37
  102.6 12.1 %collective-permute-start.15 = (bf16[256,512]{1,0:T(8,128)(2,1)S(1)}, bf16[256,512]{1,0:T(8,128)(2,1)S(1)}, u32[]{:S(2)}, u32[]{:S(2)}) collective-permute-start(bf16[256,512]{1,0:T(8,128)(2,1)S(1)} %get-tuple-element.10), channel_id=1, source_target_pairs={{0,64},{1,65},{2,66},{3,67},{4,68},{5,69},{6,70},{7,71},{8,72},{9,... | collective-permute-start | bytes 786440 | tf_op jit(solution)/shard_map/ppermute | solution.py:37
  102.7 18.8 %collective-permute-start.16 = (bf16[256,512]{1,0:T(8,128)(2,1)S(1)}, bf16[256,512]{1,0:T(8,128)(2,1)S(1)}, u32[]{:S(2)}, u32[]{:S(2)}) collective-permute-start(bf16[256,512]{1,0:T(8,128)(2,1)S(1)} %get-tuple-element.11), channel_id=1, source_target_pairs={{0,1},{1,0},{2,3},{3,2},{4,5},{5,4},{6,7},{7,6},{8,9},{9,8},{10,11... | collective-permute-start | bytes 786440 | tf_op jit(solution)/shard_map/ppermute | solution.py:37
  109.2 12.2 %collective-permute-start.17 = (bf16[256,512]{1,0:T(8,128)(2,1)S(1)}, bf16[256,512]{1,0:T(8,128)(2,1)S(1)}, u32[]{:S(2)}, u32[]{:S(2)}) collective-permute-start(bf16[256,512]{1,0:T(8,128)(2,1)S(1)} %get-tuple-element.12), channel_id=1, source_target_pairs={{0,65},{1,64},{2,67},{3,66},{4,69},{5,68},{6,71},{7,70},{8,73},{9,... | collective-permute-start | bytes 786440 | tf_op jit(solution)/shard_map/ppermute | solution.py:37
  121.6 9.1 %collective-permute-start.18 = (bf16[128,512]{1,0:T(8,128)(2,1)S(1)}, bf16[128,512]{1,0:T(8,128)(2,1)S(1)}, u32[]{:S(2)}, u32[]{:S(2)}) collective-permute-start(bf16[128,512]{1,0:T(8,128)(2,1)S(1)} %slice.87), channel_id=1, source_target_pairs={{0,8},{1,9},{2,10},{3,11},{4,12},{5,13},{6,14},{7,15},{8,0},{9,1},... | collective-permute-start | bytes 393224 | tf_op jit(solution)/shard_map/ppermute | solution.py:37
  122.1 14.1 %collective-permute-start.20 = (bf16[512,256]{1,0:T(8,128)(2,1)S(1)}, bf16[512,256]{1,0:T(8,128)(2,1)S(1)}, u32[]{:S(2)}, u32[]{:S(2)}) collective-permute-start(bf16[512,256]{1,0:T(8,128)(2,1)S(1)} %get-tuple-element.15), channel_id=1, source_target_pairs={{0,2},{1,3},{2,4},{3,5},{4,6},{5,7},{6,0},{7,1},{8,10},{9,11},{10,... | collective-permute-start | bytes 786440 | tf_op jit(solution)/shard_map/ppermute | solution.py:37
  122.2 19.0 %collective-permute-start.22 = (bf16[512,256]{1,0:T(8,128)(2,1)S(1)}, bf16[512,256]{1,0:T(8,128)(2,1)S(1)}, u32[]{:S(2)}, u32[]{:S(2)}) collective-permute-start(bf16[512,256]{1,0:T(8,128)(2,1)S(1)} %get-tuple-element.16), channel_id=1, source_target_pairs={{0,6},{1,7},{2,0},{3,1},{4,2},{5,3},{6,4},{7,5},{8,14},{9,15},{10,... | collective-permute-start | bytes 786440 | tf_op jit(solution)/shard_map/ppermute | solution.py:37
  129.3 13.7 %collective-permute-start.21 = (bf16[512,256]{1,0:T(8,128)(2,1)S(1)}, bf16[512,256]{1,0:T(8,128)(2,1)S(1)}, u32[]{:S(2)}, u32[]{:S(2)}) collective-permute-start(bf16[512,256]{1,0:T(8,128)(2,1)S(1)} %get-tuple-element.17), channel_id=1, source_target_pairs={{0,4},{1,5},{2,6},{3,7},{4,0},{5,1},{6,2},{7,3},{8,12},{9,13},{10,... | collective-permute-start | bytes 786440 | tf_op jit(solution)/shard_map/ppermute | solution.py:37
  143.2 5.5 %collective-permute-start.23 = (bf16[128,256]{1,0:T(8,128)(2,1)S(1)}, bf16[128,256]{1,0:T(8,128)(2,1)S(1)}, u32[]{:S(2)}, u32[]{:S(2)}) collective-permute-start(bf16[128,256]{1,0:T(8,128)(2,1)S(1)} %get-tuple-element.20), channel_id=1, source_target_pairs={{0,16},{1,17},{2,18},{3,19},{4,20},{5,21},{6,22},{7,23},{8,24},{9,... | collective-permute-start | bytes 196616 | tf_op jit(solution)/shard_map/ppermute | solution.py:37
  143.3 5.7 %collective-permute-start.25 = (bf16[128,256]{1,0:T(8,128)(2,1)S(1)}, bf16[128,256]{1,0:T(8,128)(2,1)S(1)}, u32[]{:S(2)}, u32[]{:S(2)}) collective-permute-start(bf16[128,256]{1,0:T(8,128)(2,1)S(1)} %get-tuple-element.21), channel_id=1, source_target_pairs={{0,48},{1,49},{2,50},{3,51},{4,52},{5,53},{6,54},{7,55},{8,56},{9,... | collective-permute-start | bytes 196616 | tf_op jit(solution)/shard_map/ppermute | solution.py:37
  146.5 5.8 %collective-permute-start.24 = (bf16[128,256]{1,0:T(8,128)(2,1)S(1)}, bf16[128,256]{1,0:T(8,128)(2,1)S(1)}, u32[]{:S(2)}, u32[]{:S(2)}) collective-permute-start(bf16[128,256]{1,0:T(8,128)(2,1)S(1)} %get-tuple-element.22), channel_id=1, source_target_pairs={{0,32},{1,33},{2,34},{3,35},{4,36},{5,37},{6,38},{7,39},{8,40},{9,... | collective-permute-start | bytes 196616 | tf_op jit(solution)/shard_map/ppermute | solution.py:37

commit v2 on v1

--- a/solution.py
+++ b/solution.py
@@ -14,6 +14,8 @@
 PAIR = 2
 HALF_HEADS = 4
 COLS = HALF_HEADS * BLOCK
+STAT_ROWS = 16
+PAY_ROWS = 2 * BLOCK + STAT_ROWS
 LOG2E = 1.4426950408889634
 AXES = ("outer", "inner")
 
@@ -47,11 +49,10 @@
 
 def attend_kernel(
     q_rank, k_rank, q_sorted, k_sorted,
-    pay0, pay1, pay2, pay3, st0, st1, st2, st3, kv_own, kv_sib,
-    dq0, dq1, dq2, dq3, dkv_own, dkv_sib,
+    pay0, pay1, pay2a, pay2b, pay3, kv_own, kv_sib,
+    dq_own, dq_sib, dkv_own, dkv_sib,
     ks, vs, kt, dk, dv, qs, gs, dq, lse_s, del_s, s_scr, p_scr, ti, tj,
 ):
-    pays, stats, dqs = (pay0, pay1, pay2, pay3), (st0, st1, st2, st3), (dq0, dq1, dq2, dq3)
     key_blocks, query_blocks = k_rank.shape[0], q_rank.shape[0]
     per_tile = KEY_TILE // BLOCK
     key_tiles, query_tiles = key_blocks // per_tile, query_blocks // PAIR
@@ -77,19 +78,24 @@
     lax.fori_loop(0, key_tiles, ready, 0)
 
     for s in range(query_blocks):
-        pay, stat, rows = pays[s // 4], stats[s // 4], (s % 4) * BLOCK
+        pay, own = ((pay0, pay1, pay2a, pay3)[s // 4], s % 4 // 2 * PAY_ROWS)
+        if s // 4 == 2:
+            pay, own = (pay2a, pay2b)[s % 4 // 2], 0
+        rows = own + s % 2 * BLOCK
         rank = q_rank[s]
         dst = pl.multiple_of(rank * COLS, COLS)
         for h in range(HALF_HEADS):
             qs[pl.ds(dst + h * BLOCK, BLOCK), :] = pay[rows:rows + BLOCK, h * WIDTH:(h + 1) * WIDTH]
             gs[pl.ds(dst + h * BLOCK, BLOCK), :] = pay[
                 rows:rows + BLOCK, (HALF_HEADS + h) * WIDTH:(HALF_HEADS + h + 1) * WIDTH]
-        top, lanes = (s % 4) // 2 * 8, slice((s % 2) * BLOCK, (s % 2 + 1) * BLOCK)
+        stat = sum(
+            pay[own + PAY_ROWS - STAT_ROWS:own + PAY_ROWS, n * WIDTH:(n + 1) * WIDTH].astype(jnp.float32)
+            for n in range(3))
+        lanes = slice(s % 2 * BLOCK, (s % 2 + 1) * BLOCK)
         lse_s[pl.ds(rank, 1), :] = jnp.concatenate(
-            [stat[top + h:top + h + 1, lanes] for h in range(HALF_HEADS)], axis=1) * LOG2E
+            [stat[h:h + 1, lanes] for h in range(HALF_HEADS)], axis=1) * LOG2E
         del_s[pl.ds(rank, 1), :] = jnp.concatenate(
-            [stat[top + HALF_HEADS + h:top + HALF_HEADS + h + 1, lanes] for h in range(HALF_HEADS)],
-            axis=1)
+            [stat[HALF_HEADS + h:HALF_HEADS + h + 1, lanes] for h in range(HALF_HEADS)], axis=1)
 
     def listing(i, carry):
         n, total = carry
@@ -157,9 +163,10 @@
     lax.fori_loop(0, query_tiles, turn, 0)
     for s in range(query_blocks):
         src = pl.multiple_of(q_rank[s] * COLS, COLS)
-        rows = (s % 4) * BLOCK
+        out = (dq_own, dq_sib)[s % 4 // 2]
+        rows = s // 4 * 2 * BLOCK + s % 2 * BLOCK
         for h in range(HALF_HEADS):
-            dqs[s // 4][rows:rows + BLOCK, h * WIDTH:(h + 1) * WIDTH] = qs[
+            out[rows:rows + BLOCK, h * WIDTH:(h + 1) * WIDTH] = qs[
                 pl.ds(src + h * BLOCK, BLOCK), :]
     for half, out in enumerate((dkv_own, dkv_sib)):
         def give(r, _, out=out, half=half):
@@ -172,7 +179,7 @@
         lax.fori_loop(0, half_keys, give, 0, unroll=4)
 
 
-def attend(q_rank, k_rank, q_sorted, k_sorted, pays, stats, kv_own, kv_sib):
+def attend(q_rank, k_rank, q_sorted, k_sorted, pays, kv_own, kv_sib):
     key_blocks, query_blocks = k_rank.shape[0], q_rank.shape[0]
     keys = key_blocks * BLOCK
     key_tiles, query_tiles = keys // KEY_TILE, query_blocks // PAIR
@@ -182,9 +189,9 @@
     listed = query_tiles * key_tiles + 2
     return pl.pallas_call(
         attend_kernel,
-        in_specs=[smem] * 4 + [vmem] * 10,
-        out_specs=[vmem] * 6,
-        out_shape=[jax.ShapeDtypeStruct((4 * BLOCK, HALF_HEADS * WIDTH), bf16)] * 4
+        in_specs=[smem] * 4 + [vmem] * 7,
+        out_specs=[vmem] * 4,
+        out_shape=[jax.ShapeDtypeStruct((8 * BLOCK, HALF_HEADS * WIDTH), bf16)] * 2
         + [jax.ShapeDtypeStruct((keys // 2, 2 * WIDTH), bf16)] * 2,
         scratch_shapes=[
             pltpu.VMEM((keys, WIDTH), bf16),
@@ -203,7 +210,7 @@
             pltpu.SMEM((listed,), jnp.int32),
         ],
         compiler_params=pltpu.CompilerParams(vmem_limit_bytes=48 * 1024 * 1024),
-    )(q_rank, k_rank, q_sorted, k_sorted, *pays, *stats, kv_own, kv_sib)
+    )(q_rank, k_rank, q_sorted, k_sorted, *pays, kv_own, kv_sib)
 
 
 def ranked(block_order, blocks):
@@ -218,6 +225,13 @@
     return functools.reduce(lambda a, b: a + b, [p.astype(jnp.float32) for p in parts])
 
 
+def thirds(array):
+    high = lax.reduce_precision(array, 8, 7)
+    middle = lax.reduce_precision(array - high, 8, 7)
+    low = lax.reduce_precision(array - high - middle, 8, 7)
+    return jnp.concatenate([high, middle, low], axis=1).astype(jnp.bfloat16)
+
+
 def body(query_rows, key_rows, value_rows, saved_output, output_grad, logsumexp, block_order):
     rows = query_rows.shape[0]
     half = HALF_HEADS * WIDTH
@@ -230,24 +244,29 @@
     def other(array):
         return jnp.where(first, array[:, half:], array[:, :half])
 
-    kv = jnp.concatenate([key_rows, value_rows], axis=1)
-    kv_line = jnp.concatenate([kv] + [shift(kv, dz=-d) for d in (1, 2, 3)], axis=0)
-    sib = shift(jnp.concatenate([other(query_rows), other(output_grad)], axis=1), dcore=1)
-    pay = jnp.concatenate(
-        [jnp.concatenate([mine(query_rows), mine(output_grad)], axis=1), sib], axis=0)
-    pays = [pay] + [shift(pay, dy=-d) for d in (1, 2, 3)]
-    kv_own = jnp.concatenate([kv_line] + [shift(kv_line, dx=-d) for d in (1, 2, 3)], axis=0)
-    kv_sib = shift(kv_own, dcore=1)
-
     heads = (rows, 2 * HALF_HEADS, WIDTH)
     delta = jnp.sum(
         output_grad.reshape(heads).astype(jnp.float32)
         * saved_output.reshape(heads).astype(jnp.float32), axis=2).T
-    low = jnp.concatenate([logsumexp[:HALF_HEADS], delta[:HALF_HEADS]], axis=0)
-    high = jnp.concatenate([logsumexp[HALF_HEADS:], delta[HALF_HEADS:]], axis=0)
-    stat = jnp.concatenate(
-        [jnp.where(first, low, high), shift(jnp.where(first, high, low), dcore=1)], axis=0)
-    stats = [stat] + [shift(stat, dy=-d) for d in (1, 2, 3)]
+    low = thirds(jnp.concatenate([logsumexp[:HALF_HEADS], delta[:HALF_HEADS]], axis=0))
+    high = thirds(jnp.concatenate([logsumexp[HALF_HEADS:], delta[HALF_HEADS:]], axis=0))
+
+    def packed(side, stat):
+        stat = jnp.pad(stat, ((0, STAT_ROWS - stat.shape[0]), (0, 2 * half - stat.shape[1])))
+        return jnp.concatenate(
+            [jnp.concatenate([side(query_rows), side(output_grad)], axis=1), stat], axis=0)
+
+    kv = jnp.concatenate([key_rows, value_rows], axis=1)
+    sib = shift(packed(other, jnp.where(first, high, low)), dcore=1)
+    pay = jnp.concatenate([packed(mine, jnp.where(first, low, high)), sib], axis=0)
+    after, before = shift(pay, dy=-1), shift(pay, dy=1)
+    kv_line = jnp.concatenate([kv] + [shift(kv, dz=-d) for d in (1, 2, 3)], axis=0)
+    lines = [kv_line] + [shift(kv_line, dx=-d) for d in (1, 2, 3)]
+    after, before, *lines = lax.optimization_barrier((after, before, *lines))
+    kv_own = jnp.concatenate(lines, axis=0)
+    kv_sib = shift(kv_own, dcore=1)
+    across = shift(after[:PAY_ROWS], dy=-1), shift(before[PAY_ROWS:], dy=1)
+    pays = [pay, after, *across, before]
 
     four = jnp.arange(4, dtype=jnp.int32)
     two = jnp.arange(2, dtype=jnp.int32)
@@ -257,19 +276,20 @@
     k_rank, k_sorted = ranked(
         block_order, 2 * linear((x + dx) % 4, y, (z + dz) % 4, (core + cs) % 2) + b)
 
-    *dqs, dkv_own, dkv_sib = attend(
-        q_rank, k_rank, q_sorted, k_sorted, pays, stats, kv_own, kv_sib)
+    dq_own, dq_sib, dkv_own, dkv_sib = attend(
+        q_rank, k_rank, q_sorted, k_sorted, pays, kv_own, kv_sib)
 
     dkv = total_of([dkv_own, shift(dkv_sib, dcore=1)]).astype(jnp.bfloat16)
-    dq = total_of([dqs[0]] + [shift(dqs[d], dy=d) for d in (1, 2, 3)]).astype(jnp.bfloat16)
+    dq_far = shift(dq_sib, dcore=1)
+    dq = jnp.concatenate(
+        [jnp.where(first, dq_own, dq_far), jnp.where(first, dq_far, dq_own)], axis=1)
     quarter = dkv.shape[0] // 4
     parts = [dkv[d * quarter:(d + 1) * quarter] for d in range(4)]
     line = total_of([parts[0]] + [shift(parts[d], dx=d) for d in (1, 2, 3)]).astype(jnp.bfloat16)
     parts = [line[d * rows:(d + 1) * rows] for d in range(4)]
     done = total_of([parts[0]] + [shift(parts[d], dz=d) for d in (1, 2, 3)])
-    near, far = dq[:rows], shift(dq[rows:], dcore=1)
-    query_grad = jnp.concatenate(
-        [jnp.where(first, near, far), jnp.where(first, far, near)], axis=1)
+    parts = [dq[d * rows:(d + 1) * rows] for d in range(4)]
+    query_grad = total_of([parts[0]] + [shift(parts[d], dy=d) for d in (1, 2, 3)]).astype(jnp.bfloat16)
     return (
         query_grad,
         done[:, :WIDTH].astype(jnp.bfloat16),

time: 153 us -> 113 us (0.74)
  waiting for transfers between devices: 59.1 us -> 26.7 us
  starting transfers between devices: 47.4 us -> 40.6 us
  Pallas kernels: 36.9 us -> 35.3 us
    ppermute x26 -> x23, waiting for transfers between devices: 59.1 us -> 26.7 us  [shift(): return lax.ppermute(block, AXES, route)]
    ppermute x26 -> x23, starting transfers between devices: 47.4 us -> 40.6 us  [shift(): return lax.ppermute(block, AXES, route)]
    pallas_call x1, Pallas kernels: 36.9 us -> 35.3 us  [attend(): pl.pallas_call(attend_kernel, in_specs=[smem] * 4 + [vmem] * 7, out_specs...]
  transfers between devices with their start and end apart: 26 -> 23, of which waited for: 13 -> 8; matrix products, arithmetic and copies ran while one was open for 3% -> 3% of each run, Pallas kernels for 0% -> 0%
where the time goes in v2:
time: 113 us; the launch traced here: 112 us
  starting transfers between devices  40.6 us (36%)
  Pallas kernels  35.3 us (31%)
  waiting for transfers between devices  26.7 us (24%)
  local copies, waits for them, and re-layouts  4.08 us (4%)
  other arithmetic  3.96 us (4%)
    ppermute x23, starting transfers between devices, shift(): return lax.ppermute(block, AXES, route)  40.6 us
    pallas_call x1, Pallas kernels, attend(): pl.pallas_call(attend_kernel, in_specs=[smem] * 4 + [vmem] * 7, out_specs...  35.3 us
    ppermute x23, waiting for transfers between devices, shift(): return lax.ppermute(block, AXES, route)  26.7 us
  transfers between devices with their start and end apart: 23, of which 8 were waited for; matrix products, arithmetic and copies ran while one was open for 3% of the time, Pallas kernels for 0%

profile of v2, /device:TPU:0, one launch (start us, length us, event | category | flops | bytes accessed | tf_op | source)
XLA Modules:
  0.0 111.7 jit_solution(17103065427624873303)
XLA Ops:
  0.7 0.8 fusion.30
  1.4 1.1 multiply_bitcast_fusion
  3.0 0.5 copy-done.2
  3.8 2.1 %collective-permute-start.5 = (bf16[128,256]{1,0:T(8,128)(2,1)S(1)}, bf16[128,256]{1,0:T(8,128)(2,1)S(1)}, u32[]{:S(2)}, u32[]{:S(2)}) collective-permute-start(bf16[128,256]{1,0:T(8,128)(2,1)S(1)} %constant_dynamic-update-slice_fusion), channel_id=1, source_target_pairs={{0,16},{1,17},{2,18},{3,19},{4,20},{5,21},{6,22},{7,23},{8,24},{9,... | collective-permute-start | bytes 196616 | tf_op jit(solution)/shard_map/ppermute | solution.py:39
  5.9 3.6 %collective-permute-start.4 = (bf16[128,256]{1,0:T(8,128)(2,1)S(1)}, bf16[128,256]{1,0:T(8,128)(2,1)S(1)}, u32[]{:S(2)}, u32[]{:S(2)}) collective-permute-start(bf16[128,256]{1,0:T(8,128)(2,1)S(1)} %constant_dynamic-update-slice_fusion), channel_id=1, source_target_pairs={{0,32},{1,33},{2,34},{3,35},{4,36},{5,37},{6,38},{7,39},{8,40},{9,... | collective-permute-start | bytes 196616 | tf_op jit(solution)/shard_map/ppermute | solution.py:39
  9.5 1.0 collective-permute-start.3
  10.5 1.6 %collective-permute-start.2 = (bf16[288,1024]{1,0:T(8,128)(2,1)S(1)}, bf16[288,1024]{1,0:T(8,128)(2,1)S(1)}, u32[]{:S(2)}, u32[]{:S(2)}) collective-permute-start(bf16[288,1024]{1,0:T(8,128)(2,1)S(1)} %fusion.3.pay0), channel_id=1, source_target_pairs={{0,64},{1,65},{2,66},{3,67},{4,68},{5,69},{6,70},{7,71},{8,72},{9,... | collective-permute-start | bytes 1769480 | tf_op jit(solution)/shard_map/ppermute | solution.py:39
  12.2 1.7 %collective-permute-start.1 = (bf16[288,1024]{1,0:T(8,128)(2,1)S(1)}, bf16[288,1024]{1,0:T(8,128)(2,1)S(1)}, u32[]{:S(2)}, u32[]{:S(2)}) collective-permute-start(bf16[288,1024]{1,0:T(8,128)(2,1)S(1)} %fusion.3.pay0), channel_id=1, source_target_pairs={{0,65},{1,64},{2,67},{3,66},{4,69},{5,68},{6,71},{7,70},{8,73},{9,... | collective-permute-start | bytes 1769480 | tf_op jit(solution)/shard_map/ppermute | solution.py:39
  13.9 1.6 %collective-permute-start.8 = (bf16[512,256]{1,0:T(8,128)(2,1)S(1)}, bf16[512,256]{1,0:T(8,128)(2,1)S(1)}, u32[]{:S(2)}, u32[]{:S(2)}) collective-permute-start(bf16[512,256]{1,0:T(8,128)(2,1)S(1)} %pad_maximum_fusion.1), channel_id=1, source_target_pairs={{0,2},{1,3},{2,4},{3,5},{4,6},{5,7},{6,0},{7,1},{8,10},{9,11},{10,... | collective-permute-start | bytes 786440 | tf_op jit(solution)/shard_map/ppermute | solution.py:39
  15.5 2.7 %collective-permute-start.7 = (bf16[512,256]{1,0:T(8,128)(2,1)S(1)}, bf16[512,256]{1,0:T(8,128)(2,1)S(1)}, u32[]{:S(2)}, u32[]{:S(2)}) collective-permute-start(bf16[512,256]{1,0:T(8,128)(2,1)S(1)} %pad_maximum_fusion.1), channel_id=1, source_target_pairs={{0,4},{1,5},{2,6},{3,7},{4,0},{5,1},{6,2},{7,3},{8,12},{9,13},{10,... | collective-permute-start | bytes 786440 | tf_op jit(solution)/shard_map/ppermute | solution.py:39
  18.2 1.4 %collective-permute-start.6 = (bf16[512,256]{1,0:T(8,128)(2,1)S(1)}, bf16[512,256]{1,0:T(8,128)(2,1)S(1)}, u32[]{:S(2)}, u32[]{:S(2)}) collective-permute-start(bf16[512,256]{1,0:T(8,128)(2,1)S(1)} %pad_maximum_fusion.1), channel_id=1, source_target_pairs={{0,6},{1,7},{2,0},{3,1},{4,2},{5,3},{6,4},{7,5},{8,14},{9,15},{10,... | collective-permute-start | bytes 786440 | tf_op jit(solution)/shard_map/ppermute | solution.py:39
  20.4 3.0 %collective-permute-done.8 = bf16[512,256]{1,0:T(8,128)(2,1)S(1)} collective-permute-done((bf16[512,256]{1,0:T(8,128)(2,1)S(1)}, bf16[512,256]{1,0:T(8,128)(2,1)S(1)}, u32[]{:S(2)}, u32[]{:S(2)}) %collective-permute-start.8) | collective-permute-done | bytes 262176 | tf_op jit(solution)/shard_map/ppermute | solution.py:39
  23.5 5.8 %collective-permute-done.7 = bf16[512,256]{1,0:T(8,128)(2,1)S(1)} collective-permute-done((bf16[512,256]{1,0:T(8,128)(2,1)S(1)}, bf16[512,256]{1,0:T(8,128)(2,1)S(1)}, u32[]{:S(2)}, u32[]{:S(2)}) %collective-permute-start.7) | collective-permute-done | bytes 262176 | tf_op jit(solution)/shard_map/ppermute | solution.py:39
  30.1 1.6 %collective-permute-start.10 = (bf16[144,1024]{1,0:T(8,128)(2,1)S(1)}, bf16[144,1024]{1,0:T(8,128)(2,1)S(1)}, u32[]{:S(2)}, u32[]{:S(2)}) collective-permute-start(bf16[144,1024]{1,0:T(8,128)(2,1)S(1)} %slice.87), channel_id=1, source_target_pairs={{0,64},{1,65},{2,66},{3,67},{4,68},{5,69},{6,70},{7,71},{8,72},{9,... | collective-permute-start | bytes 884744 | tf_op jit(solution)/shard_map/ppermute | solution.py:39
  31.7 1.7 %collective-permute-start.9 = (bf16[144,1024]{1,0:T(8,128)(2,1)S(1)}, bf16[144,1024]{1,0:T(8,128)(2,1)S(1)}, u32[]{:S(2)}, u32[]{:S(2)}) collective-permute-start(bf16[144,1024]{1,0:T(8,128)(2,1)S(1)} %slice.86), channel_id=1, source_target_pairs={{0,65},{1,64},{2,67},{3,66},{4,69},{5,68},{6,71},{7,70},{8,73},{9,... | collective-permute-start | bytes 884744 | tf_op jit(solution)/shard_map/ppermute | solution.py:39
  33.9 7.0 %collective-permute-done.10.pay2b = bf16[144,1024]{1,0:T(8,128)(2,1)S(1)} collective-permute-done((bf16[144,1024]{1,0:T(8,128)(2,1)S(1)}, bf16[144,1024]{1,0:T(8,128)(2,1)S(1)}, u32[]{:S(2)}, u32[]{:S(2)}) %collective-permute-start.10) | collective-permute-done | bytes 294944 | tf_op jit(solution)/shard_map/ppermute | solution.py:39
  40.8 1.0 copy-done.1
  41.8 35.3 %shard_map.94 = (bf16[512,512]{1,0:T(8,128)(2,1)S(1)}, bf16[512,512]{1,0:T(8,128)(2,1)S(1)}, bf16[2048,256]{1,0:T(8,128)(2,1)S(1)}, bf16[2048,256]{1,0:T(8,128)(2,1)S(1)}) custom-call(s32[16]{0:T(128)S(1)} %convert_reduce_fusion.1.q_rank, s32[64]{0:T(128)S(1)} %convert_reduce_fusion.k_rank, s32[16]{0:T(128)S(1)} %select_reduce_fusion.3.q_sorted, ...), custom_call_target="tpu_custom_call" | custom-call | tf_op jit(solution)/shard_map/pallas_call | solution.py:190
  77.2 0.5 collective-permute-start.12
  77.7 2.1 %collective-permute-done.16 = bf16[2048,256]{1,0:T(8,128)(2,1)S(1)} collective-permute-done((bf16[2048,256]{1,0:T(8,128)(2,1)S(1)}, bf16[2048,256]{1,0:T(8,128)(2,1)S(1)}, u32[]{:S(2)}, u32[]{:S(2)}) %collective-permute-start.16) | collective-permute-done | bytes 1048608 | tf_op jit(solution)/shard_map/ppermute | solution.py:39
  80.2 4.7 %collective-permute-start.17 = (bf16[512,256]{1,0:T(8,128)(2,1)S(1)}, bf16[512,256]{1,0:T(8,128)(2,1)S(1)}, u32[]{:S(2)}, u32[]{:S(2)}) collective-permute-start(bf16[512,256]{1,0:T(8,128)(2,1)S(1)} %get-tuple-element.23), channel_id=1, source_target_pairs={{0,2},{1,3},{2,4},{3,5},{4,6},{5,7},{6,0},{7,1},{8,10},{9,11},{10,... | collective-permute-start | bytes 786440 | tf_op jit(solution)/shard_map/ppermute | solution.py:39
  84.9 2.6 %collective-permute-start.19 = (bf16[512,256]{1,0:T(8,128)(2,1)S(1)}, bf16[512,256]{1,0:T(8,128)(2,1)S(1)}, u32[]{:S(2)}, u32[]{:S(2)}) collective-permute-start(bf16[512,256]{1,0:T(8,128)(2,1)S(1)} %get-tuple-element.24), channel_id=1, source_target_pairs={{0,6},{1,7},{2,0},{3,1},{4,2},{5,3},{6,4},{7,5},{8,14},{9,15},{10,... | collective-permute-start | bytes 786440 | tf_op jit(solution)/shard_map/ppermute | solution.py:39
  87.5 1.4 %collective-permute-start.18 = (bf16[512,256]{1,0:T(8,128)(2,1)S(1)}, bf16[512,256]{1,0:T(8,128)(2,1)S(1)}, u32[]{:S(2)}, u32[]{:S(2)}) collective-permute-start(bf16[512,256]{1,0:T(8,128)(2,1)S(1)} %get-tuple-element.25), channel_id=1, source_target_pairs={{0,4},{1,5},{2,6},{3,7},{4,0},{5,1},{6,2},{7,3},{8,12},{9,13},{10,... | collective-permute-start | bytes 786440 | tf_op jit(solution)/shard_map/ppermute | solution.py:39
  89.1 4.5 %collective-permute-start.15 = (bf16[128,1024]{1,0:T(8,128)(2,1)S(1)}, bf16[128,1024]{1,0:T(8,128)(2,1)S(1)}, u32[]{:S(2)}, u32[]{:S(2)}) collective-permute-start(bf16[128,1024]{1,0:T(8,128)(2,1)S(1)} %get-tuple-element.27), channel_id=1, source_target_pairs={{0,65},{1,64},{2,67},{3,66},{4,69},{5,68},{6,71},{7,70},{8,73},{9,... | collective-permute-start | bytes 786440 | tf_op jit(solution)/shard_map/ppermute | solution.py:39
  94.0 1.3 %collective-permute-start.14 = (bf16[128,1024]{1,0:T(8,128)(2,1)S(1)}, bf16[128,1024]{1,0:T(8,128)(2,1)S(1)}, u32[]{:S(2)}, u32[]{:S(2)}) collective-permute-start(bf16[128,1024]{1,0:T(8,128)(2,1)S(1)} %get-tuple-element.28), channel_id=1, source_target_pairs={{0,1},{1,0},{2,3},{3,2},{4,5},{5,4},{6,7},{7,6},{8,9},{9,8},{10,11... | collective-permute-start | bytes 786440 | tf_op jit(solution)/shard_map/ppermute | solution.py:39
  95.2 3.7 %collective-permute-done.19 = bf16[512,256]{1,0:T(8,128)(2,1)S(1)} collective-permute-done((bf16[512,256]{1,0:T(8,128)(2,1)S(1)}, bf16[512,256]{1,0:T(8,128)(2,1)S(1)}, u32[]{:S(2)}, u32[]{:S(2)}) %collective-permute-start.19) | collective-permute-done | bytes 262176 | tf_op jit(solution)/shard_map/ppermute | solution.py:39
  99.0 1.8 %collective-permute-done.18 = bf16[512,256]{1,0:T(8,128)(2,1)S(1)} collective-permute-done((bf16[512,256]{1,0:T(8,128)(2,1)S(1)}, bf16[512,256]{1,0:T(8,128)(2,1)S(1)}, u32[]{:S(2)}, u32[]{:S(2)}) %collective-permute-start.18) | collective-permute-done | bytes 262176 | tf_op jit(solution)/shard_map/ppermute | solution.py:39
  101.3 4.0 %collective-permute-start.22 = (bf16[128,256]{1,0:T(8,128)(2,1)S(1)}, bf16[128,256]{1,0:T(8,128)(2,1)S(1)}, u32[]{:S(2)}, u32[]{:S(2)}) collective-permute-start(bf16[128,256]{1,0:T(8,128)(2,1)S(1)} %get-tuple-element.32), channel_id=1, source_target_pairs={{0,48},{1,49},{2,50},{3,51},{4,52},{5,53},{6,54},{7,55},{8,56},{9,... | collective-permute-start | bytes 196616 | tf_op jit(solution)/shard_map/ppermute | solution.py:39
  105.2 2.1 %collective-permute-start.21 = (bf16[128,256]{1,0:T(8,128)(2,1)S(1)}, bf16[128,256]{1,0:T(8,128)(2,1)S(1)}, u32[]{:S(2)}, u32[]{:S(2)}) collective-permute-start(bf16[128,256]{1,0:T(8,128)(2,1)S(1)} %get-tuple-element.33), channel_id=1, source_target_pairs={{0,32},{1,33},{2,34},{3,35},{4,36},{5,37},{6,38},{7,39},{8,40},{9,... | collective-permute-start | bytes 196616 | tf_op jit(solution)/shard_map/ppermute | solution.py:39
  107.4 0.9 add_convert_fusion.2
  108.3 2.8 %collective-permute-done.21 = bf16[128,256]{1,0:T(8,128)(2,1)S(1)} collective-permute-done((bf16[128,256]{1,0:T(8,128)(2,1)S(1)}, bf16[128,256]{1,0:T(8,128)(2,1)S(1)}, u32[]{:S(2)}, u32[]{:S(2)}) %collective-permute-start.21) | collective-permute-done | bytes 65568 | tf_op jit(solution)/shard_map/ppermute | solution.py:39
  111.1 0.6 fusion.29
  (80 shorter events, 4.3 us)
Async XLA Ops:
  2.5 1.0 copy-start.2
  2.5 1.0 copy-start.3
  2.7 1.1 copy-start.4
  2.9 0.9 copy-start.5
  3.7 6.8 %collective-permute-start = (bf16[144,1024]{1,0:T(8,128)(2,1)S(1)}, bf16[144,1024]{1,0:T(8,128)(2,1)S(1)}, u32[]{:S(2)}, u32[]{:S(2)}) collective-permute-start(bf16[144,1024]{1,0:T(8,128)(2,1)S(1)} %fusion.5), channel_id=1, source_target_pairs={{0,8},{1,9},{2,10},{3,11},{4,12},{5,13},{6,14},{7,15},{8,0},{9,1},... | collective-permute-start | bytes 884744 | tf_op jit(solution)/shard_map/ppermute | solution.py:39
  3.8 10.0 %collective-permute-start.5 = (bf16[128,256]{1,0:T(8,128)(2,1)S(1)}, bf16[128,256]{1,0:T(8,128)(2,1)S(1)}, u32[]{:S(2)}, u32[]{:S(2)}) collective-permute-start(bf16[128,256]{1,0:T(8,128)(2,1)S(1)} %constant_dynamic-update-slice_fusion), channel_id=1, source_target_pairs={{0,16},{1,17},{2,18},{3,19},{4,20},{5,21},{6,22},{7,23},{8,24},{9,... | collective-permute-start | bytes 196616 | tf_op jit(solution)/shard_map/ppermute | solution.py:39
  5.9 8.0 %collective-permute-start.4 = (bf16[128,256]{1,0:T(8,128)(2,1)S(1)}, bf16[128,256]{1,0:T(8,128)(2,1)S(1)}, u32[]{:S(2)}, u32[]{:S(2)}) collective-permute-start(bf16[128,256]{1,0:T(8,128)(2,1)S(1)} %constant_dynamic-update-slice_fusion), channel_id=1, source_target_pairs={{0,32},{1,33},{2,34},{3,35},{4,36},{5,37},{6,38},{7,39},{8,40},{9,... | collective-permute-start | bytes 196616 | tf_op jit(solution)/shard_map/ppermute | solution.py:39
  9.5 4.4 %collective-permute-start.3 = (bf16[128,256]{1,0:T(8,128)(2,1)S(1)}, bf16[128,256]{1,0:T(8,128)(2,1)S(1)}, u32[]{:S(2)}, u32[]{:S(2)}) collective-permute-start(bf16[128,256]{1,0:T(8,128)(2,1)S(1)} %constant_dynamic-update-slice_fusion), channel_id=1, source_target_pairs={{0,48},{1,49},{2,50},{3,51},{4,52},{5,53},{6,54},{7,55},{8,56},{9,... | collective-permute-start | bytes 196616 | tf_op jit(solution)/shard_map/ppermute | solution.py:39
  10.5 18.7 %collective-permute-start.2 = (bf16[288,1024]{1,0:T(8,128)(2,1)S(1)}, bf16[288,1024]{1,0:T(8,128)(2,1)S(1)}, u32[]{:S(2)}, u32[]{:S(2)}) collective-permute-start(bf16[288,1024]{1,0:T(8,128)(2,1)S(1)} %fusion.3.pay0), channel_id=1, source_target_pairs={{0,64},{1,65},{2,66},{3,67},{4,68},{5,69},{6,70},{7,71},{8,72},{9,... | collective-permute-start | bytes 1769480 | tf_op jit(solution)/shard_map/ppermute | solution.py:39
  12.2 17.1 %collective-permute-start.1 = (bf16[288,1024]{1,0:T(8,128)(2,1)S(1)}, bf16[288,1024]{1,0:T(8,128)(2,1)S(1)}, u32[]{:S(2)}, u32[]{:S(2)}) collective-permute-start(bf16[288,1024]{1,0:T(8,128)(2,1)S(1)} %fusion.3.pay0), channel_id=1, source_target_pairs={{0,65},{1,64},{2,67},{3,66},{4,69},{5,68},{6,71},{7,70},{8,73},{9,... | collective-permute-start | bytes 1769480 | tf_op jit(solution)/shard_map/ppermute | solution.py:39
  13.9 9.5 %collective-permute-start.8 = (bf16[512,256]{1,0:T(8,128)(2,1)S(1)}, bf16[512,256]{1,0:T(8,128)(2,1)S(1)}, u32[]{:S(2)}, u32[]{:S(2)}) collective-permute-start(bf16[512,256]{1,0:T(8,128)(2,1)S(1)} %pad_maximum_fusion.1), channel_id=1, source_target_pairs={{0,2},{1,3},{2,4},{3,5},{4,6},{5,7},{6,0},{7,1},{8,10},{9,11},{10,... | collective-permute-start | bytes 786440 | tf_op jit(solution)/shard_map/ppermute | solution.py:39
  15.5 13.8 %collective-permute-start.7 = (bf16[512,256]{1,0:T(8,128)(2,1)S(1)}, bf16[512,256]{1,0:T(8,128)(2,1)S(1)}, u32[]{:S(2)}, u32[]{:S(2)}) collective-permute-start(bf16[512,256]{1,0:T(8,128)(2,1)S(1)} %pad_maximum_fusion.1), channel_id=1, source_target_pairs={{0,4},{1,5},{2,6},{3,7},{4,0},{5,1},{6,2},{7,3},{8,12},{9,13},{10,... | collective-permute-start | bytes 786440 | tf_op jit(solution)/shard_map/ppermute | solution.py:39
  18.2 11.0 %collective-permute-start.6 = (bf16[512,256]{1,0:T(8,128)(2,1)S(1)}, bf16[512,256]{1,0:T(8,128)(2,1)S(1)}, u32[]{:S(2)}, u32[]{:S(2)}) collective-permute-start(bf16[512,256]{1,0:T(8,128)(2,1)S(1)} %pad_maximum_fusion.1), channel_id=1, source_target_pairs={{0,6},{1,7},{2,0},{3,1},{4,2},{5,3},{6,4},{7,5},{8,14},{9,15},{10,... | collective-permute-start | bytes 786440 | tf_op jit(solution)/shard_map/ppermute | solution.py:39
  20.4 9.1 %copy-start.6 = (s32[256]{0:T(256)S(1)}, s32[256]{0:T(256)}, u32[]{:S(2)}) copy-start(s32[256]{0:T(256)} %param.13) | copy-start | bytes 3076
  29.4 11.5 %copy-start = (bf16[2048,256]{1,0:T(8,128)(2,1)}, bf16[2048,256]{1,0:T(8,128)(2,1)S(1)}, u32[]{:S(2)}) copy-start(bf16[2048,256]{1,0:T(8,128)(2,1)S(1)} %constant_dynamic-update-slice_fusion.2.kv_own) | copy-start | bytes 3145732
  29.4 11.5 %collective-permute-start.11 = (bf16[2048,256]{1,0:T(8,128)(2,1)S(1)}, bf16[2048,256]{1,0:T(8,128)(2,1)S(1)}, u32[]{:S(2)}, u32[]{:S(2)}) collective-permute-start(bf16[2048,256]{1,0:T(8,128)(2,1)S(1)} %constant_dynamic-update-slice_fusion.2.kv_own), channel_id=1, source_target_pairs={{0,8},{1,9},{2,10},{3,11},{4,12},{5,13},{6,14},{7,15},{8,0},{9,1},... | collective-permute-start | bytes 3145736 | tf_op jit(solution)/shard_map/ppermute | solution.py:39
  30.1 10.7 %collective-permute-start.10 = (bf16[144,1024]{1,0:T(8,128)(2,1)S(1)}, bf16[144,1024]{1,0:T(8,128)(2,1)S(1)}, u32[]{:S(2)}, u32[]{:S(2)}) collective-permute-start(bf16[144,1024]{1,0:T(8,128)(2,1)S(1)} %slice.87), channel_id=1, source_target_pairs={{0,64},{1,65},{2,66},{3,67},{4,68},{5,69},{6,70},{7,71},{8,72},{9,... | collective-permute-start | bytes 884744 | tf_op jit(solution)/shard_map/ppermute | solution.py:39
  31.7 9.1 %collective-permute-start.9 = (bf16[144,1024]{1,0:T(8,128)(2,1)S(1)}, bf16[144,1024]{1,0:T(8,128)(2,1)S(1)}, u32[]{:S(2)}, u32[]{:S(2)}) collective-permute-start(bf16[144,1024]{1,0:T(8,128)(2,1)S(1)} %slice.86), channel_id=1, source_target_pairs={{0,65},{1,64},{2,67},{3,66},{4,69},{5,68},{6,71},{7,70},{8,73},{9,... | collective-permute-start | bytes 884744 | tf_op jit(solution)/shard_map/ppermute | solution.py:39
  40.8 1.0 copy-start.1
  77.1 2.7 %collective-permute-start.16 = (bf16[2048,256]{1,0:T(8,128)(2,1)S(1)}, bf16[2048,256]{1,0:T(8,128)(2,1)S(1)}, u32[]{:S(2)}, u32[]{:S(2)}) collective-permute-start(bf16[2048,256]{1,0:T(8,128)(2,1)S(1)} %get-tuple-element.22), channel_id=1, source_target_pairs={{0,8},{1,9},{2,10},{3,11},{4,12},{5,13},{6,14},{7,15},{8,0},{9,1},... | collective-permute-start | bytes 3145736 | tf_op jit(solution)/shard_map/ppermute | solution.py:39
  77.2 11.7 %collective-permute-start.12 = (bf16[512,512]{1,0:T(8,128)(2,1)S(1)}, bf16[512,512]{1,0:T(8,128)(2,1)S(1)}, u32[]{:S(2)}, u32[]{:S(2)}) collective-permute-start(bf16[512,512]{1,0:T(8,128)(2,1)S(1)} %get-tuple-element.20), channel_id=1, source_target_pairs={{0,8},{1,9},{2,10},{3,11},{4,12},{5,13},{6,14},{7,15},{8,0},{9,1},... | collective-permute-start | bytes 1572872 | tf_op jit(solution)/shard_map/ppermute | solution.py:39
  80.2 13.8 %collective-permute-start.17 = (bf16[512,256]{1,0:T(8,128)(2,1)S(1)}, bf16[512,256]{1,0:T(8,128)(2,1)S(1)}, u32[]{:S(2)}, u32[]{:S(2)}) collective-permute-start(bf16[512,256]{1,0:T(8,128)(2,1)S(1)} %get-tuple-element.23), channel_id=1, source_target_pairs={{0,2},{1,3},{2,4},{3,5},{4,6},{5,7},{6,0},{7,1},{8,10},{9,11},{10,... | collective-permute-start | bytes 786440 | tf_op jit(solution)/shard_map/ppermute | solution.py:39
  84.9 14.1 %collective-permute-start.19 = (bf16[512,256]{1,0:T(8,128)(2,1)S(1)}, bf16[512,256]{1,0:T(8,128)(2,1)S(1)}, u32[]{:S(2)}, u32[]{:S(2)}) collective-permute-start(bf16[512,256]{1,0:T(8,128)(2,1)S(1)} %get-tuple-element.24), channel_id=1, source_target_pairs={{0,6},{1,7},{2,0},{3,1},{4,2},{5,3},{6,4},{7,5},{8,14},{9,15},{10,... | collective-permute-start | bytes 786440 | tf_op jit(solution)/shard_map/ppermute | solution.py:39
  87.5 13.3 %collective-permute-start.18 = (bf16[512,256]{1,0:T(8,128)(2,1)S(1)}, bf16[512,256]{1,0:T(8,128)(2,1)S(1)}, u32[]{:S(2)}, u32[]{:S(2)}) collective-permute-start(bf16[512,256]{1,0:T(8,128)(2,1)S(1)} %get-tuple-element.25), channel_id=1, source_target_pairs={{0,4},{1,5},{2,6},{3,7},{4,0},{5,1},{6,2},{7,3},{8,12},{9,13},{10,... | collective-permute-start | bytes 786440 | tf_op jit(solution)/shard_map/ppermute | solution.py:39
  89.0 16.2 %collective-permute-start.13 = (bf16[128,1024]{1,0:T(8,128)(2,1)S(1)}, bf16[128,1024]{1,0:T(8,128)(2,1)S(1)}, u32[]{:S(2)}, u32[]{:S(2)}) collective-permute-start(bf16[128,1024]{1,0:T(8,128)(2,1)S(1)} %get-tuple-element.26), channel_id=1, source_target_pairs={{0,64},{1,65},{2,66},{3,67},{4,68},{5,69},{6,70},{7,71},{8,72},{9,... | collective-permute-start | bytes 786440 | tf_op jit(solution)/shard_map/ppermute | solution.py:39
  89.1 18.3 %collective-permute-start.15 = (bf16[128,1024]{1,0:T(8,128)(2,1)S(1)}, bf16[128,1024]{1,0:T(8,128)(2,1)S(1)}, u32[]{:S(2)}, u32[]{:S(2)}) collective-permute-start(bf16[128,1024]{1,0:T(8,128)(2,1)S(1)} %get-tuple-element.27), channel_id=1, source_target_pairs={{0,65},{1,64},{2,67},{3,66},{4,69},{5,68},{6,71},{7,70},{8,73},{9,... | collective-permute-start | bytes 786440 | tf_op jit(solution)/shard_map/ppermute | solution.py:39
  94.0 13.4 %collective-permute-start.14 = (bf16[128,1024]{1,0:T(8,128)(2,1)S(1)}, bf16[128,1024]{1,0:T(8,128)(2,1)S(1)}, u32[]{:S(2)}, u32[]{:S(2)}) collective-permute-start(bf16[128,1024]{1,0:T(8,128)(2,1)S(1)} %get-tuple-element.28), channel_id=1, source_target_pairs={{0,1},{1,0},{2,3},{3,2},{4,5},{5,4},{6,7},{7,6},{8,9},{9,8},{10,11... | collective-permute-start | bytes 786440 | tf_op jit(solution)/shard_map/ppermute | solution.py:39
  101.0 7.3 %collective-permute-start.20 = (bf16[128,256]{1,0:T(8,128)(2,1)S(1)}, bf16[128,256]{1,0:T(8,128)(2,1)S(1)}, u32[]{:S(2)}, u32[]{:S(2)}) collective-permute-start(bf16[128,256]{1,0:T(8,128)(2,1)S(1)} %get-tuple-element.31), channel_id=1, source_target_pairs={{0,16},{1,17},{2,18},{3,19},{4,20},{5,21},{6,22},{7,23},{8,24},{9,... | collective-permute-start | bytes 196616 | tf_op jit(solution)/shard_map/ppermute | solution.py:39
  101.3 7.0 %collective-permute-start.22 = (bf16[128,256]{1,0:T(8,128)(2,1)S(1)}, bf16[128,256]{1,0:T(8,128)(2,1)S(1)}, u32[]{:S(2)}, u32[]{:S(2)}) collective-permute-start(bf16[128,256]{1,0:T(8,128)(2,1)S(1)} %get-tuple-element.32), channel_id=1, source_target_pairs={{0,48},{1,49},{2,50},{3,51},{4,52},{5,53},{6,54},{7,55},{8,56},{9,... | collective-permute-start | bytes 196616 | tf_op jit(solution)/shard_map/ppermute | solution.py:39
  105.2 5.8 %collective-permute-start.21 = (bf16[128,256]{1,0:T(8,128)(2,1)S(1)}, bf16[128,256]{1,0:T(8,128)(2,1)S(1)}, u32[]{:S(2)}, u32[]{:S(2)}) collective-permute-start(bf16[128,256]{1,0:T(8,128)(2,1)S(1)} %get-tuple-element.33), channel_id=1, source_target_pairs={{0,32},{1,33},{2,34},{3,35},{4,36},{5,37},{6,38},{7,39},{8,40},{9,... | collective-permute-start | bytes 196616 | tf_op jit(solution)/shard_map/ppermute | solution.py:39

commit v3 on v2

v3 whole, which is shorter than its diff:
```python
import functools
import math

import jax
import jax.numpy as jnp
from jax import lax
from jax.experimental import pallas as pl
from jax.experimental.pallas import tpu as pltpu
from jax.sharding import PartitionSpec as P

WIDTH = 128
BLOCK = 64
KEY_TILE = 512
PAIR = 2
HALF_HEADS = 4
COLS = HALF_HEADS * BLOCK
STAT_ROWS = 16
SIB_AT = 2 * BLOCK + STAT_ROWS
LOG2E = 1.4426950408889634
AXES = ("outer", "inner")


def linear(x, y, z, core):
    return (((y % 2) * 4 + z) * 2 + core) * 8 + x * 2 + y // 2


def place(index):
    inner = index % 8
    outer = index // 8
    return inner // 2, (inner % 2) * 2 + outer // 8, (outer // 2) % 4, outer % 2


def shift(block, dx=0, dy=0, dz=0, dcore=0):
    route = []
    for index in range(128):
        x, y, z, core = place(index)
        to = linear((x + dx) % 4, (y + dy) % 4, (z + dz) % 4, (core + dcore) % 2)
        route.append((index, to))
    return lax.ppermute(block, AXES, route)


def nt(a, b):
    return lax.dot_general(a, b, (((1,), (1,)), ((), ())), preferred_element_type=jnp.float32)


def nn(a, b):
    return lax.dot_general(a, b, (((1,), (0,)), ((), ())), preferred_element_type=jnp.float32)


def attend_kernel(
    q_rank, k_rank, q_sorted, k_sorted, counts,
    pay0, pay1, pay2a, pay2b, pay3, own0, own1, own2, own3, sib0, sib1, sib2,
    dq_own, dq_sib, dkv_own, dkv_sib,
    ks, vs, kt, dk, dv, qs, gs, dq, lse_s, del_s, s_scr, p_scr, plain, edge,
):
    key_blocks, query_blocks = k_rank.shape[0], q_rank.shape[0]
    per_tile = KEY_TILE // BLOCK
    key_tiles, query_tiles = key_blocks // per_tile, query_blocks // PAIR
    half_keys = key_blocks // 2
    span = PAIR * COLS
    scale = 1.0 / math.sqrt(WIDTH)
    factor = scale * LOG2E

    listed = 0
    for kv in (own0, own1, own2, own3, sib0, sib1, sib2):
        def bring(r, _, kv=kv, listed=listed):
            src = pl.multiple_of(r * BLOCK, BLOCK)
            dst = pl.multiple_of(k_rank[listed + r] * BLOCK, BLOCK)
            ks[pl.ds(dst, BLOCK), :] = kv[pl.ds(src, BLOCK), :WIDTH]
            vs[pl.ds(dst, BLOCK), :] = kv[pl.ds(src, BLOCK), WIDTH:]
            return 0
        lax.fori_loop(0, kv.shape[0] // BLOCK, bring, 0, unroll=4)
        listed += kv.shape[0] // BLOCK

    def ready(j, _):
        kt[j] = ks[pl.ds(pl.multiple_of(j * KEY_TILE, KEY_TILE), KEY_TILE), :].T
        dk[j] = jnp.zeros((KEY_TILE, WIDTH), jnp.float32)
        dv[j] = jnp.zeros((KEY_TILE, WIDTH), jnp.float32)
        return 0
    lax.fori_loop(0, key_tiles, ready, 0)

    for s in range(query_blocks):
        pay, side = (pay0, pay1, pay2a, pay3)[s // 4], s % 4 // 2
        stats, rows = pay, side * SIB_AT + s % 2 * BLOCK
        if s // 4 == 2 and side:
            pay, rows = pay2b, s % 2 * BLOCK
        rank = q_rank[s]
        dst = pl.multiple_of(rank * COLS, COLS)
        for h in range(HALF_HEADS):
            qs[pl.ds(dst + h * BLOCK, BLOCK), :] = pay[rows:rows + BLOCK, h * WIDTH:(h + 1) * WIDTH]
            gs[pl.ds(dst + h * BLOCK, BLOCK), :] = pay[
                rows:rows + BLOCK, (HALF_HEADS + h) * WIDTH:(HALF_HEADS + h + 1) * WIDTH]
        stat = sum(
            stats[2 * BLOCK:SIB_AT, n * WIDTH:(n + 1) * WIDTH].astype(jnp.float32)
            for n in range(3))
        top, lanes = side * 2 * HALF_HEADS, slice(s % 2 * BLOCK, (s % 2 + 1) * BLOCK)
        lse_s[pl.ds(rank, 1), :] = jnp.concatenate(
            [stat[top + h:top + h + 1, lanes] for h in range(HALF_HEADS)], axis=1) * LOG2E
        top += HALF_HEADS
        del_s[pl.ds(rank, 1), :] = jnp.concatenate(
            [stat[top + h:top + h + 1, lanes] for h in range(HALF_HEADS)], axis=1)

    def listing(i, carry):
        dq[i] = jnp.zeros((WIDTH, span), jnp.float32)

        def put(listed):
            def one(j, at):
                listed[0, at] = i
                listed[1, at] = j
                return at + 1
            return one
        plains, edges = carry
        plains = lax.fori_loop(0, counts[0, i], put(plain), plains)
        return plains, lax.fori_loop(counts[0, i], counts[1, i], put(edge), edges)
    plains, edges = lax.fori_loop(0, query_tiles, listing, (jnp.int32(0), jnp.int32(0)))
    for listed, total in ((plain, plains), (edge, edges)):
        for extra in range(2):
            listed[0, total + extra] = 0
            listed[1, total + extra] = 0

    in_query = lax.broadcasted_iota(jnp.int32, (1, span), 1) % BLOCK
    in_key = lax.broadcasted_iota(jnp.int32, (BLOCK, span), 0)

    def sweep(listed, total, masked):
        def front(t, slot):
            i, j = listed[0, t], listed[1, t]
            ko, qo = pl.multiple_of(j * KEY_TILE, KEY_TILE), pl.multiple_of(i * span, span)
            s_scr[slot] = nt(ks[pl.ds(ko, KEY_TILE), :], qs[pl.ds(qo, span), :])
            p_scr[slot] = nt(vs[pl.ds(ko, KEY_TILE), :], gs[pl.ds(qo, span), :])

        def back(t, slot):
            i, j = listed[0, t], listed[1, t]
            qo = pl.multiple_of(i * span, span)
            lse = jnp.concatenate([lse_s[pl.ds(i * PAIR + u, 1), :] for u in range(PAIR)], axis=1)
            lse = jnp.where(t < total, lse, 1e30)
            delta = jnp.concatenate([del_s[pl.ds(i * PAIR + u, 1), :] for u in range(PAIR)], axis=1)
            query_pos = in_query + jnp.concatenate(
                [jnp.full((1, COLS), q_sorted[i * PAIR + u] * BLOCK, jnp.int32) for u in range(PAIR)],
                axis=1)
            probs_parts, dscores_parts = [], []
            for u in range(per_tile):
                scores = s_scr[slot, u * BLOCK:(u + 1) * BLOCK, :]
                dprobs = p_scr[slot, u * BLOCK:(u + 1) * BLOCK, :]
                probs = jnp.exp2(scores * factor - lse)
                if masked:
                    allowed = in_key <= query_pos - k_sorted[j * per_tile + u] * BLOCK
                    probs = jnp.where(allowed, probs, 0.0)
                dscores_parts.append((probs * (dprobs - delta)).astype(jnp.bfloat16))
                probs_parts.append(probs.astype(jnp.bfloat16))
            probs_half = jnp.concatenate(probs_parts, axis=0)
            dscores_half = jnp.concatenate(dscores_parts, axis=0)
            dv[j] += nn(probs_half, gs[pl.ds(qo, span), :])
            dk[j] += nn(dscores_half, qs[pl.ds(qo, span), :])
            dq[i] += nn(kt[j], dscores_half)

        front(0, 0)

        def two(h, _):
            front(2 * h + 1, 1)
            back(2 * h, 0)
            front(2 * h + 2, 0)
            back(2 * h + 1, 1)
            return 0
        lax.fori_loop(0, (total + 1) // 2, two, 0)

    sweep(plain, plains, False)
    sweep(edge, edges, True)

    for s in range(query_blocks):
        rank = q_rank[s]
        out = (dq_own, dq_sib)[s % 4 // 2]
        rows = s // 4 * 2 * BLOCK + s % 2 * BLOCK
        block = dq[rank // PAIR, :, pl.ds(pl.multiple_of(rank % PAIR * COLS, COLS), COLS)]
        block = (block.T * scale).astype(jnp.bfloat16)
        for h in range(HALF_HEADS):
            out[rows:rows + BLOCK, h * WIDTH:(h + 1) * WIDTH] = block[h * BLOCK:(h + 1) * BLOCK]
    for half, out in enumerate((dkv_own, dkv_sib)):
        def give(r, _, out=out, half=half):
            dst = pl.multiple_of(r * BLOCK, BLOCK)
            rank = k_rank[half * half_keys + r]
            j, src = rank // per_tile, pl.multiple_of(rank % per_tile * BLOCK, BLOCK)
            out[pl.ds(dst, BLOCK), :WIDTH] = (dk[j, pl.ds(src, BLOCK), :] * scale).astype(jnp.bfloat16)
            out[pl.ds(dst, BLOCK), WIDTH:] = dv[j, pl.ds(src, BLOCK), :].astype(jnp.bfloat16)
            return 0
        lax.fori_loop(0, half_keys, give, 0, unroll=4)


def attend(q_rank, k_rank, q_sorted, k_sorted, counts, pays, kvs):
    key_blocks, query_blocks = k_rank.shape[0], q_rank.shape[0]
    keys = key_blocks * BLOCK
    key_tiles, query_tiles = keys // KEY_TILE, query_blocks // PAIR
    span = PAIR * COLS
    bf16, f32 = jnp.bfloat16, jnp.float32
    smem, vmem = pl.BlockSpec(memory_space=pltpu.SMEM), pl.BlockSpec(memory_space=pltpu.VMEM)
    listed = query_tiles * key_tiles + 2
    return pl.pallas_call(
        attend_kernel,
        in_specs=[smem] * 5 + [vmem] * 12,
        out_specs=[vmem] * 4,
        out_shape=[jax.ShapeDtypeStruct((8 * BLOCK, HALF_HEADS * WIDTH), bf16)] * 2
        + [jax.ShapeDtypeStruct((keys // 2, 2 * WIDTH), bf16)] * 2,
        scratch_shapes=[
            pltpu.VMEM((keys, WIDTH), bf16),
            pltpu.VMEM((keys, WIDTH), bf16),
            pltpu.VMEM((key_tiles, WIDTH, KEY_TILE), bf16),
            pltpu.VMEM((key_tiles, KEY_TILE, WIDTH), f32),
            pltpu.VMEM((key_tiles, KEY_TILE, WIDTH), f32),
            pltpu.VMEM((query_blocks * COLS, WIDTH), bf16),
            pltpu.VMEM((query_blocks * COLS, WIDTH), bf16),
            pltpu.VMEM((query_tiles, WIDTH, span), f32),
            pltpu.VMEM((query_blocks, COLS), f32),
            pltpu.VMEM((query_blocks, COLS), f32),
            pltpu.VMEM((2, KEY_TILE, span), f32),
            pltpu.VMEM((2, KEY_TILE, span), f32),
            pltpu.SMEM((2, listed), jnp.int32),
            pltpu.SMEM((2, listed), jnp.int32),
        ],
        compiler_params=pltpu.CompilerParams(vmem_limit_bytes=32 * 1024 * 1024),
    )(q_rank, k_rank, q_sorted, k_sorted, counts, *pays, *kvs)


def ranked(block_order, blocks):
    listed = jnp.arange(block_order.shape[0], dtype=jnp.int32)
    pos = jnp.sum(jnp.where(blocks[:, None] == listed[None, :], block_order[None, :], 0), axis=1)
    rank = jnp.sum((pos[None, :] < pos[:, None]).astype(jnp.int32), axis=1)
    at = jnp.arange(blocks.shape[0], dtype=jnp.int32)
    return rank, jnp.sum(jnp.where(rank[None, :] == at[:, None], pos[None, :], 0), axis=1)


def total_of(parts):
    return functools.reduce(lambda a, b: a + b, [p.astype(jnp.float32) for p in parts])


def thirds(array):
    high = lax.reduce_precision(array, 8, 7)
    middle = lax.reduce_precision(array - high, 8, 7)
    low = lax.reduce_precision(array - high - middle, 8, 7)
    return jnp.concatenate([high, middle, low], axis=1).astype(jnp.bfloat16)


def body(query_rows, key_rows, value_rows, saved_output, output_grad, logsumexp, block_order):
    rows = query_rows.shape[0]
    half = HALF_HEADS * WIDTH
    x, y, z, core = place(lax.axis_index("outer") * 8 + lax.axis_index("inner"))
    first = core == 0

    def mine(array):
        return jnp.where(first, array[:, :half], array[:, half:])

    def other(array):
        return jnp.where(first, array[:, half:], array[:, :half])

    heads = (rows, 2 * HALF_HEADS, WIDTH)
    delta = jnp.sum(
        output_grad.reshape(heads).astype(jnp.float32)
        * saved_output.reshape(heads).astype(jnp.float32), axis=2).T
    low = jnp.concatenate([logsumexp[:HALF_HEADS], delta[:HALF_HEADS]], axis=0)
    high = jnp.concatenate([logsumexp[HALF_HEADS:], delta[HALF_HEADS:]], axis=0)

    kv = jnp.concatenate([key_rows, value_rows], axis=1)
    sib = shift(jnp.concatenate([other(query_rows), other(output_grad)], axis=1), dcore=1)
    sib, kv = lax.optimization_barrier((sib, kv))
    stat_sib = shift(jnp.where(first, high, low), dcore=1)
    stat = thirds(jnp.concatenate([jnp.where(first, low, high), stat_sib], axis=0))
    stat = jnp.pad(stat, ((0, 0), (0, 2 * half - stat.shape[1])))
    pay = jnp.concatenate(
        [jnp.concatenate([mine(query_rows), mine(output_grad)], axis=1), stat, sib], axis=0)
    kv_line = jnp.concatenate([kv] + [shift(kv, dz=-d) for d in (1, 2, 3)], axis=0)
    lines = [kv_line] + [shift(kv_line, dx=-d) for d in (1, 2, 3)]
    after, before = shift(pay, dy=-1), shift(pay, dy=1)
    after, before, *lines = lax.optimization_barrier((after, before, *lines))
    across = shift(after[:SIB_AT], dy=-1), shift(before[SIB_AT:], dy=1)
    pays = [pay, after, *across, before]
    joined = [jnp.concatenate(lines[:2], axis=0), *lines[2:]]
    kvs = lines + [shift(line, dcore=1) for line in joined]

    four = jnp.arange(4, dtype=jnp.int32)
    two = jnp.arange(2, dtype=jnp.int32)
    dy, cs, b = (a.reshape(-1) for a in jnp.meshgrid(four, two, two, indexing="ij"))
    q_rank, q_sorted = ranked(block_order, 2 * linear(x, (y + dy) % 4, z, (core + cs) % 2) + b)
    cs, dx, dz, b = (a.reshape(-1) for a in jnp.meshgrid(two, four, four, two, indexing="ij"))
    k_rank, k_sorted = ranked(
        block_order, 2 * linear((x + dx) % 4, y, (z + dz) % 4, (core + cs) % 2) + b)

    tops, lows = q_sorted[PAIR - 1::PAIR], q_sorted[::PAIR]
    reached = jnp.sum((k_sorted[None, :] <= tops[:, None]).astype(jnp.int32), axis=1)
    passed = jnp.sum((k_sorted[None, :] < lows[:, None]).astype(jnp.int32), axis=1)
    per_tile = KEY_TILE // BLOCK
    counts = jnp.stack([passed // per_tile, (reached + per_tile - 1) // per_tile])

    dq_own, dq_sib, dkv_own, dkv_sib = attend(
        q_rank, k_rank, q_sorted, k_sorted, counts, pays, kvs)

    dkv = total_of([dkv_own, shift(dkv_sib, dcore=1)]).astype(jnp.bfloat16)
    dq_far = shift(dq_sib, dcore=1)
    dq = jnp.concatenate(
        [jnp.where(first, dq_own, dq_far), jnp.where(first, dq_far, dq_own)], axis=1)
    quarter = dkv.shape[0] // 4
    parts = [dkv[d * quarter:(d + 1) * quarter] for d in range(4)]
    line = total_of([parts[0]] + [shift(parts[d], dx=d) for d in (1, 2, 3)]).astype(jnp.bfloat16)
    parts = [line[d * rows:(d + 1) * rows] for d in range(4)]
    done = total_of([parts[0]] + [shift(parts[d], dz=d) for d in (1, 2, 3)])
    parts = [dq[d * rows:(d + 1) * rows] for d in range(4)]
    query_grad = total_of([parts[0]] + [shift(parts[d], dy=d) for d in (1, 2, 3)]).astype(jnp.bfloat16)
    return (
        query_grad,
        done[:, :WIDTH].astype(jnp.bfloat16),
        done[:, WIDTH:].astype(jnp.bfloat16),
    )


def solution(mesh):
    rows = P(AXES, None)
    return jax.shard_map(
        body,
        mesh=mesh,
        in_specs=(rows, rows, rows, rows, rows, P(None, AXES), P()),
        out_specs=(rows, rows, rows),
        check_vma=False,
    )
```

time: 113 us -> 111 us (0.982)
  starting transfers between devices: 40.6 us -> 52.3 us
  Pallas kernels: 35.3 us -> 27.2 us
  waiting for transfers between devices: 26.7 us -> 22 us
  local copies, waits for them, and re-layouts: 4.08 us -> 2.34 us
    ppermute x23 -> x26, starting transfers between devices: 40.6 us -> 52.3 us  [shift(): return lax.ppermute(block, AXES, route)]
    pallas_call x1, Pallas kernels: 35.3 us -> 27.2 us  [attend(): pl.pallas_call(attend_kernel, in_specs=[smem] * 5 + [vmem] * 12, out_spec...]
    ppermute x23 -> x26, waiting for transfers between devices: 26.7 us -> 22 us  [shift(): return lax.ppermute(block, AXES, route)]
  transfers between devices with their start and end apart: 23 -> 26, of which waited for: 8 -> 8; matrix products, arithmetic and copies ran while one was open for 3% -> 4% of each run, Pallas kernels for 0% -> 0%
where the time goes in v3:
time: 111 us; the launch traced here: 109 us
  starting transfers between devices  52.3 us (47%)
  Pallas kernels  27.2 us (25%)
  waiting for transfers between devices  22 us (20%)
  other arithmetic  4.22 us (4%)
  local copies, waits for them, and re-layouts  2.34 us (2%)
    ppermute x26, starting transfers between devices, shift(): return lax.ppermute(block, AXES, route)  52.3 us
    pallas_call x1, Pallas kernels, attend(): pl.pallas_call(attend_kernel, in_specs=[smem] * 5 + [vmem] * 12, out_spec...  27.2 us
    ppermute x26, waiting for transfers between devices, shift(): return lax.ppermute(block, AXES, route)  22 us
  transfers between devices with their start and end apart: 26, of which 8 were waited for; matrix products, arithmetic and copies ran while one was open for 4% of the time, Pallas kernels for 0%

profile of v3, /device:TPU:0, one launch (start us, length us, event | category | flops | bytes accessed | tf_op | source)
XLA Modules:
  0.0 109.2 jit_solution(17022205544952512772)
XLA Ops:
  0.7 1.1 multiply_bitcast_fusion
  2.9 0.3 collective-permute-start.1
  4.5 2.1 %collective-permute-start.6 = (bf16[128,256]{1,0:T(8,128)(2,1)S(1)}, bf16[128,256]{1,0:T(8,128)(2,1)S(1)}, u32[]{:S(2)}, u32[]{:S(2)}) collective-permute-start(bf16[128,256]{1,0:T(8,128)(2,1)S(1)} %pad_maximum_fusion.4), channel_id=1, source_target_pairs={{0,16},{1,17},{2,18},{3,19},{4,20},{5,21},{6,22},{7,23},{8,24},{9,... | collective-permute-start | bytes 196616 | tf_op jit(solution)/shard_map/ppermute | solution.py:39
  6.6 3.6 %collective-permute-start.5 = (bf16[128,256]{1,0:T(8,128)(2,1)S(1)}, bf16[128,256]{1,0:T(8,128)(2,1)S(1)}, u32[]{:S(2)}, u32[]{:S(2)}) collective-permute-start(bf16[128,256]{1,0:T(8,128)(2,1)S(1)} %pad_maximum_fusion.4), channel_id=1, source_target_pairs={{0,32},{1,33},{2,34},{3,35},{4,36},{5,37},{6,38},{7,39},{8,40},{9,... | collective-permute-start | bytes 196616 | tf_op jit(solution)/shard_map/ppermute | solution.py:39
  10.2 1.0 collective-permute-start.4
  11.3 1.6 %collective-permute-start.3 = (bf16[272,1024]{1,0:T(8,128)(2,1)S(1)}, bf16[272,1024]{1,0:T(8,128)(2,1)S(1)}, u32[]{:S(2)}, u32[]{:S(2)}) collective-permute-start(bf16[272,1024]{1,0:T(8,128)(2,1)S(1)} %pad_maximum_fusion.pay0), channel_id=1, source_target_pairs={{0,64},{1,65},{2,66},{3,67},{4,68},{5,69},{6,70},{7,71},{8,72},{9,... | collective-permute-start | bytes 1671176 | tf_op jit(solution)/shard_map/ppermute | solution.py:39
  12.9 1.7 %collective-permute-start.2 = (bf16[272,1024]{1,0:T(8,128)(2,1)S(1)}, bf16[272,1024]{1,0:T(8,128)(2,1)S(1)}, u32[]{:S(2)}, u32[]{:S(2)}) collective-permute-start(bf16[272,1024]{1,0:T(8,128)(2,1)S(1)} %pad_maximum_fusion.pay0), channel_id=1, source_target_pairs={{0,65},{1,64},{2,67},{3,66},{4,69},{5,68},{6,71},{7,70},{8,73},{9,... | collective-permute-start | bytes 1671176 | tf_op jit(solution)/shard_map/ppermute | solution.py:39
  14.6 1.6 %collective-permute-start.9 = (bf16[512,256]{1,0:T(8,128)(2,1)S(1)}, bf16[512,256]{1,0:T(8,128)(2,1)S(1)}, u32[]{:S(2)}, u32[]{:S(2)}) collective-permute-start(bf16[512,256]{1,0:T(8,128)(2,1)S(1)} %constant_dynamic-update-slice_fusion.own0), channel_id=1, source_target_pairs={{0,2},{1,3},{2,4},{3,5},{4,6},{5,7},{6,0},{7,1},{8,10},{9,11},{10,... | collective-permute-start | bytes 786440 | tf_op jit(solution)/shard_map/ppermute | solution.py:39
  16.2 2.7 %collective-permute-start.8 = (bf16[512,256]{1,0:T(8,128)(2,1)S(1)}, bf16[512,256]{1,0:T(8,128)(2,1)S(1)}, u32[]{:S(2)}, u32[]{:S(2)}) collective-permute-start(bf16[512,256]{1,0:T(8,128)(2,1)S(1)} %constant_dynamic-update-slice_fusion.own0), channel_id=1, source_target_pairs={{0,4},{1,5},{2,6},{3,7},{4,0},{5,1},{6,2},{7,3},{8,12},{9,13},{10,... | collective-permute-start | bytes 786440 | tf_op jit(solution)/shard_map/ppermute | solution.py:39
  18.9 1.4 %collective-permute-start.7 = (bf16[512,256]{1,0:T(8,128)(2,1)S(1)}, bf16[512,256]{1,0:T(8,128)(2,1)S(1)}, u32[]{:S(2)}, u32[]{:S(2)}) collective-permute-start(bf16[512,256]{1,0:T(8,128)(2,1)S(1)} %constant_dynamic-update-slice_fusion.own0), channel_id=1, source_target_pairs={{0,6},{1,7},{2,0},{3,1},{4,2},{5,3},{6,4},{7,5},{8,14},{9,15},{10,... | collective-permute-start | bytes 786440 | tf_op jit(solution)/shard_map/ppermute | solution.py:39
  21.1 3.1 %collective-permute-done.9.own3 = bf16[512,256]{1,0:T(8,128)(2,1)S(1)} collective-permute-done((bf16[512,256]{1,0:T(8,128)(2,1)S(1)}, bf16[512,256]{1,0:T(8,128)(2,1)S(1)}, u32[]{:S(2)}, u32[]{:S(2)}) %collective-permute-start.9) | collective-permute-done | bytes 262176 | tf_op jit(solution)/shard_map/ppermute | solution.py:39
  24.2 5.6 %collective-permute-done.8.own2 = bf16[512,256]{1,0:T(8,128)(2,1)S(1)} collective-permute-done((bf16[512,256]{1,0:T(8,128)(2,1)S(1)}, bf16[512,256]{1,0:T(8,128)(2,1)S(1)}, u32[]{:S(2)}, u32[]{:S(2)}) %collective-permute-start.8) | collective-permute-done | bytes 262176 | tf_op jit(solution)/shard_map/ppermute | solution.py:39
  30.2 1.4 %collective-permute-start.11 = (bf16[128,1024]{1,0:T(8,128)(2,1)S(1)}, bf16[128,1024]{1,0:T(8,128)(2,1)S(1)}, u32[]{:S(2)}, u32[]{:S(2)}) collective-permute-start(bf16[128,1024]{1,0:T(8,128)(2,1)S(1)} %slice.95), channel_id=1, source_target_pairs={{0,64},{1,65},{2,66},{3,67},{4,68},{5,69},{6,70},{7,71},{8,72},{9,... | collective-permute-start | bytes 786440 | tf_op jit(solution)/shard_map/ppermute | solution.py:39
  32.1 2.0 %collective-permute-start.10 = (bf16[144,1024]{1,0:T(8,128)(2,1)S(1)}, bf16[144,1024]{1,0:T(8,128)(2,1)S(1)}, u32[]{:S(2)}, u32[]{:S(2)}) collective-permute-start(bf16[144,1024]{1,0:T(8,128)(2,1)S(1)} %slice.94), channel_id=1, source_target_pairs={{0,65},{1,64},{2,67},{3,66},{4,69},{5,68},{6,71},{7,70},{8,73},{9,... | collective-permute-start | bytes 884744 | tf_op jit(solution)/shard_map/ppermute | solution.py:39
  34.2 6.0 %collective-permute-done.11.pay2b = bf16[128,1024]{1,0:T(8,128)(2,1)S(1)} collective-permute-done((bf16[128,1024]{1,0:T(8,128)(2,1)S(1)}, bf16[128,1024]{1,0:T(8,128)(2,1)S(1)}, u32[]{:S(2)}, u32[]{:S(2)}) %collective-permute-start.11) | collective-permute-done | bytes 262176 | tf_op jit(solution)/shard_map/ppermute | solution.py:39
  40.2 1.1 %collective-permute-done.10.pay2a = bf16[144,1024]{1,0:T(8,128)(2,1)S(1)} collective-permute-done((bf16[144,1024]{1,0:T(8,128)(2,1)S(1)}, bf16[144,1024]{1,0:T(8,128)(2,1)S(1)}, u32[]{:S(2)}, u32[]{:S(2)}) %collective-permute-start.10) | collective-permute-done | bytes 294944 | tf_op jit(solution)/shard_map/ppermute | solution.py:39
  41.3 27.2 %shard_map.94 = (bf16[512,512]{1,0:T(8,128)(2,1)S(1)}, bf16[512,512]{1,0:T(8,128)(2,1)S(1)}, bf16[2048,256]{1,0:T(8,128)(2,1)S(1)}, bf16[2048,256]{1,0:T(8,128)(2,1)S(1)}) custom-call(s32[16]{0:T(128)S(1)} %convert_reduce_fusion.1.q_rank, s32[64]{0:T(128)S(1)} %convert_reduce_fusion.k_rank, s32[16]{0:T(128)S(1)} %select_reduce_fusion.3.q_sorted, ...), custom_call_target="tpu_custom_call" | custom-call | tf_op jit(solution)/shard_map/pallas_call | solution.py:196
  68.6 0.5 collective-permute-start.15
  69.1 2.1 %collective-permute-done.19 = bf16[2048,256]{1,0:T(8,128)(2,1)S(1)} collective-permute-done((bf16[2048,256]{1,0:T(8,128)(2,1)S(1)}, bf16[2048,256]{1,0:T(8,128)(2,1)S(1)}, u32[]{:S(2)}, u32[]{:S(2)}) %collective-permute-start.19) | collective-permute-done | bytes 1048608 | tf_op jit(solution)/shard_map/ppermute | solution.py:39
  71.6 5.5 %collective-permute-start.20 = (bf16[512,256]{1,0:T(8,128)(2,1)S(1)}, bf16[512,256]{1,0:T(8,128)(2,1)S(1)}, u32[]{:S(2)}, u32[]{:S(2)}) collective-permute-start(bf16[512,256]{1,0:T(8,128)(2,1)S(1)} %get-tuple-element.29), channel_id=1, source_target_pairs={{0,2},{1,3},{2,4},{3,5},{4,6},{5,7},{6,0},{7,1},{8,10},{9,11},{10,... | collective-permute-start | bytes 786440 | tf_op jit(solution)/shard_map/ppermute | solution.py:39
  77.1 2.8 %collective-permute-start.22 = (bf16[512,256]{1,0:T(8,128)(2,1)S(1)}, bf16[512,256]{1,0:T(8,128)(2,1)S(1)}, u32[]{:S(2)}, u32[]{:S(2)}) collective-permute-start(bf16[512,256]{1,0:T(8,128)(2,1)S(1)} %get-tuple-element.30), channel_id=1, source_target_pairs={{0,6},{1,7},{2,0},{3,1},{4,2},{5,3},{6,4},{7,5},{8,14},{9,15},{10,... | collective-permute-start | bytes 786440 | tf_op jit(solution)/shard_map/ppermute | solution.py:39
  79.9 1.4 %collective-permute-start.21 = (bf16[512,256]{1,0:T(8,128)(2,1)S(1)}, bf16[512,256]{1,0:T(8,128)(2,1)S(1)}, u32[]{:S(2)}, u32[]{:S(2)}) collective-permute-start(bf16[512,256]{1,0:T(8,128)(2,1)S(1)} %get-tuple-element.31), channel_id=1, source_target_pairs={{0,4},{1,5},{2,6},{3,7},{4,0},{5,1},{6,2},{7,3},{8,12},{9,13},{10,... | collective-permute-start | bytes 786440 | tf_op jit(solution)/shard_map/ppermute | solution.py:39
  81.5 4.9 %collective-permute-start.16 = (bf16[128,1024]{1,0:T(8,128)(2,1)S(1)}, bf16[128,1024]{1,0:T(8,128)(2,1)S(1)}, u32[]{:S(2)}, u32[]{:S(2)}) collective-permute-start(bf16[128,1024]{1,0:T(8,128)(2,1)S(1)} %get-tuple-element.32), channel_id=1, source_target_pairs={{0,64},{1,65},{2,66},{3,67},{4,68},{5,69},{6,70},{7,71},{8,72},{9,... | collective-permute-start | bytes 786440 | tf_op jit(solution)/shard_map/ppermute | solution.py:39
  86.4 2.0 %collective-permute-start.18 = (bf16[128,1024]{1,0:T(8,128)(2,1)S(1)}, bf16[128,1024]{1,0:T(8,128)(2,1)S(1)}, u32[]{:S(2)}, u32[]{:S(2)}) collective-permute-start(bf16[128,1024]{1,0:T(8,128)(2,1)S(1)} %get-tuple-element.33), channel_id=1, source_target_pairs={{0,65},{1,64},{2,67},{3,66},{4,69},{5,68},{6,71},{7,70},{8,73},{9,... | collective-permute-start | bytes 786440 | tf_op jit(solution)/shard_map/ppermute | solution.py:39
  88.4 2.2 %collective-permute-start.17 = (bf16[128,1024]{1,0:T(8,128)(2,1)S(1)}, bf16[128,1024]{1,0:T(8,128)(2,1)S(1)}, u32[]{:S(2)}, u32[]{:S(2)}) collective-permute-start(bf16[128,1024]{1,0:T(8,128)(2,1)S(1)} %get-tuple-element.34), channel_id=1, source_target_pairs={{0,1},{1,0},{2,3},{3,2},{4,5},{5,4},{6,7},{7,6},{8,9},{9,8},{10,11... | collective-permute-start | bytes 786440 | tf_op jit(solution)/shard_map/ppermute | solution.py:39
  90.6 0.8 collective-permute-done.22
  91.4 1.8 %collective-permute-done.21 = bf16[512,256]{1,0:T(8,128)(2,1)S(1)} collective-permute-done((bf16[512,256]{1,0:T(8,128)(2,1)S(1)}, bf16[512,256]{1,0:T(8,128)(2,1)S(1)}, u32[]{:S(2)}, u32[]{:S(2)}) %collective-permute-start.21) | collective-permute-done | bytes 262176 | tf_op jit(solution)/shard_map/ppermute | solution.py:39
  93.5 3.2 %collective-permute-start.25 = (bf16[128,256]{1,0:T(8,128)(2,1)S(1)}, bf16[128,256]{1,0:T(8,128)(2,1)S(1)}, u32[]{:S(2)}, u32[]{:S(2)}) collective-permute-start(bf16[128,256]{1,0:T(8,128)(2,1)S(1)} %get-tuple-element.38), channel_id=1, source_target_pairs={{0,48},{1,49},{2,50},{3,51},{4,52},{5,53},{6,54},{7,55},{8,56},{9,... | collective-permute-start | bytes 196616 | tf_op jit(solution)/shard_map/ppermute | solution.py:39
  96.7 9.6 %collective-permute-start.24 = (bf16[128,256]{1,0:T(8,128)(2,1)S(1)}, bf16[128,256]{1,0:T(8,128)(2,1)S(1)}, u32[]{:S(2)}, u32[]{:S(2)}) collective-permute-start(bf16[128,256]{1,0:T(8,128)(2,1)S(1)} %get-tuple-element.39), channel_id=1, source_target_pairs={{0,32},{1,33},{2,34},{3,35},{4,36},{5,37},{6,38},{7,39},{8,40},{9,... | collective-permute-start | bytes 196616 | tf_op jit(solution)/shard_map/ppermute | solution.py:39
  106.3 0.9 add_convert_fusion.2
  107.1 1.4 %collective-permute-done.24 = bf16[128,256]{1,0:T(8,128)(2,1)S(1)} collective-permute-done((bf16[128,256]{1,0:T(8,128)(2,1)S(1)}, bf16[128,256]{1,0:T(8,128)(2,1)S(1)}, u32[]{:S(2)}, u32[]{:S(2)}) %collective-permute-start.24) | collective-permute-done | bytes 65568 | tf_op jit(solution)/shard_map/ppermute | solution.py:39
  108.6 0.6 fusion.28
  (88 shorter events, 4.9 us)
Async XLA Ops:
  1.8 0.7 copy-start.5
  1.8 1.0 copy-start
  1.8 1.0 copy-start.1
  2.1 2.0 %copy-start.4 = (s32[256]{0:T(256)S(1)}, s32[256]{0:T(256)}, u32[]{:S(2)}) copy-start(s32[256]{0:T(256)} %param.13) | copy-start | bytes 3076
  2.1 2.1 %copy-start.2 = (bf16[128,128]{1,0:T(8,128)(2,1)S(1)}, bf16[128,128]{1,0:T(8,128)(2,1)}, u32[]{:S(2)}) copy-start(bf16[128,128]{1,0:T(8,128)(2,1)} %param.9) | copy-start | bytes 98308
  2.1 2.1 %copy-start.3 = (bf16[128,128]{1,0:T(8,128)(2,1)S(1)}, bf16[128,128]{1,0:T(8,128)(2,1)}, u32[]{:S(2)}) copy-start(bf16[128,128]{1,0:T(8,128)(2,1)} %param.8) | copy-start | bytes 98308
  2.5 2.0 %collective-permute-start = (f32[8,128]{1,0:T(8,128)S(1)}, f32[8,128]{1,0:T(8,128)S(1)}, u32[]{:S(2)}, u32[]{:S(2)}) collective-permute-start(f32[8,128]{1,0:T(8,128)S(1)} %get-tuple-element.50), channel_id=1, source_target_pairs={{0,8},{1,9},{2,10},{3,11},{4,12},{5,13},{6,14},{7,15},{8,0},{9,1},... | collective-permute-start | bytes 12296 | tf_op jit(solution)/shard_map/ppermute | solution.py:39
  2.9 1.7 %collective-permute-start.1 = (bf16[128,1024]{1,0:T(8,128)(2,1)S(1)}, bf16[128,1024]{1,0:T(8,128)(2,1)S(1)}, u32[]{:S(2)}, u32[]{:S(2)}) collective-permute-start(bf16[128,1024]{1,0:T(8,128)(2,1)S(1)} %pad_maximum_fusion.3), channel_id=1, source_target_pairs={{0,8},{1,9},{2,10},{3,11},{4,12},{5,13},{6,14},{7,15},{8,0},{9,1},... | collective-permute-start | bytes 786440 | tf_op jit(solution)/shard_map/ppermute | solution.py:39
  4.5 10.1 %collective-permute-start.6 = (bf16[128,256]{1,0:T(8,128)(2,1)S(1)}, bf16[128,256]{1,0:T(8,128)(2,1)S(1)}, u32[]{:S(2)}, u32[]{:S(2)}) collective-permute-start(bf16[128,256]{1,0:T(8,128)(2,1)S(1)} %pad_maximum_fusion.4), channel_id=1, source_target_pairs={{0,16},{1,17},{2,18},{3,19},{4,20},{5,21},{6,22},{7,23},{8,24},{9,... | collective-permute-start | bytes 196616 | tf_op jit(solution)/shard_map/ppermute | solution.py:39
  6.6 8.0 %collective-permute-start.5 = (bf16[128,256]{1,0:T(8,128)(2,1)S(1)}, bf16[128,256]{1,0:T(8,128)(2,1)S(1)}, u32[]{:S(2)}, u32[]{:S(2)}) collective-permute-start(bf16[128,256]{1,0:T(8,128)(2,1)S(1)} %pad_maximum_fusion.4), channel_id=1, source_target_pairs={{0,32},{1,33},{2,34},{3,35},{4,36},{5,37},{6,38},{7,39},{8,40},{9,... | collective-permute-start | bytes 196616 | tf_op jit(solution)/shard_map/ppermute | solution.py:39
  10.2 4.4 %collective-permute-start.4 = (bf16[128,256]{1,0:T(8,128)(2,1)S(1)}, bf16[128,256]{1,0:T(8,128)(2,1)S(1)}, u32[]{:S(2)}, u32[]{:S(2)}) collective-permute-start(bf16[128,256]{1,0:T(8,128)(2,1)S(1)} %pad_maximum_fusion.4), channel_id=1, source_target_pairs={{0,48},{1,49},{2,50},{3,51},{4,52},{5,53},{6,54},{7,55},{8,56},{9,... | collective-permute-start | bytes 196616 | tf_op jit(solution)/shard_map/ppermute | solution.py:39
  11.3 18.5 %collective-permute-start.3 = (bf16[272,1024]{1,0:T(8,128)(2,1)S(1)}, bf16[272,1024]{1,0:T(8,128)(2,1)S(1)}, u32[]{:S(2)}, u32[]{:S(2)}) collective-permute-start(bf16[272,1024]{1,0:T(8,128)(2,1)S(1)} %pad_maximum_fusion.pay0), channel_id=1, source_target_pairs={{0,64},{1,65},{2,66},{3,67},{4,68},{5,69},{6,70},{7,71},{8,72},{9,... | collective-permute-start | bytes 1671176 | tf_op jit(solution)/shard_map/ppermute | solution.py:39
  12.9 16.8 %collective-permute-start.2 = (bf16[272,1024]{1,0:T(8,128)(2,1)S(1)}, bf16[272,1024]{1,0:T(8,128)(2,1)S(1)}, u32[]{:S(2)}, u32[]{:S(2)}) collective-permute-start(bf16[272,1024]{1,0:T(8,128)(2,1)S(1)} %pad_maximum_fusion.pay0), channel_id=1, source_target_pairs={{0,65},{1,64},{2,67},{3,66},{4,69},{5,68},{6,71},{7,70},{8,73},{9,... | collective-permute-start | bytes 1671176 | tf_op jit(solution)/shard_map/ppermute | solution.py:39
  14.6 9.5 %collective-permute-start.9 = (bf16[512,256]{1,0:T(8,128)(2,1)S(1)}, bf16[512,256]{1,0:T(8,128)(2,1)S(1)}, u32[]{:S(2)}, u32[]{:S(2)}) collective-permute-start(bf16[512,256]{1,0:T(8,128)(2,1)S(1)} %constant_dynamic-update-slice_fusion.own0), channel_id=1, source_target_pairs={{0,2},{1,3},{2,4},{3,5},{4,6},{5,7},{6,0},{7,1},{8,10},{9,11},{10,... | collective-permute-start | bytes 786440 | tf_op jit(solution)/shard_map/ppermute | solution.py:39
  16.2 13.5 %collective-permute-start.8 = (bf16[512,256]{1,0:T(8,128)(2,1)S(1)}, bf16[512,256]{1,0:T(8,128)(2,1)S(1)}, u32[]{:S(2)}, u32[]{:S(2)}) collective-permute-start(bf16[512,256]{1,0:T(8,128)(2,1)S(1)} %constant_dynamic-update-slice_fusion.own0), channel_id=1, source_target_pairs={{0,4},{1,5},{2,6},{3,7},{4,0},{5,1},{6,2},{7,3},{8,12},{9,13},{10,... | collective-permute-start | bytes 786440 | tf_op jit(solution)/shard_map/ppermute | solution.py:39
  18.9 10.8 %collective-permute-start.7 = (bf16[512,256]{1,0:T(8,128)(2,1)S(1)}, bf16[512,256]{1,0:T(8,128)(2,1)S(1)}, u32[]{:S(2)}, u32[]{:S(2)}) collective-permute-start(bf16[512,256]{1,0:T(8,128)(2,1)S(1)} %constant_dynamic-update-slice_fusion.own0), channel_id=1, source_target_pairs={{0,6},{1,7},{2,0},{3,1},{4,2},{5,3},{6,4},{7,5},{8,14},{9,15},{10,... | collective-permute-start | bytes 786440 | tf_op jit(solution)/shard_map/ppermute | solution.py:39
  29.8 11.6 %collective-permute-start.12 = (bf16[1024,256]{1,0:T(8,128)(2,1)S(1)}, bf16[1024,256]{1,0:T(8,128)(2,1)S(1)}, u32[]{:S(2)}, u32[]{:S(2)}) collective-permute-start(bf16[1024,256]{1,0:T(8,128)(2,1)S(1)} %pad_maximum_fusion.1), channel_id=1, source_target_pairs={{0,8},{1,9},{2,10},{3,11},{4,12},{5,13},{6,14},{7,15},{8,0},{9,1},... | collective-permute-start | bytes 1572872 | tf_op jit(solution)/shard_map/ppermute | solution.py:39
  30.2 10.0 %collective-permute-start.11 = (bf16[128,1024]{1,0:T(8,128)(2,1)S(1)}, bf16[128,1024]{1,0:T(8,128)(2,1)S(1)}, u32[]{:S(2)}, u32[]{:S(2)}) collective-permute-start(bf16[128,1024]{1,0:T(8,128)(2,1)S(1)} %slice.95), channel_id=1, source_target_pairs={{0,64},{1,65},{2,66},{3,67},{4,68},{5,69},{6,70},{7,71},{8,72},{9,... | collective-permute-start | bytes 786440 | tf_op jit(solution)/shard_map/ppermute | solution.py:39
  31.6 8.6 %collective-permute-start.13 = (bf16[512,256]{1,0:T(8,128)(2,1)S(1)}, bf16[512,256]{1,0:T(8,128)(2,1)S(1)}, u32[]{:S(2)}, u32[]{:S(2)}) collective-permute-start(bf16[512,256]{1,0:T(8,128)(2,1)S(1)} %collective-permute-done.8.own2), channel_id=1, source_target_pairs={{0,8},{1,9},{2,10},{3,11},{4,12},{5,13},{6,14},{7,15},{8,0},{9,1},... | collective-permute-start | bytes 786440 | tf_op jit(solution)/shard_map/ppermute | solution.py:39
  31.8 8.4 %collective-permute-start.14 = (bf16[512,256]{1,0:T(8,128)(2,1)S(1)}, bf16[512,256]{1,0:T(8,128)(2,1)S(1)}, u32[]{:S(2)}, u32[]{:S(2)}) collective-permute-start(bf16[512,256]{1,0:T(8,128)(2,1)S(1)} %collective-permute-done.9.own3), channel_id=1, source_target_pairs={{0,8},{1,9},{2,10},{3,11},{4,12},{5,13},{6,14},{7,15},{8,0},{9,1},... | collective-permute-start | bytes 786440 | tf_op jit(solution)/shard_map/ppermute | solution.py:39
  32.1 9.2 %collective-permute-start.10 = (bf16[144,1024]{1,0:T(8,128)(2,1)S(1)}, bf16[144,1024]{1,0:T(8,128)(2,1)S(1)}, u32[]{:S(2)}, u32[]{:S(2)}) collective-permute-start(bf16[144,1024]{1,0:T(8,128)(2,1)S(1)} %slice.94), channel_id=1, source_target_pairs={{0,65},{1,64},{2,67},{3,66},{4,69},{5,68},{6,71},{7,70},{8,73},{9,... | collective-permute-start | bytes 884744 | tf_op jit(solution)/shard_map/ppermute | solution.py:39
  68.5 2.7 %collective-permute-start.19 = (bf16[2048,256]{1,0:T(8,128)(2,1)S(1)}, bf16[2048,256]{1,0:T(8,128)(2,1)S(1)}, u32[]{:S(2)}, u32[]{:S(2)}) collective-permute-start(bf16[2048,256]{1,0:T(8,128)(2,1)S(1)} %get-tuple-element.26), channel_id=1, source_target_pairs={{0,8},{1,9},{2,10},{3,11},{4,12},{5,13},{6,14},{7,15},{8,0},{9,1},... | collective-permute-start | bytes 3145736 | tf_op jit(solution)/shard_map/ppermute | solution.py:39
  68.6 12.7 %collective-permute-start.15 = (bf16[512,512]{1,0:T(8,128)(2,1)S(1)}, bf16[512,512]{1,0:T(8,128)(2,1)S(1)}, u32[]{:S(2)}, u32[]{:S(2)}) collective-permute-start(bf16[512,512]{1,0:T(8,128)(2,1)S(1)} %get-tuple-element.24), channel_id=1, source_target_pairs={{0,8},{1,9},{2,10},{3,11},{4,12},{5,13},{6,14},{7,15},{8,0},{9,1},... | collective-permute-start | bytes 1572872 | tf_op jit(solution)/shard_map/ppermute | solution.py:39
  71.6 16.8 %collective-permute-start.20 = (bf16[512,256]{1,0:T(8,128)(2,1)S(1)}, bf16[512,256]{1,0:T(8,128)(2,1)S(1)}, u32[]{:S(2)}, u32[]{:S(2)}) collective-permute-start(bf16[512,256]{1,0:T(8,128)(2,1)S(1)} %get-tuple-element.29), channel_id=1, source_target_pairs={{0,2},{1,3},{2,4},{3,5},{4,6},{5,7},{6,0},{7,1},{8,10},{9,11},{10,... | collective-permute-start | bytes 786440 | tf_op jit(solution)/shard_map/ppermute | solution.py:39
  77.1 14.3 %collective-permute-start.22 = (bf16[512,256]{1,0:T(8,128)(2,1)S(1)}, bf16[512,256]{1,0:T(8,128)(2,1)S(1)}, u32[]{:S(2)}, u32[]{:S(2)}) collective-permute-start(bf16[512,256]{1,0:T(8,128)(2,1)S(1)} %get-tuple-element.30), channel_id=1, source_target_pairs={{0,6},{1,7},{2,0},{3,1},{4,2},{5,3},{6,4},{7,5},{8,14},{9,15},{10,... | collective-permute-start | bytes 786440 | tf_op jit(solution)/shard_map/ppermute | solution.py:39
  79.9 13.3 %collective-permute-start.21 = (bf16[512,256]{1,0:T(8,128)(2,1)S(1)}, bf16[512,256]{1,0:T(8,128)(2,1)S(1)}, u32[]{:S(2)}, u32[]{:S(2)}) collective-permute-start(bf16[512,256]{1,0:T(8,128)(2,1)S(1)} %get-tuple-element.31), channel_id=1, source_target_pairs={{0,4},{1,5},{2,6},{3,7},{4,0},{5,1},{6,2},{7,3},{8,12},{9,13},{10,... | collective-permute-start | bytes 786440 | tf_op jit(solution)/shard_map/ppermute | solution.py:39
  81.5 15.2 %collective-permute-start.16 = (bf16[128,1024]{1,0:T(8,128)(2,1)S(1)}, bf16[128,1024]{1,0:T(8,128)(2,1)S(1)}, u32[]{:S(2)}, u32[]{:S(2)}) collective-permute-start(bf16[128,1024]{1,0:T(8,128)(2,1)S(1)} %get-tuple-element.32), channel_id=1, source_target_pairs={{0,64},{1,65},{2,66},{3,67},{4,68},{5,69},{6,70},{7,71},{8,72},{9,... | collective-permute-start | bytes 786440 | tf_op jit(solution)/shard_map/ppermute | solution.py:39
  86.4 19.9 %collective-permute-start.18 = (bf16[128,1024]{1,0:T(8,128)(2,1)S(1)}, bf16[128,1024]{1,0:T(8,128)(2,1)S(1)}, u32[]{:S(2)}, u32[]{:S(2)}) collective-permute-start(bf16[128,1024]{1,0:T(8,128)(2,1)S(1)} %get-tuple-element.33), channel_id=1, source_target_pairs={{0,65},{1,64},{2,67},{3,66},{4,69},{5,68},{6,71},{7,70},{8,73},{9,... | collective-permute-start | bytes 786440 | tf_op jit(solution)/shard_map/ppermute | solution.py:39
  88.4 17.9 %collective-permute-start.17 = (bf16[128,1024]{1,0:T(8,128)(2,1)S(1)}, bf16[128,1024]{1,0:T(8,128)(2,1)S(1)}, u32[]{:S(2)}, u32[]{:S(2)}) collective-permute-start(bf16[128,1024]{1,0:T(8,128)(2,1)S(1)} %get-tuple-element.34), channel_id=1, source_target_pairs={{0,1},{1,0},{2,3},{3,2},{4,5},{5,4},{6,7},{7,6},{8,9},{9,8},{10,11... | collective-permute-start | bytes 786440 | tf_op jit(solution)/shard_map/ppermute | solution.py:39
  93.4 13.7 %collective-permute-start.23 = (bf16[128,256]{1,0:T(8,128)(2,1)S(1)}, bf16[128,256]{1,0:T(8,128)(2,1)S(1)}, u32[]{:S(2)}, u32[]{:S(2)}) collective-permute-start(bf16[128,256]{1,0:T(8,128)(2,1)S(1)} %get-tuple-element.37), channel_id=1, source_target_pairs={{0,16},{1,17},{2,18},{3,19},{4,20},{5,21},{6,22},{7,23},{8,24},{9,... | collective-permute-start | bytes 196616 | tf_op jit(solution)/shard_map/ppermute | solution.py:39
  93.5 13.7 %collective-permute-start.25 = (bf16[128,256]{1,0:T(8,128)(2,1)S(1)}, bf16[128,256]{1,0:T(8,128)(2,1)S(1)}, u32[]{:S(2)}, u32[]{:S(2)}) collective-permute-start(bf16[128,256]{1,0:T(8,128)(2,1)S(1)} %get-tuple-element.38), channel_id=1, source_target_pairs={{0,48},{1,49},{2,50},{3,51},{4,52},{5,53},{6,54},{7,55},{8,56},{9,... | collective-permute-start | bytes 196616 | tf_op jit(solution)/shard_map/ppermute | solution.py:39
  96.7 11.8 %collective-permute-start.24 = (bf16[128,256]{1,0:T(8,128)(2,1)S(1)}, bf16[128,256]{1,0:T(8,128)(2,1)S(1)}, u32[]{:S(2)}, u32[]{:S(2)}) collective-permute-start(bf16[128,256]{1,0:T(8,128)(2,1)S(1)} %get-tuple-element.39), channel_id=1, source_target_pairs={{0,32},{1,33},{2,34},{3,35},{4,36},{5,37},{6,38},{7,39},{8,40},{9,... | collective-permute-start | bytes 196616 | tf_op jit(solution)/shard_map/ppermute | solution.py:39

commit v4 on v3

--- a/solution.py
+++ b/solution.py
@@ -49,7 +49,7 @@
 
 def attend_kernel(
     q_rank, k_rank, q_sorted, k_sorted, counts,
-    pay0, pay1, pay2a, pay2b, pay3, own0, own1, own2, own3, sib0, sib1, sib2,
+    pay0, pay1, pay2a, pay2b, pay3, own0, own1, own2, own3, sib0, sib1, sib2, sib3,
     dq_own, dq_sib, dkv_own, dkv_sib,
     ks, vs, kt, dk, dv, qs, gs, dq, lse_s, del_s, s_scr, p_scr, plain, edge,
 ):
@@ -61,16 +61,14 @@
     scale = 1.0 / math.sqrt(WIDTH)
     factor = scale * LOG2E
 
-    listed = 0
-    for kv in (own0, own1, own2, own3, sib0, sib1, sib2):
-        def bring(r, _, kv=kv, listed=listed):
+    for n, kv in enumerate((own0, own1, own2, own3, sib0, sib1, sib2, sib3)):
+        def bring(r, _, kv=kv, n=n):
             src = pl.multiple_of(r * BLOCK, BLOCK)
-            dst = pl.multiple_of(k_rank[listed + r] * BLOCK, BLOCK)
+            dst = pl.multiple_of(k_rank[n * 8 + r] * BLOCK, BLOCK)
             ks[pl.ds(dst, BLOCK), :] = kv[pl.ds(src, BLOCK), :WIDTH]
             vs[pl.ds(dst, BLOCK), :] = kv[pl.ds(src, BLOCK), WIDTH:]
             return 0
-        lax.fori_loop(0, kv.shape[0] // BLOCK, bring, 0, unroll=4)
-        listed += kv.shape[0] // BLOCK
+        lax.fori_loop(0, 8, bring, 0, unroll=4)
 
     def ready(j, _):
         kt[j] = ks[pl.ds(pl.multiple_of(j * KEY_TILE, KEY_TILE), KEY_TILE), :].T
@@ -195,7 +193,7 @@
     listed = query_tiles * key_tiles + 2
     return pl.pallas_call(
         attend_kernel,
-        in_specs=[smem] * 5 + [vmem] * 12,
+        in_specs=[smem] * 5 + [vmem] * 13,
         out_specs=[vmem] * 4,
         out_shape=[jax.ShapeDtypeStruct((8 * BLOCK, HALF_HEADS * WIDTH), bf16)] * 2
         + [jax.ShapeDtypeStruct((keys // 2, 2 * WIDTH), bf16)] * 2,
@@ -266,13 +264,15 @@
     pay = jnp.concatenate(
         [jnp.concatenate([mine(query_rows), mine(output_grad)], axis=1), stat, sib], axis=0)
     kv_line = jnp.concatenate([kv] + [shift(kv, dz=-d) for d in (1, 2, 3)], axis=0)
-    lines = [kv_line] + [shift(kv_line, dx=-d) for d in (1, 2, 3)]
     after, before = shift(pay, dy=-1), shift(pay, dy=1)
-    after, before, *lines = lax.optimization_barrier((after, before, *lines))
+    right, left, line_sib = shift(kv_line, dx=-1), shift(kv_line, dx=1), shift(kv_line, dcore=1)
+    after, before, kv_line, line_sib, right, left = lax.optimization_barrier(
+        (after, before, kv_line, line_sib, right, left))
     across = shift(after[:SIB_AT], dy=-1), shift(before[SIB_AT:], dy=1)
+    beyond = shift(kv_line, dx=2)
     pays = [pay, after, *across, before]
-    joined = [jnp.concatenate(lines[:2], axis=0), *lines[2:]]
-    kvs = lines + [shift(line, dcore=1) for line in joined]
+    kvs = [kv_line, right, beyond, left, line_sib]
+    kvs += [shift(line, dcore=1) for line in (right, beyond, left)]
 
     four = jnp.arange(4, dtype=jnp.int32)
     two = jnp.arange(2, dtype=jnp.int32)

time: 111 us -> 110 us (level); the launches traced: 109 us -> 111 us
  Pallas kernels: 27.2 us -> 35.6 us
  starting transfers between devices: 52.3 us -> 45 us
    pallas_call x1, Pallas kernels: 27.2 us -> 35.6 us  [attend(): pl.pallas_call(attend_kernel, in_specs=[smem] * 5 + [vmem] * 13, out_spec...]
    ppermute x26 -> x27, starting transfers between devices: 52.3 us -> 45 us  [shift(): return lax.ppermute(block, AXES, route)]
    ppermute x26 -> x27, waiting for transfers between devices: 22 us -> 23 us  [shift(): return lax.ppermute(block, AXES, route)]
  transfers between devices with their start and end apart: 26 -> 27, of which waited for: 8 -> 10; matrix products, arithmetic and copies ran while one was open for 4% -> 3% of each run, Pallas kernels for 0% -> 0%
where the time goes in v4:
time: 110 us; the launch traced here: 111 us
  starting transfers between devices  45 us (41%)
  Pallas kernels  35.6 us (32%)
  waiting for transfers between devices  23 us (21%)
  other arithmetic  4.18 us (4%)
  local copies, waits for them, and re-layouts  2.35 us (2%)
    ppermute x27, starting transfers between devices, shift(): return lax.ppermute(block, AXES, route)  45 us
    pallas_call x1, Pallas kernels, attend(): pl.pallas_call(attend_kernel, in_specs=[smem] * 5 + [vmem] * 13, out_spec...  35.6 us
    ppermute x27, waiting for transfers between devices, shift(): return lax.ppermute(block, AXES, route)  23 us
  transfers between devices with their start and end apart: 27, of which 10 were waited for; matrix products, arithmetic and copies ran while one was open for 3% of the time, Pallas kernels for 0%

profile of v4, /device:TPU:0, one launch (start us, length us, event | category | flops | bytes accessed | tf_op | source)
XLA Modules:
  0.0 111.3 jit_solution(1614202594940155661)
XLA Ops:
  0.7 1.1 multiply_bitcast_fusion
  2.9 0.3 collective-permute-start.1
  4.5 2.0 %collective-permute-start.6 = (bf16[128,256]{1,0:T(8,128)(2,1)S(1)}, bf16[128,256]{1,0:T(8,128)(2,1)S(1)}, u32[]{:S(2)}, u32[]{:S(2)}) collective-permute-start(bf16[128,256]{1,0:T(8,128)(2,1)S(1)} %pad_maximum_fusion.3), channel_id=1, source_target_pairs={{0,16},{1,17},{2,18},{3,19},{4,20},{5,21},{6,22},{7,23},{8,24},{9,... | collective-permute-start | bytes 196616 | tf_op jit(solution)/shard_map/ppermute | solution.py:39
  6.5 3.6 %collective-permute-start.5 = (bf16[128,256]{1,0:T(8,128)(2,1)S(1)}, bf16[128,256]{1,0:T(8,128)(2,1)S(1)}, u32[]{:S(2)}, u32[]{:S(2)}) collective-permute-start(bf16[128,256]{1,0:T(8,128)(2,1)S(1)} %pad_maximum_fusion.3), channel_id=1, source_target_pairs={{0,32},{1,33},{2,34},{3,35},{4,36},{5,37},{6,38},{7,39},{8,40},{9,... | collective-permute-start | bytes 196616 | tf_op jit(solution)/shard_map/ppermute | solution.py:39
  10.1 1.0 collective-permute-start.4
  11.1 1.6 %collective-permute-start.3 = (bf16[272,1024]{1,0:T(8,128)(2,1)S(1)}, bf16[272,1024]{1,0:T(8,128)(2,1)S(1)}, u32[]{:S(2)}, u32[]{:S(2)}) collective-permute-start(bf16[272,1024]{1,0:T(8,128)(2,1)S(1)} %pad_maximum_fusion.pay0), channel_id=1, source_target_pairs={{0,64},{1,65},{2,66},{3,67},{4,68},{5,69},{6,70},{7,71},{8,72},{9,... | collective-permute-start | bytes 1671176 | tf_op jit(solution)/shard_map/ppermute | solution.py:39
  12.8 1.7 %collective-permute-start.2 = (bf16[272,1024]{1,0:T(8,128)(2,1)S(1)}, bf16[272,1024]{1,0:T(8,128)(2,1)S(1)}, u32[]{:S(2)}, u32[]{:S(2)}) collective-permute-start(bf16[272,1024]{1,0:T(8,128)(2,1)S(1)} %pad_maximum_fusion.pay0), channel_id=1, source_target_pairs={{0,65},{1,64},{2,67},{3,66},{4,69},{5,68},{6,71},{7,70},{8,73},{9,... | collective-permute-start | bytes 1671176 | tf_op jit(solution)/shard_map/ppermute | solution.py:39
  14.5 1.6 %collective-permute-start.9 = (bf16[512,256]{1,0:T(8,128)(2,1)S(1)}, bf16[512,256]{1,0:T(8,128)(2,1)S(1)}, u32[]{:S(2)}, u32[]{:S(2)}) collective-permute-start(bf16[512,256]{1,0:T(8,128)(2,1)S(1)} %constant_dynamic-update-slice_fusion.own0), channel_id=1, source_target_pairs={{0,2},{1,3},{2,4},{3,5},{4,6},{5,7},{6,0},{7,1},{8,10},{9,11},{10,... | collective-permute-start | bytes 786440 | tf_op jit(solution)/shard_map/ppermute | solution.py:39
  16.1 1.7 %collective-permute-start.8 = (bf16[512,256]{1,0:T(8,128)(2,1)S(1)}, bf16[512,256]{1,0:T(8,128)(2,1)S(1)}, u32[]{:S(2)}, u32[]{:S(2)}) collective-permute-start(bf16[512,256]{1,0:T(8,128)(2,1)S(1)} %constant_dynamic-update-slice_fusion.own0), channel_id=1, source_target_pairs={{0,6},{1,7},{2,0},{3,1},{4,2},{5,3},{6,4},{7,5},{8,14},{9,15},{10,... | collective-permute-start | bytes 786440 | tf_op jit(solution)/shard_map/ppermute | solution.py:39
  18.4 4.6 %collective-permute-done.9.own3 = bf16[512,256]{1,0:T(8,128)(2,1)S(1)} collective-permute-done((bf16[512,256]{1,0:T(8,128)(2,1)S(1)}, bf16[512,256]{1,0:T(8,128)(2,1)S(1)}, u32[]{:S(2)}, u32[]{:S(2)}) %collective-permute-start.9) | collective-permute-done | bytes 262176 | tf_op jit(solution)/shard_map/ppermute | solution.py:39
  23.0 3.4 %collective-permute-done.3.pay3 = bf16[272,1024]{1,0:T(8,128)(2,1)S(1)} collective-permute-done((bf16[272,1024]{1,0:T(8,128)(2,1)S(1)}, bf16[272,1024]{1,0:T(8,128)(2,1)S(1)}, u32[]{:S(2)}, u32[]{:S(2)}) %collective-permute-start.3) | collective-permute-done | bytes 557088 | tf_op jit(solution)/shard_map/ppermute | solution.py:39
  26.5 3.0 %collective-permute-start.12 = (bf16[512,256]{1,0:T(8,128)(2,1)S(1)}, bf16[512,256]{1,0:T(8,128)(2,1)S(1)}, u32[]{:S(2)}, u32[]{:S(2)}) collective-permute-start(bf16[512,256]{1,0:T(8,128)(2,1)S(1)} %constant_dynamic-update-slice_fusion.own0), channel_id=1, source_target_pairs={{0,4},{1,5},{2,6},{3,7},{4,0},{5,1},{6,2},{7,3},{8,12},{9,13},{10,... | collective-permute-start | bytes 786440 | tf_op jit(solution)/shard_map/ppermute | solution.py:39
  30.2 1.6 %collective-permute-start.11 = (bf16[128,1024]{1,0:T(8,128)(2,1)S(1)}, bf16[128,1024]{1,0:T(8,128)(2,1)S(1)}, u32[]{:S(2)}, u32[]{:S(2)}) collective-permute-start(bf16[128,1024]{1,0:T(8,128)(2,1)S(1)} %slice.95), channel_id=1, source_target_pairs={{0,64},{1,65},{2,66},{3,67},{4,68},{5,69},{6,70},{7,71},{8,72},{9,... | collective-permute-start | bytes 786440 | tf_op jit(solution)/shard_map/ppermute | solution.py:39
  31.8 0.5 collective-permute-start.15
  32.3 1.7 %collective-permute-start.10 = (bf16[144,1024]{1,0:T(8,128)(2,1)S(1)}, bf16[144,1024]{1,0:T(8,128)(2,1)S(1)}, u32[]{:S(2)}, u32[]{:S(2)}) collective-permute-start(bf16[144,1024]{1,0:T(8,128)(2,1)S(1)} %slice.94), channel_id=1, source_target_pairs={{0,65},{1,64},{2,67},{3,66},{4,69},{5,68},{6,71},{7,70},{8,73},{9,... | collective-permute-start | bytes 884744 | tf_op jit(solution)/shard_map/ppermute | solution.py:39
  34.1 0.6 collective-permute-done.12.own2
  34.7 3.2 %collective-permute-done.11.pay2b = bf16[128,1024]{1,0:T(8,128)(2,1)S(1)} collective-permute-done((bf16[128,1024]{1,0:T(8,128)(2,1)S(1)}, bf16[128,1024]{1,0:T(8,128)(2,1)S(1)}, u32[]{:S(2)}, u32[]{:S(2)}) %collective-permute-start.11) | collective-permute-done | bytes 262176 | tf_op jit(solution)/shard_map/ppermute | solution.py:39
  37.9 3.4 %collective-permute-done.10.pay2a = bf16[144,1024]{1,0:T(8,128)(2,1)S(1)} collective-permute-done((bf16[144,1024]{1,0:T(8,128)(2,1)S(1)}, bf16[144,1024]{1,0:T(8,128)(2,1)S(1)}, u32[]{:S(2)}, u32[]{:S(2)}) %collective-permute-start.10) | collective-permute-done | bytes 294944 | tf_op jit(solution)/shard_map/ppermute | solution.py:39
  41.3 35.6 %shard_map.94 = (bf16[512,512]{1,0:T(8,128)(2,1)S(1)}, bf16[512,512]{1,0:T(8,128)(2,1)S(1)}, bf16[2048,256]{1,0:T(8,128)(2,1)S(1)}, bf16[2048,256]{1,0:T(8,128)(2,1)S(1)}) custom-call(s32[16]{0:T(128)S(1)} %convert_reduce_fusion.1.q_rank, s32[64]{0:T(128)S(1)} %convert_reduce_fusion.k_rank, s32[16]{0:T(128)S(1)} %select_reduce_fusion.3.q_sorted, ...), custom_call_target="tpu_custom_call" | custom-call | tf_op jit(solution)/shard_map/pallas_call | solution.py:194
  77.2 0.5 collective-permute-start.16
  77.7 2.1 %collective-permute-done.20 = bf16[2048,256]{1,0:T(8,128)(2,1)S(1)} collective-permute-done((bf16[2048,256]{1,0:T(8,128)(2,1)S(1)}, bf16[2048,256]{1,0:T(8,128)(2,1)S(1)}, u32[]{:S(2)}, u32[]{:S(2)}) %collective-permute-start.20) | collective-permute-done | bytes 1048608 | tf_op jit(solution)/shard_map/ppermute | solution.py:39
  80.3 3.2 %collective-permute-start.23 = (bf16[512,256]{1,0:T(8,128)(2,1)S(1)}, bf16[512,256]{1,0:T(8,128)(2,1)S(1)}, u32[]{:S(2)}, u32[]{:S(2)}) collective-permute-start(bf16[512,256]{1,0:T(8,128)(2,1)S(1)} %get-tuple-element.30), channel_id=1, source_target_pairs={{0,6},{1,7},{2,0},{3,1},{4,2},{5,3},{6,4},{7,5},{8,14},{9,15},{10,... | collective-permute-start | bytes 786440 | tf_op jit(solution)/shard_map/ppermute | solution.py:39
  83.5 2.3 %collective-permute-start.22 = (bf16[512,256]{1,0:T(8,128)(2,1)S(1)}, bf16[512,256]{1,0:T(8,128)(2,1)S(1)}, u32[]{:S(2)}, u32[]{:S(2)}) collective-permute-start(bf16[512,256]{1,0:T(8,128)(2,1)S(1)} %get-tuple-element.31), channel_id=1, source_target_pairs={{0,4},{1,5},{2,6},{3,7},{4,0},{5,1},{6,2},{7,3},{8,12},{9,13},{10,... | collective-permute-start | bytes 786440 | tf_op jit(solution)/shard_map/ppermute | solution.py:39
  86.0 1.2 %collective-permute-start.17 = (bf16[128,1024]{1,0:T(8,128)(2,1)S(1)}, bf16[128,1024]{1,0:T(8,128)(2,1)S(1)}, u32[]{:S(2)}, u32[]{:S(2)}) collective-permute-start(bf16[128,1024]{1,0:T(8,128)(2,1)S(1)} %get-tuple-element.32), channel_id=1, source_target_pairs={{0,64},{1,65},{2,66},{3,67},{4,68},{5,69},{6,70},{7,71},{8,72},{9,... | collective-permute-start | bytes 786440 | tf_op jit(solution)/shard_map/ppermute | solution.py:39
  87.1 2.1 %collective-permute-start.19 = (bf16[128,1024]{1,0:T(8,128)(2,1)S(1)}, bf16[128,1024]{1,0:T(8,128)(2,1)S(1)}, u32[]{:S(2)}, u32[]{:S(2)}) collective-permute-start(bf16[128,1024]{1,0:T(8,128)(2,1)S(1)} %get-tuple-element.33), channel_id=1, source_target_pairs={{0,65},{1,64},{2,67},{3,66},{4,69},{5,68},{6,71},{7,70},{8,73},{9,... | collective-permute-start | bytes 786440 | tf_op jit(solution)/shard_map/ppermute | solution.py:39
  89.3 0.5 collective-permute-done.21
  89.8 11.5 %collective-permute-start.18 = (bf16[128,1024]{1,0:T(8,128)(2,1)S(1)}, bf16[128,1024]{1,0:T(8,128)(2,1)S(1)}, u32[]{:S(2)}, u32[]{:S(2)}) collective-permute-start(bf16[128,1024]{1,0:T(8,128)(2,1)S(1)} %get-tuple-element.34), channel_id=1, source_target_pairs={{0,1},{1,0},{2,3},{3,2},{4,5},{5,4},{6,7},{7,6},{8,9},{9,8},{10,11... | collective-permute-start | bytes 786440 | tf_op jit(solution)/shard_map/ppermute | solution.py:39
  101.6 3.2 %collective-permute-start.26 = (bf16[128,256]{1,0:T(8,128)(2,1)S(1)}, bf16[128,256]{1,0:T(8,128)(2,1)S(1)}, u32[]{:S(2)}, u32[]{:S(2)}) collective-permute-start(bf16[128,256]{1,0:T(8,128)(2,1)S(1)} %get-tuple-element.38), channel_id=1, source_target_pairs={{0,48},{1,49},{2,50},{3,51},{4,52},{5,53},{6,54},{7,55},{8,56},{9,... | collective-permute-start | bytes 196616 | tf_op jit(solution)/shard_map/ppermute | solution.py:39
  104.8 2.3 %collective-permute-done.18 = bf16[128,1024]{1,0:T(8,128)(2,1)S(1)} collective-permute-done((bf16[128,1024]{1,0:T(8,128)(2,1)S(1)}, bf16[128,1024]{1,0:T(8,128)(2,1)S(1)}, u32[]{:S(2)}, u32[]{:S(2)}) %collective-permute-start.18) | collective-permute-done | bytes 262176 | tf_op jit(solution)/shard_map/ppermute | solution.py:39
  107.1 0.9 add_convert_fusion.2
  108.0 2.6 %collective-permute-done.25 = bf16[128,256]{1,0:T(8,128)(2,1)S(1)} collective-permute-done((bf16[128,256]{1,0:T(8,128)(2,1)S(1)}, bf16[128,256]{1,0:T(8,128)(2,1)S(1)}, u32[]{:S(2)}, u32[]{:S(2)}) %collective-permute-start.25) | collective-permute-done | bytes 65568 | tf_op jit(solution)/shard_map/ppermute | solution.py:39
  110.6 0.6 fusion.28
  (89 shorter events, 4.7 us)
Async XLA Ops:
  1.8 1.0 copy-start
  1.8 1.0 copy-start.1
  2.1 1.9 %copy-start.2 = (bf16[128,128]{1,0:T(8,128)(2,1)S(1)}, bf16[128,128]{1,0:T(8,128)(2,1)}, u32[]{:S(2)}) copy-start(bf16[128,128]{1,0:T(8,128)(2,1)} %param.9) | copy-start | bytes 98308
  2.1 1.9 %copy-start.3 = (bf16[128,128]{1,0:T(8,128)(2,1)S(1)}, bf16[128,128]{1,0:T(8,128)(2,1)}, u32[]{:S(2)}) copy-start(bf16[128,128]{1,0:T(8,128)(2,1)} %param.8) | copy-start | bytes 98308
  2.2 1.9 %copy-start.4 = (s32[256]{0:T(256)S(1)}, s32[256]{0:T(256)}, u32[]{:S(2)}) copy-start(s32[256]{0:T(256)} %param.13) | copy-start | bytes 3076
  2.5 1.9 %collective-permute-start = (f32[8,128]{1,0:T(8,128)S(1)}, f32[8,128]{1,0:T(8,128)S(1)}, u32[]{:S(2)}, u32[]{:S(2)}) collective-permute-start(f32[8,128]{1,0:T(8,128)S(1)} %get-tuple-element.50), channel_id=1, source_target_pairs={{0,8},{1,9},{2,10},{3,11},{4,12},{5,13},{6,14},{7,15},{8,0},{9,1},... | collective-permute-start | bytes 12296 | tf_op jit(solution)/shard_map/ppermute | solution.py:39
  2.9 1.6 %collective-permute-start.1 = (bf16[128,1024]{1,0:T(8,128)(2,1)S(1)}, bf16[128,1024]{1,0:T(8,128)(2,1)S(1)}, u32[]{:S(2)}, u32[]{:S(2)}) collective-permute-start(bf16[128,1024]{1,0:T(8,128)(2,1)S(1)} %pad_maximum_fusion.2), channel_id=1, source_target_pairs={{0,8},{1,9},{2,10},{3,11},{4,12},{5,13},{6,14},{7,15},{8,0},{9,1},... | collective-permute-start | bytes 786440 | tf_op jit(solution)/shard_map/ppermute | solution.py:39
  4.5 10.0 %collective-permute-start.6 = (bf16[128,256]{1,0:T(8,128)(2,1)S(1)}, bf16[128,256]{1,0:T(8,128)(2,1)S(1)}, u32[]{:S(2)}, u32[]{:S(2)}) collective-permute-start(bf16[128,256]{1,0:T(8,128)(2,1)S(1)} %pad_maximum_fusion.3), channel_id=1, source_target_pairs={{0,16},{1,17},{2,18},{3,19},{4,20},{5,21},{6,22},{7,23},{8,24},{9,... | collective-permute-start | bytes 196616 | tf_op jit(solution)/shard_map/ppermute | solution.py:39
  6.5 8.0 %collective-permute-start.5 = (bf16[128,256]{1,0:T(8,128)(2,1)S(1)}, bf16[128,256]{1,0:T(8,128)(2,1)S(1)}, u32[]{:S(2)}, u32[]{:S(2)}) collective-permute-start(bf16[128,256]{1,0:T(8,128)(2,1)S(1)} %pad_maximum_fusion.3), channel_id=1, source_target_pairs={{0,32},{1,33},{2,34},{3,35},{4,36},{5,37},{6,38},{7,39},{8,40},{9,... | collective-permute-start | bytes 196616 | tf_op jit(solution)/shard_map/ppermute | solution.py:39
  10.1 4.4 %collective-permute-start.4 = (bf16[128,256]{1,0:T(8,128)(2,1)S(1)}, bf16[128,256]{1,0:T(8,128)(2,1)S(1)}, u32[]{:S(2)}, u32[]{:S(2)}) collective-permute-start(bf16[128,256]{1,0:T(8,128)(2,1)S(1)} %pad_maximum_fusion.3), channel_id=1, source_target_pairs={{0,48},{1,49},{2,50},{3,51},{4,52},{5,53},{6,54},{7,55},{8,56},{9,... | collective-permute-start | bytes 196616 | tf_op jit(solution)/shard_map/ppermute | solution.py:39
  11.1 15.3 %collective-permute-start.3 = (bf16[272,1024]{1,0:T(8,128)(2,1)S(1)}, bf16[272,1024]{1,0:T(8,128)(2,1)S(1)}, u32[]{:S(2)}, u32[]{:S(2)}) collective-permute-start(bf16[272,1024]{1,0:T(8,128)(2,1)S(1)} %pad_maximum_fusion.pay0), channel_id=1, source_target_pairs={{0,64},{1,65},{2,66},{3,67},{4,68},{5,69},{6,70},{7,71},{8,72},{9,... | collective-permute-start | bytes 1671176 | tf_op jit(solution)/shard_map/ppermute | solution.py:39
  12.8 13.7 %collective-permute-start.2 = (bf16[272,1024]{1,0:T(8,128)(2,1)S(1)}, bf16[272,1024]{1,0:T(8,128)(2,1)S(1)}, u32[]{:S(2)}, u32[]{:S(2)}) collective-permute-start(bf16[272,1024]{1,0:T(8,128)(2,1)S(1)} %pad_maximum_fusion.pay0), channel_id=1, source_target_pairs={{0,65},{1,64},{2,67},{3,66},{4,69},{5,68},{6,71},{7,70},{8,73},{9,... | collective-permute-start | bytes 1671176 | tf_op jit(solution)/shard_map/ppermute | solution.py:39
  14.5 8.5 %collective-permute-start.9 = (bf16[512,256]{1,0:T(8,128)(2,1)S(1)}, bf16[512,256]{1,0:T(8,128)(2,1)S(1)}, u32[]{:S(2)}, u32[]{:S(2)}) collective-permute-start(bf16[512,256]{1,0:T(8,128)(2,1)S(1)} %constant_dynamic-update-slice_fusion.own0), channel_id=1, source_target_pairs={{0,2},{1,3},{2,4},{3,5},{4,6},{5,7},{6,0},{7,1},{8,10},{9,11},{10,... | collective-permute-start | bytes 786440 | tf_op jit(solution)/shard_map/ppermute | solution.py:39
  16.1 6.9 %collective-permute-start.8 = (bf16[512,256]{1,0:T(8,128)(2,1)S(1)}, bf16[512,256]{1,0:T(8,128)(2,1)S(1)}, u32[]{:S(2)}, u32[]{:S(2)}) collective-permute-start(bf16[512,256]{1,0:T(8,128)(2,1)S(1)} %constant_dynamic-update-slice_fusion.own0), channel_id=1, source_target_pairs={{0,6},{1,7},{2,0},{3,1},{4,2},{5,3},{6,4},{7,5},{8,14},{9,15},{10,... | collective-permute-start | bytes 786440 | tf_op jit(solution)/shard_map/ppermute | solution.py:39
  17.8 5.2 %collective-permute-start.7 = (bf16[512,256]{1,0:T(8,128)(2,1)S(1)}, bf16[512,256]{1,0:T(8,128)(2,1)S(1)}, u32[]{:S(2)}, u32[]{:S(2)}) collective-permute-start(bf16[512,256]{1,0:T(8,128)(2,1)S(1)} %constant_dynamic-update-slice_fusion.own0), channel_id=1, source_target_pairs={{0,8},{1,9},{2,10},{3,11},{4,12},{5,13},{6,14},{7,15},{8,0},{9,1},... | collective-permute-start | bytes 786440 | tf_op jit(solution)/shard_map/ppermute | solution.py:39
  26.5 8.2 %collective-permute-start.12 = (bf16[512,256]{1,0:T(8,128)(2,1)S(1)}, bf16[512,256]{1,0:T(8,128)(2,1)S(1)}, u32[]{:S(2)}, u32[]{:S(2)}) collective-permute-start(bf16[512,256]{1,0:T(8,128)(2,1)S(1)} %constant_dynamic-update-slice_fusion.own0), channel_id=1, source_target_pairs={{0,4},{1,5},{2,6},{3,7},{4,0},{5,1},{6,2},{7,3},{8,12},{9,13},{10,... | collective-permute-start | bytes 786440 | tf_op jit(solution)/shard_map/ppermute | solution.py:39
  30.2 7.7 %collective-permute-start.11 = (bf16[128,1024]{1,0:T(8,128)(2,1)S(1)}, bf16[128,1024]{1,0:T(8,128)(2,1)S(1)}, u32[]{:S(2)}, u32[]{:S(2)}) collective-permute-start(bf16[128,1024]{1,0:T(8,128)(2,1)S(1)} %slice.95), channel_id=1, source_target_pairs={{0,64},{1,65},{2,66},{3,67},{4,68},{5,69},{6,70},{7,71},{8,72},{9,... | collective-permute-start | bytes 786440 | tf_op jit(solution)/shard_map/ppermute | solution.py:39
  31.8 6.1 %collective-permute-start.13 = (bf16[512,256]{1,0:T(8,128)(2,1)S(1)}, bf16[512,256]{1,0:T(8,128)(2,1)S(1)}, u32[]{:S(2)}, u32[]{:S(2)}) collective-permute-start(bf16[512,256]{1,0:T(8,128)(2,1)S(1)} %collective-permute-done.8.own1), channel_id=1, source_target_pairs={{0,8},{1,9},{2,10},{3,11},{4,12},{5,13},{6,14},{7,15},{8,0},{9,1},... | collective-permute-start | bytes 786440 | tf_op jit(solution)/shard_map/ppermute | solution.py:39
  31.8 6.1 %collective-permute-start.15 = (bf16[512,256]{1,0:T(8,128)(2,1)S(1)}, bf16[512,256]{1,0:T(8,128)(2,1)S(1)}, u32[]{:S(2)}, u32[]{:S(2)}) collective-permute-start(bf16[512,256]{1,0:T(8,128)(2,1)S(1)} %collective-permute-done.9.own3), channel_id=1, source_target_pairs={{0,8},{1,9},{2,10},{3,11},{4,12},{5,13},{6,14},{7,15},{8,0},{9,1},... | collective-permute-start | bytes 786440 | tf_op jit(solution)/shard_map/ppermute | solution.py:39
  32.3 9.0 %collective-permute-start.10 = (bf16[144,1024]{1,0:T(8,128)(2,1)S(1)}, bf16[144,1024]{1,0:T(8,128)(2,1)S(1)}, u32[]{:S(2)}, u32[]{:S(2)}) collective-permute-start(bf16[144,1024]{1,0:T(8,128)(2,1)S(1)} %slice.94), channel_id=1, source_target_pairs={{0,65},{1,64},{2,67},{3,66},{4,69},{5,68},{6,71},{7,70},{8,73},{9,... | collective-permute-start | bytes 884744 | tf_op jit(solution)/shard_map/ppermute | solution.py:39
  34.7 6.6 %collective-permute-start.14 = (bf16[512,256]{1,0:T(8,128)(2,1)S(1)}, bf16[512,256]{1,0:T(8,128)(2,1)S(1)}, u32[]{:S(2)}, u32[]{:S(2)}) collective-permute-start(bf16[512,256]{1,0:T(8,128)(2,1)S(1)} %collective-permute-done.12.own2), channel_id=1, source_target_pairs={{0,8},{1,9},{2,10},{3,11},{4,12},{5,13},{6,14},{7,15},{8,0},{9,1},... | collective-permute-start | bytes 786440 | tf_op jit(solution)/shard_map/ppermute | solution.py:39
  76.9 2.9 %collective-permute-start.20 = (bf16[2048,256]{1,0:T(8,128)(2,1)S(1)}, bf16[2048,256]{1,0:T(8,128)(2,1)S(1)}, u32[]{:S(2)}, u32[]{:S(2)}) collective-permute-start(bf16[2048,256]{1,0:T(8,128)(2,1)S(1)} %get-tuple-element.26), channel_id=1, source_target_pairs={{0,8},{1,9},{2,10},{3,11},{4,12},{5,13},{6,14},{7,15},{8,0},{9,1},... | collective-permute-start | bytes 3145736 | tf_op jit(solution)/shard_map/ppermute | solution.py:39
  77.2 8.6 %collective-permute-start.16 = (bf16[512,512]{1,0:T(8,128)(2,1)S(1)}, bf16[512,512]{1,0:T(8,128)(2,1)S(1)}, u32[]{:S(2)}, u32[]{:S(2)}) collective-permute-start(bf16[512,512]{1,0:T(8,128)(2,1)S(1)} %get-tuple-element.24), channel_id=1, source_target_pairs={{0,8},{1,9},{2,10},{3,11},{4,12},{5,13},{6,14},{7,15},{8,0},{9,1},... | collective-permute-start | bytes 1572872 | tf_op jit(solution)/shard_map/ppermute | solution.py:39
  80.2 9.6 %collective-permute-start.21 = (bf16[512,256]{1,0:T(8,128)(2,1)S(1)}, bf16[512,256]{1,0:T(8,128)(2,1)S(1)}, u32[]{:S(2)}, u32[]{:S(2)}) collective-permute-start(bf16[512,256]{1,0:T(8,128)(2,1)S(1)} %get-tuple-element.29), channel_id=1, source_target_pairs={{0,2},{1,3},{2,4},{3,5},{4,6},{5,7},{6,0},{7,1},{8,10},{9,11},{10,... | collective-permute-start | bytes 786440 | tf_op jit(solution)/shard_map/ppermute | solution.py:39
  80.3 21.1 %collective-permute-start.23 = (bf16[512,256]{1,0:T(8,128)(2,1)S(1)}, bf16[512,256]{1,0:T(8,128)(2,1)S(1)}, u32[]{:S(2)}, u32[]{:S(2)}) collective-permute-start(bf16[512,256]{1,0:T(8,128)(2,1)S(1)} %get-tuple-element.30), channel_id=1, source_target_pairs={{0,6},{1,7},{2,0},{3,1},{4,2},{5,3},{6,4},{7,5},{8,14},{9,15},{10,... | collective-permute-start | bytes 786440 | tf_op jit(solution)/shard_map/ppermute | solution.py:39
  83.5 17.9 %collective-permute-start.22 = (bf16[512,256]{1,0:T(8,128)(2,1)S(1)}, bf16[512,256]{1,0:T(8,128)(2,1)S(1)}, u32[]{:S(2)}, u32[]{:S(2)}) collective-permute-start(bf16[512,256]{1,0:T(8,128)(2,1)S(1)} %get-tuple-element.31), channel_id=1, source_target_pairs={{0,4},{1,5},{2,6},{3,7},{4,0},{5,1},{6,2},{7,3},{8,12},{9,13},{10,... | collective-permute-start | bytes 786440 | tf_op jit(solution)/shard_map/ppermute | solution.py:39
  86.0 18.8 %collective-permute-start.17 = (bf16[128,1024]{1,0:T(8,128)(2,1)S(1)}, bf16[128,1024]{1,0:T(8,128)(2,1)S(1)}, u32[]{:S(2)}, u32[]{:S(2)}) collective-permute-start(bf16[128,1024]{1,0:T(8,128)(2,1)S(1)} %get-tuple-element.32), channel_id=1, source_target_pairs={{0,64},{1,65},{2,66},{3,67},{4,68},{5,69},{6,70},{7,71},{8,72},{9,... | collective-permute-start | bytes 786440 | tf_op jit(solution)/shard_map/ppermute | solution.py:39
  87.1 17.7 %collective-permute-start.19 = (bf16[128,1024]{1,0:T(8,128)(2,1)S(1)}, bf16[128,1024]{1,0:T(8,128)(2,1)S(1)}, u32[]{:S(2)}, u32[]{:S(2)}) collective-permute-start(bf16[128,1024]{1,0:T(8,128)(2,1)S(1)} %get-tuple-element.33), channel_id=1, source_target_pairs={{0,65},{1,64},{2,67},{3,66},{4,69},{5,68},{6,71},{7,70},{8,73},{9,... | collective-permute-start | bytes 786440 | tf_op jit(solution)/shard_map/ppermute | solution.py:39
  89.8 17.3 %collective-permute-start.18 = (bf16[128,1024]{1,0:T(8,128)(2,1)S(1)}, bf16[128,1024]{1,0:T(8,128)(2,1)S(1)}, u32[]{:S(2)}, u32[]{:S(2)}) collective-permute-start(bf16[128,1024]{1,0:T(8,128)(2,1)S(1)} %get-tuple-element.34), channel_id=1, source_target_pairs={{0,1},{1,0},{2,3},{3,2},{4,5},{5,4},{6,7},{7,6},{8,9},{9,8},{10,11... | collective-permute-start | bytes 786440 | tf_op jit(solution)/shard_map/ppermute | solution.py:39
  101.5 6.5 %collective-permute-start.24 = (bf16[128,256]{1,0:T(8,128)(2,1)S(1)}, bf16[128,256]{1,0:T(8,128)(2,1)S(1)}, u32[]{:S(2)}, u32[]{:S(2)}) collective-permute-start(bf16[128,256]{1,0:T(8,128)(2,1)S(1)} %get-tuple-element.37), channel_id=1, source_target_pairs={{0,16},{1,17},{2,18},{3,19},{4,20},{5,21},{6,22},{7,23},{8,24},{9,... | collective-permute-start | bytes 196616 | tf_op jit(solution)/shard_map/ppermute | solution.py:39
  101.6 6.4 %collective-permute-start.26 = (bf16[128,256]{1,0:T(8,128)(2,1)S(1)}, bf16[128,256]{1,0:T(8,128)(2,1)S(1)}, u32[]{:S(2)}, u32[]{:S(2)}) collective-permute-start(bf16[128,256]{1,0:T(8,128)(2,1)S(1)} %get-tuple-element.38), channel_id=1, source_target_pairs={{0,48},{1,49},{2,50},{3,51},{4,52},{5,53},{6,54},{7,55},{8,56},{9,... | collective-permute-start | bytes 196616 | tf_op jit(solution)/shard_map/ppermute | solution.py:39
  104.8 5.8 %collective-permute-start.25 = (bf16[128,256]{1,0:T(8,128)(2,1)S(1)}, bf16[128,256]{1,0:T(8,128)(2,1)S(1)}, u32[]{:S(2)}, u32[]{:S(2)}) collective-permute-start(bf16[128,256]{1,0:T(8,128)(2,1)S(1)} %get-tuple-element.39), channel_id=1, source_target_pairs={{0,32},{1,33},{2,34},{3,35},{4,36},{5,37},{6,38},{7,39},{8,40},{9,... | collective-permute-start | bytes 196616 | tf_op jit(solution)/shard_map/ppermute | solution.py:39
  (1 other events, 0.7 us)
